TPU v7x, 512 devices: a whole 4x4x16 slice. The times are simulated.
512 devices in a mesh: row: 32 (over y, x, core), col: 16 (over z).
Axes of the slice: x: 4, y: 4, z: 16, core: 2. Of those that a mesh axis runs over, the one named last changes fastest.
Arguments:
- inverse_cov: float32 [18432, 18432], P('row', 'col'), as said below
- key_table: bfloat16 [1024, 18432], P(None, 'row'), may hold values from -6 to 6
- weight: bfloat16 [18432, 7168], P('row', 'col'), may hold values from -0.046875 to 0.046875
- edit_index: int32 [2, 256], replicated, may hold values from 0 to 1023
- targets: bfloat16 [2, 256, 7168], P(None, None, 'col'), may hold values from -24 to 24
Outputs:
- weight_change: bfloat16 [18432, 7168], P('row', 'col')
Inputs may be any that keep to these rules, and one draw needn't show every extreme that they name: inverse_cov is symmetric and positive definite.
All inputs are finite; a program needn't handle non-finite values.
Results may differ from a plain program's by a relative error of at most 0.001.
Values may be sent and summed in bfloat16 or wider, within the bound.
No kernel may reach another device: no remote copies, remote signals or barrier semaphores. Data moves between devices by JAX's collectives and lax.ppermute only.
A program may use at most 64 MiB of HBM per device.

v0:
```python
import math

import jax
import jax.numpy as jnp
from jax import lax
from jax.sharding import PartitionSpec as P

F = 18432


def spread(value, axis, source):
    kept = jnp.where(lax.axis_index(axis) == source, value, 0).astype(value.dtype)
    return lax.psum(kept, axis)


def shards(inverse_cov, key_table, weight, edit_index, targets):
    highest = lax.Precision.HIGHEST
    rows_here = inverse_cov.shape[0]
    cols_here = inverse_cov.shape[1]
    fold_ratio = cols_here // rows_here
    row_index = lax.axis_index("row")
    key_count = edit_index.shape[1]
    local_keys = jnp.take(key_table, edit_index.reshape(-1), axis=0)
    identity = jnp.eye(key_count, dtype=jnp.float32)
    targets_full = targets.astype(jnp.float32)

    def key_panel(first, last):
        key_block = local_keys[first:last].astype(jnp.float32)
        shares = lax.psum_scatter(
            lax.dot_general(inverse_cov, key_block, (((0,), (1,)), ((), ())), precision=highest),
            "row",
            scatter_dimension=0,
            tiled=True,
        )
        gathered = lax.all_gather(shares, "row", axis=0, tiled=True)
        own_rows = lax.dynamic_slice_in_dim(
            gathered, row_index % fold_ratio * rows_here, rows_here, 0
        )
        return spread(own_rows, "col", row_index // fold_ratio)

    def factorize(gram_matrix):
        return jnp.linalg.cholesky(identity + gram_matrix)

    def solve_with(factor, rhs):
        return jax.scipy.linalg.cho_solve((factor, True), rhs)

    def reduce_batch(batch_keys, batch_panel, earlier):
        keys_full = batch_keys.astype(jnp.float32)
        gram_part = jnp.dot(keys_full, batch_panel, precision=highest)
        value_part = jnp.dot(batch_keys, weight, preferred_element_type=jnp.float32)
        if earlier is not None:
            value_part = value_part + jnp.dot(keys_full, earlier, precision=highest)
        return lax.psum((gram_part, value_part), "row")

    first_keys = local_keys[:key_count]
    second_keys = local_keys[key_count:]
    first_panel = key_panel(0, key_count)
    gram_one, values_one = reduce_batch(first_keys, first_panel, None)
    factor_one = factorize(gram_one)
    solved_one = solve_with(factor_one, targets_full[0] - values_one)
    delta_one = jnp.dot(first_panel, solved_one, precision=highest)
    cross_part = jnp.dot(first_panel.T, second_keys.astype(jnp.float32).T, precision=highest)
    cross_terms = lax.psum(cross_part, "row")
    second_panel = key_panel(key_count, 2 * key_count) - jnp.dot(
        first_panel, solve_with(factor_one, cross_terms), precision=highest
    )
    gram_two, values_two = reduce_batch(second_keys, second_panel, delta_one)
    factor_two = factorize(gram_two)
    solved_two = solve_with(factor_two, targets_full[1] - values_two)
    change = delta_one + jnp.dot(second_panel, solved_two, precision=highest)
    return (math.sqrt(F) * change).astype(jnp.bfloat16)


def solution(mesh):
    in_specs = (P("row", "col"), P(None, "row"), P("row", "col"), P(), P(None, None, "col"))
    out_specs = P("row", "col")
    return jax.shard_map(shards, mesh=mesh, in_specs=in_specs, out_specs=out_specs, check_vma=False)
```

profile of v0, /device:TPU:1, one launch (start us, length us, event | category | flops | bytes accessed | tf_op | source)
XLA Modules:
  0.0 1001.9 jit_solution(16634637840187185980)
XLA Ops:
  6.5 2.6 copy.18
  9.2 4.3 gather_fusion
  14.7 2.8 convolution_bitcast_fusion.1
  19.5 139.1 %all-reduce.15.cloned.1.call-done = f32[1152,256]{0,1:T(8,128)} async-done(((f32[1152,256]{0,1:T(8,128)}), f32[1152,256]{0,1:T(8,128)}) %all-reduce.15.cloned.1.call-update) | async-done | bytes 1179664
  160.5 60.0 %all-gather.5.cloned.1.call-done = f32[32,36,256]{2,1,0:T(8,128)} async-done(((f32[1,36,256]{2,1,0:T(8,128)}), f32[32,36,256]{2,1,0:T(8,128)}) %all-gather.5.cloned.1.call-update) | async-done | bytes 1179664 | tf_op jit(solution)/shard_map/all_gather | solution.py:35
  220.5 2.4 reshape.122
  222.9 1.9 dynamic-slice_select_fusion.1
  224.9 2.2 fusion.16
  227.1 2.8 convolution_bitcast_fusion
  229.9 122.1 %all-reduce.11.cloned.1.call-done = f32[576,256]{1,0:T(8,128)} async-done(((f32[576,256]{1,0:T(8,128)}), f32[576,256]{1,0:T(8,128)}) %all-reduce.11.cloned.1.call-update) | async-done | bytes 589840 | tf_op jit(solution)/shard_map/psum | solution.py:13
  351.9 2.5 fusion.30
  354.5 1.4 fusion.18
  356.4 2.1 convert_element_type.20
  359.7 140.8 %all-reduce.19.cloned.1.call-done = (f32[256,448]{0,1:T(8,128)}, f32[256,256]{0,1:T(8,128)}, f32[1152,256]{0,1:T(8,128)}, f32[256,256]{1,0:T(8,128)}) async-done(((f32[256,448]{0,1:T(8,128)}, f32[256,256]{0,1:T(8,128)}, f32[1152,256]{0,1:T(8,128)}, f32[256,256]{1,0:T(8,128)}), (f32[256,448]{0,1:T(8,128)}, f32[256,256]{0,1:T(8,128)}, f32[1152,256]{0,1:T(8,128)}, ...) | async-done | bytes 2162704 | tf_op jit(solution)/shard_map/psum | solution.py:53
  500.5 1.7 convert_add_fusion.1
  502.2 1.8 copy.21
  505.7 11.7 %cholesky.130 = f32[128,128]{1,0:T(8,128)S(1)} custom-call(f32[128,128]{1,0:T(8,128)S(1)} %cholesky.194), custom_call_target="Cholesky" | custom-call | tf_op jit(solution)/shard_map/jit(cholesky)/cholesky | solution.py:42
  518.2 9.8 custom-call.23
  528.0 1.7 constant_dynamic-update-slice_fusion.2
  530.8 11.7 %cholesky.147 = f32[128,128]{1,0:T(8,128)S(1)} custom-call(f32[128,128]{1,0:T(8,128)S(1)} %convolution_subtract_fusion.8), custom_call_target="Cholesky" | custom-call | tf_op jit(solution)/shard_map/jit(cholesky)/cholesky | solution.py:42
  545.0 1.7 select_select_fusion.1
  546.8 18.0 %while.5 = (s32[]{:T(128)}, f32[256,256]{1,0:T(8,128)}, s32[2,2]{1,0:T(2,128)S(1)}, f32[2,128,128]{2,1,0:T(8,128)S(1)}, s32[]{:T(128)}) while((s32[]{:T(128)}, f32[256,256]{1,0:T(8,128)}, s32[2,2]{1,0:T(2,128)S(1)}, f32[2,128,128]{2,1,0:T(8,128)S(1)}, s32[]{:T(128)}) %tuple.46), condition=%wide.while_cond, body=%wide.while_body.sunk | while | flops 2 | bytes 131181 | solution.py:45
  559.8 2.2 bitcast_dynamic-update-slice_fusion.4
  562.7 2.1 bitcast_dynamic-update-slice_fusion.4
  565.5 20.5 %custom-call.24 = f32[2,128,128]{1,2,0:T(8,128)S(1)} custom-call(f32[2,128,128]{2,1,0:T(8,128)} %copy-done.16), custom_call_target="InvertDiagBlocksLowerTriangular" | custom-call | tf_op jit(solution)/shard_map/jit(_cho_solve)/triangular_solve | solution.py:45
  587.8 1.9 convolution_subtract_fusion.6
  589.7 1.7 dynamic-slice_bitcast_fusion
  591.4 1.6 copy.22
  593.1 1.3 fusion.49
  594.7 2.0 convolution_subtract_fusion.5
  600.9 50.8 %all-gather.7.cloned.1.call-done = f32[32,36,256]{2,1,0:T(8,128)} async-done(((f32[1,36,256]{2,1,0:T(8,128)}), f32[32,36,256]{2,1,0:T(8,128)}) %all-gather.7.cloned.1.call-update) | async-done | bytes 1179664 | tf_op jit(solution)/shard_map/all_gather | solution.py:35
  651.7 2.4 reshape.124
  654.1 1.9 dynamic-slice_select_fusion
  656.1 1.9 fusion.46
  657.9 2.5 fusion.4
  661.4 1.5 convolution_add_fusion.1
  663.0 120.2 %all-reduce.13.cloned.1.call-done = f32[576,256]{1,0:T(8,128)} async-done(((f32[576,256]{1,0:T(8,128)}), f32[576,256]{1,0:T(8,128)}) %all-reduce.13.cloned.1.call-update) | async-done | bytes 589840 | tf_op jit(solution)/shard_map/psum | solution.py:13
  783.1 1.9 convolution_subtract_fusion
  785.9 1.4 fusion.28
  787.4 140.5 %all-reduce.17.cloned.1.call-done = (f32[256,448]{0,1:T(8,128)}, f32[256,256]{0,1:T(8,128)}) async-done(((f32[256,448]{0,1:T(8,128)}, f32[256,256]{0,1:T(8,128)}), (f32[256,448]{0,1:T(8,128)}, f32[256,256]{0,1:T(8,128)})) %all-reduce.17.cloned.1.call-update) | async-done | bytes 720912 | tf_op jit(solution)/shard_map/psum | solution.py:53
  929.1 11.7 %cholesky.164 = f32[128,128]{1,0:T(8,128)S(1)} custom-call(f32[128,128]{1,0:T(8,128)S(1)} %cholesky.197), custom_call_target="Cholesky" | custom-call | tf_op jit(solution)/shard_map/jit(cholesky)/cholesky | solution.py:42
  940.9 9.8 custom-call.25
  951.2 11.9 %cholesky.181 = f32[128,128]{1,0:T(8,128)S(1)} custom-call(f32[128,128]{1,0:T(8,128)S(1)} %convolution_subtract_fusion.7), custom_call_target="Cholesky" | custom-call | tf_op jit(solution)/shard_map/jit(cholesky)/cholesky | solution.py:42
  965.8 4.0 while.6
  966.4 1.4 bitcast_dynamic-update-slice_fusion.5
  968.3 1.4 bitcast_dynamic-update-slice_fusion.5
  969.7 19.7 %custom-call.26 = f32[2,128,128]{1,2,0:T(8,128)S(1)} custom-call(f32[2,128,128]{2,1,0:T(8,128)S(1)} %get-tuple-element.30), custom_call_target="InvertDiagBlocksLowerTriangular" | custom-call | tf_op jit(solution)/shard_map/jit(_cho_solve)/triangular_solve | solution.py:45
  992.8 2.1 fusion.1
  (107 shorter events, 29.0 us)
Async XLA Ops:
  6.5 8.2 copy-start
  6.5 2.6 copy-start.17
  6.5 152.1 %all-reduce.15.cloned.1.call-start = ((), (), s32[]{:S(2)}) async-start(), calls=%async_computation.4 | async-start | bytes 2359296
  17.6 202.9 %all-gather.5.cloned.1.call-start = ((), (), s32[]{:S(2)}) async-start(), calls=%async_computation.2 | async-start | bytes 1351680 | tf_op jit(solution)/shard_map/all_gather | solution.py:35
  160.4 191.5 %all-reduce.11.cloned.1.call-start = ((), (), s32[]{:S(2)}) async-start(), calls=%async_computation | async-start | bytes 1179648 | tf_op jit(solution)/shard_map/psum | solution.py:13
  224.8 275.7 %all-reduce.19.cloned.1.call-start = ((), (), s32[]{:S(2)}) async-start(), calls=%async_computation.6 | async-start | bytes 4325376 | tf_op jit(solution)/shard_map/psum | solution.py:53
  351.9 2.5 copy-start.3
  355.9 295.7 %all-gather.7.cloned.1.call-start = ((), (), s32[]{:S(2)}) async-start(), calls=%async_computation.3 | async-start | bytes 1351680 | tf_op jit(solution)/shard_map/all_gather | solution.py:35
  356.4 2.1 copy-start.8
  505.0 0.7 copy-start.15
  564.8 0.7 copy-start.16
  587.2 0.7 copy-start.13
  593.0 190.1 %all-reduce.13.cloned.1.call-start = ((), (), s32[]{:S(2)}) async-start(), calls=%async_computation.1 | async-start | bytes 1179648 | tf_op jit(solution)/shard_map/psum | solution.py:13
  593.1 3.6 copy-start.6
  594.7 2.0 copy-start.11
  594.7 3.4 copy-start.7
  599.1 0.7 copy-start.9
  656.0 271.9 %all-reduce.17.cloned.1.call-start = ((), (), s32[]{:S(2)}) async-start(), calls=%async_computation.5 | async-start | bytes 1441792 | tf_op jit(solution)/shard_map/psum | solution.py:53
  656.1 5.4 copy-start.10
  660.4 1.0 copy-start.1
  661.4 121.7 %copy-start.12 = (f32[128,256]{1,0:T(8,128)S(1)}, f32[128,256]{1,0:T(8,128)}, u32[]{:S(2)}) copy-start(f32[128,256]{1,0:T(8,128)} %copy-done.11) | copy-start | bytes 393220
  785.1 0.8 copy-start.4
  927.9 1.2 copy-start.14
  991.3 1.4 copy-start.2
  991.3 1.4 copy-start.5
Sparse Core Ops, SparseCore 0:
  17.7 140.9 all-reduce.14
  161.8 58.6 all-gather.4
  224.9 126.9 all-reduce.10
  356.1 144.3 all-reduce.18
  593.2 58.4 all-gather.6
  656.1 126.9 all-reduce.12
  787.5 140.3 all-reduce.16
where the time goes:
time: 1010 us; the launch traced here: 1000 us
  waiting for transfers between devices  774 us (77%)
  other arithmetic  125 us (12%)
  matrix products  38.9 us (4%)
  local copies, waits for them, and re-layouts  34.5 us (3%)
  between operations  17.3 us (2%)
  loops' own time  12.4 us (1%)
    psum x2, waiting for transfers between devices, reduce_batch(): return lax.psum((gram_part, value_part), 'row')  281 us
    psum x2, waiting for transfers between devices, spread(): return lax.psum(kept, axis)  242 us
    unnamed x8, waiting for transfers between devices  139 us
    all_gather x2, waiting for transfers between devices, key_panel(): gathered = lax.all_gather(shares, 'row', axis=0, tiled=True)  111 us
    another operation x13, other arithmetic, factorize(): return jnp.linalg.cholesky(identity + gram_matrix)  69.4 us
    another operation x5, other arithmetic, solve_with(): return jax.scipy.linalg.cho_solve((factor, True), rhs)  41.9 us
  transfers between devices with their start and end apart: 7, of which 7 were waited for; matrix products, arithmetic and copies ran while one was open for 2% of the time, Pallas kernels for 0%

commit v1 on v0

v1 whole, which is shorter than its diff:
```python
import math

import jax
import jax.numpy as jnp
from jax import lax
from jax.experimental import pallas as pl
from jax.experimental.pallas import tpu as pltpu
from jax.sharding import PartitionSpec as P

F = 18432
LANES = 128
HIGHEST = lax.Precision.HIGHEST


def split(value):
    high = value.astype(jnp.bfloat16)
    return high, (value - high.astype(jnp.float32)).astype(jnp.bfloat16)


def dot16(a, b):
    return jnp.dot(a, b, preferred_element_type=jnp.float32)


def solve_kernel(gram_ref, target_ref, value_ref, out_ref, a_ref, high_ref, low_ref, z_ref, s_ref, r_ref):
    n = a_ref.shape[0]
    blocks = n // LANES
    rows = lax.broadcasted_iota(jnp.int32, (LANES, LANES), 0)
    cols = lax.broadcasted_iota(jnp.int32, (LANES, LANES), 1)
    eye = jnp.where(rows == cols, 1.0, 0.0).astype(jnp.float32)
    place = 0
    for i in range(blocks):
        for j in range(i + 1):
            block = gram_ref[place * LANES:(place + 1) * LANES, :]
            place += 1
            if i == j:
                a_ref[i * LANES:(i + 1) * LANES, j * LANES:(j + 1) * LANES] = block + eye
            else:
                a_ref[i * LANES:(i + 1) * LANES, j * LANES:(j + 1) * LANES] = block
                a_ref[j * LANES:(j + 1) * LANES, i * LANES:(i + 1) * LANES] = block.T
    a = a_ref[...]
    top = jnp.maximum(jnp.max(jnp.sum(jnp.abs(a), axis=0)), 1.0)
    r_ref[...] = target_ref[...].astype(jnp.float32) - value_ref[...]
    big_rows = lax.broadcasted_iota(jnp.int32, (n, n), 0)
    big_cols = lax.broadcasted_iota(jnp.int32, (n, n), 1)
    one = jnp.where(big_rows == big_cols, 1.0, 0.0).astype(jnp.float32)
    middle = top + 1.0
    width = top - 1.0
    scale = 2.0 * middle * middle - width * width
    first, second = 8.0 * middle / scale, 8.0 / scale
    rho = width * width / scale
    limit = jnp.max(jnp.abs(r_ref[...])) * 1e-5

    def refine(residual_of, apply):
        def more(carry):
            step, worst = carry
            return jnp.logical_and(step < 12, worst > limit)

        def body(carry):
            step, _ = carry
            residual = residual_of(out_ref[...])
            out_ref[...] += apply(residual)
            return step + 1, jnp.max(jnp.abs(residual))

        lax.while_loop(more, body, (jnp.int32(0), 2.0 * limit))

    @pl.when(top <= 32.0)
    def _():
        high, low = split(a)
        high_ref[...] = high
        low_ref[...] = low
        s_ref[...] = one - first * a + second * dot16(high, high)
        z_ref[...] = first * one - second * a

        def body(rho):
            s16 = s_ref[...].astype(jnp.bfloat16)
            z16 = z_ref[...].astype(jnp.bfloat16)
            z_ref[...] += dot16(z16, s16)
            s_ref[...] = dot16(s16, s16)
            return rho * rho

        lax.while_loop(lambda rho: rho > 0.004, body, rho)
        high_ref2 = z_ref[...].astype(jnp.bfloat16)
        s_ref[...] = high_ref2.astype(jnp.float32)
        out_ref[...] = dot16(high_ref2, r_ref[...].astype(jnp.bfloat16))

        def residual_of(y):
            y_high, y_low = split(y)
            return r_ref[...] - (
                dot16(high_ref[...], y_high) + (dot16(high_ref[...], y_low) + dot16(low_ref[...], y_high))
            )

        refine(residual_of, lambda res: dot16(s_ref[...].astype(jnp.bfloat16), res.astype(jnp.bfloat16)))

    @pl.when(top > 32.0)
    def _():
        def full(x, y):
            return jnp.dot(x, y, precision=HIGHEST, preferred_element_type=jnp.float32)

        z_ref[...] = first * one - second * a

        def body(carry):
            rho, extra = carry
            s_ref[...] = one - full(a_ref[...], z_ref[...])
            z_ref[...] += full(z_ref[...], s_ref[...])
            return rho * rho, jnp.where(rho < 0.01, extra + 1, extra)

        lax.while_loop(lambda carry: carry[1] < 2, body, (rho, jnp.int32(0)))
        out_ref[...] = full(z_ref[...], r_ref[...])
        refine(lambda y: r_ref[...] - full(a_ref[...], y), lambda res: full(z_ref[...], res))


def solve(gram_packed, targets, values):
    n, width = targets.shape
    square = pltpu.VMEM((n, n), jnp.float32)
    half = pltpu.VMEM((n, n), jnp.bfloat16)
    return pl.pallas_call(
        solve_kernel,
        out_shape=jax.ShapeDtypeStruct((n, width), jnp.float32),
        in_specs=[pl.BlockSpec(memory_space=pltpu.VMEM)] * 3,
        out_specs=pl.BlockSpec(memory_space=pltpu.VMEM),
        scratch_shapes=[square, half, half, square, square, pltpu.VMEM((n, width), jnp.float32)],
        compiler_params=pltpu.CompilerParams(vmem_limit_bytes=48 * 2**20),
    )(gram_packed, targets, values)


def dot_exact_right(a, b16, dims):
    high = lax.reduce_precision(a, 8, 7)
    low = a - high
    out = lax.dot_general(high.astype(jnp.bfloat16), b16, dims, preferred_element_type=jnp.float32)
    return out + lax.dot_general(low.astype(jnp.bfloat16), b16, dims, preferred_element_type=jnp.float32)


def shards(inverse_cov, key_table, weight, edit_index, targets):
    rows = lax.axis_size("row")
    cols = lax.axis_size("col")
    chips = rows // 2
    here, depth = inverse_cov.shape[0], inverse_cov.shape[1]
    n = edit_index.size
    width = weight.shape[1]
    piece = here // chips
    core = lax.axis_index("row") % 2
    table_rows = key_table.shape[0]
    turned = [((2 * a + h) * cols + b, (2 * b + h) * cols + a) for a in range(chips) for b in range(cols) for h in range(2)]
    same_core = [[2 * k + h for k in range(chips)] for h in range(2)]
    other_core = [(r, r ^ 1) for r in range(rows)]

    picked = (lax.broadcasted_iota(jnp.int32, (table_rows, n), 0) == edit_index.reshape(1, n)).astype(jnp.bfloat16)
    keys = lax.dot_general(key_table, picked, (((0,), (0,)), ((), ()))).astype(jnp.bfloat16)
    key_slice = lax.dynamic_slice_in_dim(keys, lax.axis_index("col") * piece, piece, 0)
    key_piece = lax.ppermute(key_slice, ("row", "col"), turned)

    part = dot_exact_right(inverse_cov, keys, (((0,), (0,)), ((), ())))
    value = lax.dot_general(keys, weight, (((0,), (0,)), ((), ())), preferred_element_type=jnp.float32)
    part = part.reshape(2, chips, piece, n)
    value = jnp.pad(value, ((0, 0), (0, n - width))).reshape(chips, 2, n // rows, n)

    def half(which):
        return jnp.concatenate(
            [
                lax.dynamic_index_in_dim(part, which, 0, keepdims=False),
                lax.dynamic_index_in_dim(value, which, 1, keepdims=False),
            ],
            axis=1,
        )

    half_sum = half(core) + lax.ppermute(half(1 - core), "row", other_core)
    received = lax.all_to_all(half_sum, "row", 0, 0, axis_index_groups=same_core, tiled=True)
    summed = jnp.sum(received, axis=0)
    panel_piece = summed[:piece]
    value_piece = summed[piece:, :width]
    values = lax.all_gather(value_piece, "row", axis=0, tiled=True)
    panel_turned = lax.ppermute(panel_piece, ("row", "col"), turned)
    panel = lax.all_gather(panel_turned, "col", axis=0, tiled=True)

    gram_part = lax.dot_general(
        key_piece.astype(jnp.float32), panel_piece, (((0,), (0,)), ((), ())), precision=HIGHEST
    )
    blocks = n // LANES
    packed = jnp.concatenate(
        [
            gram_part[i * LANES:(i + 1) * LANES, j * LANES:(j + 1) * LANES]
            for i in range(blocks)
            for j in range(i + 1)
        ],
        axis=0,
    )
    share = packed.shape[0] // rows
    gram_share = jnp.sum(lax.all_to_all(packed.reshape(rows, share, LANES), "row", 0, 0, tiled=True), axis=0)
    gram_share = jnp.sum(
        lax.all_to_all(jnp.broadcast_to(gram_share, (cols, share, LANES)), "col", 0, 0, tiled=True), axis=0
    )
    gram = lax.all_to_all(jnp.broadcast_to(gram_share, (rows, share, LANES)), "row", 0, 0, tiled=True)
    gram = gram.reshape(rows * share, LANES)
    solved = solve(gram, targets.reshape(n, width), values)
    return (math.sqrt(F) * jnp.dot(panel, solved, precision=HIGHEST)).astype(jnp.bfloat16)


def solution(mesh):
    in_specs = (P("row", "col"), P(None, "row"), P("row", "col"), P(), P(None, None, "col"))
    out_specs = P("row", "col")
    return jax.shard_map(shards, mesh=mesh, in_specs=in_specs, out_specs=out_specs, check_vma=False)
```

time: 1010 us -> 232 us (0.23)
  waiting for transfers between devices: 774 us -> 41.7 us
  other arithmetic: 125 us -> 0.89 us
  blocking collectives: 0 us -> 79 us
  Pallas kernels: 0 us -> 35.4 us
  matrix products: 38.9 us -> 9.18 us
  starting transfers between devices: 0.63 us -> 25.2 us
  loops' own time: 12.4 us -> 0 us
  local copies, waits for them, and re-layouts: 34.5 us -> 23.4 us
    psum x4 -> x0, waiting for transfers between devices: 524 us -> none  [the longest x2 281 us: reduce_batch(): return lax.psum((gram_part, value_part), 'row')]
    unnamed x8 -> x1, waiting for transfers between devices: 139 us -> 0.02 us
    another operation x18 -> x0, other arithmetic: 111 us -> none  [the longest x13 69.4 us: factorize(): return jnp.linalg.cholesky(identity + gram_matrix)]
    all_gather x2 -> x1, waiting for transfers between devices: 111 us -> 0.01 us  [shards(): panel = lax.all_gather(panel_turned, 'col', axis=0, tiled=True)]
    all_to_all x0 -> x1, blocking collectives: none -> 49.5 us  [shards(): lax.all_to_all(jnp.broadcast_to(gram_share, (cols, share, LANES)), 'col',...]
    all_to_all x0 -> x3, waiting for transfers between devices: none -> 39.5 us  [the longest x1 27.9 us: shards(): lax.all_to_all(half_sum, 'row', 0, 0, axis_index_groups=same_core, tiled=...]
    pallas_call x0 -> x1, Pallas kernels: none -> 35.4 us  [solve(): pl.pallas_call(solve_kernel, out_shape=jax.ShapeDtypeStruct((n, width), j...]
    all_gather x0 -> x1, blocking collectives: none -> 29.5 us  [shards(): values = lax.all_gather(value_piece, 'row', axis=0, tiled=True)]
  transfers between devices with their start and end apart: 7 -> 7, of which waited for: 7 -> 3; matrix products, arithmetic and copies ran while one was open for 2% -> 2% of each run, Pallas kernels for 0% -> 0%
where the time goes in v1:
time: 232 us; the launch traced here: 229 us
  blocking collectives  79 us (34%)
  waiting for transfers between devices  41.7 us (18%)
  Pallas kernels  35.4 us (15%)
  starting transfers between devices  25.2 us (11%)
  local copies, waits for them, and re-layouts  23.4 us (10%)
  between operations  13.7 us (6%)
  matrix products  9.18 us (4%)
    all_to_all x1, blocking collectives, shards(): lax.all_to_all(jnp.broadcast_to(gram_share, (cols, share, LANES)), 'col',...  49.5 us
    pallas_call x1, Pallas kernels, solve(): pl.pallas_call(solve_kernel, out_shape=jax.ShapeDtypeStruct((n, width), j...  35.4 us
    all_gather x1, blocking collectives, shards(): values = lax.all_gather(value_piece, 'row', axis=0, tiled=True)  29.5 us
    all_to_all x1, waiting for transfers between devices, shards(): lax.all_to_all(half_sum, 'row', 0, 0, axis_index_groups=same_core, tiled=...  27.9 us
    all_to_all x1, waiting for transfers between devices, shards(): lax.all_to_all(packed.reshape(rows, share, LANES), 'row', 0, 0, tiled=True)  11.6 us
    unnamed x27, local copies, waits for them, and re-layouts  11 us
    ppermute x1, starting transfers between devices, shards(): half_sum = half(core) + lax.ppermute(half(1 - core), 'row', other_core)  8.78 us
    all_to_all x1, starting transfers between devices, shards(): lax.all_to_all(jnp.broadcast_to(gram_share, (rows, share, LANES)), 'row',...  6.59 us
  transfers between devices with their start and end apart: 7, of which 3 were waited for; matrix products, arithmetic and copies ran while one was open for 2% of the time, Pallas kernels for 0%

profile of v1, /device:TPU:1, one launch (start us, length us, event | category | flops | bytes accessed | tf_op | source)
XLA Modules:
  0.0 228.5 jit_solution(5841926361327312333)
XLA Ops:
  6.5 0.8 copy.44
  7.3 0.5 copy-done
  7.8 0.8 fusion.1
  8.7 0.9 copy-done.1
  9.6 1.2 convolution_bitcast_fusion
  10.8 2.7 %convolution_add_fusion = f32[1152,512]{0,1:T(8,128)} fusion(f32[1152,512]{0,1:T(8,128)S(1)} %convolution_bitcast_fusion, bf16[512,576]{0,1:T(8,128)(2,1)S(1)} %fusion.1, f32[576,1152]{1,0:T(8,128)S(1)} %copy-done.1), kind=kOutput, calls=%fused_computation.2 | convolution fusion | flops 682057728 | bytes 7962624 | tf_op jit(solution)/shard_map/dot_general | solution.py:130
  13.5 2.0 copy.34
  15.5 1.6 reshape.17
  17.2 1.9 constant_dynamic-slice_fusion.1
  19.1 0.7 copy.47
  19.8 0.3 copy-done.3
  20.2 0.2 copy-done.5
  20.4 0.6 fusion.7
  21.2 0.3 copy.39
  21.5 0.1 pad_maximum_fusion
  21.6 8.8 %collective-permute-start = (f32[16,52,512]{2,0,1:T(8,128)S(1)}, f32[16,52,512]{2,0,1:T(8,128)S(1)}, u32[]{:S(2)}, u32[]{:S(2)}) collective-permute-start(f32[16,52,512]{2,0,1:T(8,128)S(1)} %pad_maximum_fusion), channel_id=1, source_target_pairs={{0,16},{16,0},{32,48},{48,32},{64,80},{80,64},{96,112},{112,96},{1... | collective-permute-start | bytes 5111816 | tf_op jit(solution)/shard_map/ppermute | solution.py:166
  30.4 0.7 copy.48
  31.1 0.3 copy.37
  31.4 2.2 collective-permute-done
  33.6 0.5 maximum_add_fusion
  34.2 2.3 copy.40
  36.4 3.7 %all-to-all-start = ((f32[16,52,512]{2,1,0:T(8,128)}), f32[16,52,512]{2,1,0:T(8,128)S(1)}, u32[]{:S(2)}, u32[]{:S(2)}) async-start(f32[16,52,512]{2,1,0:T(8,128)} %copy.40), calls=%async_computation | async-start | bytes 3670016 | tf_op jit(solution)/shard_map/all_to_all | solution.py:167
  40.1 0.8 dynamic-slice_bitcast_fusion.2
  41.0 0.7 collective-permute-start.2
  41.6 27.9 %all-to-all-done = f32[16,52,512]{2,1,0:T(8,128)S(1)} async-done(((f32[16,52,512]{2,1,0:T(8,128)}), f32[16,52,512]{2,1,0:T(8,128)S(1)}, u32[]{:S(2)}, u32[]{:S(2)}) %all-to-all-start) | async-done | bytes 1703968 | tf_op jit(solution)/shard_map/all_to_all | solution.py:167
  69.5 0.1 reduce_sum.27
  69.7 0.6 fusion.5
  70.3 0.7 slice_dynamic-update-slice_fusion
  71.0 0.6 slice_dynamic-update-slice_fusion.8
  71.6 0.6 slice_dynamic-update-slice_fusion.7
  72.2 0.6 slice_dynamic-update-slice_fusion.6
  72.8 0.6 slice_dynamic-update-slice_fusion.5
  73.5 0.6 slice_dynamic-update-slice_fusion.4
  74.1 0.6 slice_dynamic-update-slice_fusion.3
  74.7 0.6 slice_dynamic-update-slice_fusion.2
  75.3 0.6 slice_dynamic-update-slice_fusion.1
  76.0 4.8 %all-to-all-start.1 = ((f32[32,40,128]{2,1,0:T(8,128)}), f32[32,40,128]{2,1,0:T(8,128)S(1)}, u32[]{:S(2)}, u32[]{:S(2)}) async-start(f32[32,40,128]{2,1,0:T(8,128)} %bitcast.8), calls=%async_computation.1 | async-start | bytes 1310720 | tf_op jit(solution)/shard_map/all_to_all | solution.py:188
  80.8 0.7 collective-permute-start.1
  81.5 0.6 copy-done.7
  82.2 11.6 %all-to-all-done.1 = f32[32,40,128]{2,1,0:T(8,128)S(1)} async-done(((f32[32,40,128]{2,1,0:T(8,128)}), f32[32,40,128]{2,1,0:T(8,128)S(1)}, u32[]{:S(2)}, u32[]{:S(2)}) %all-to-all-start.1) | async-done | bytes 655392 | tf_op jit(solution)/shard_map/all_to_all | solution.py:188
  93.9 49.5 %all_to_all.20 = f32[16,40,128]{2,1,0:T(8,128)S(1)} all-to-all(f32[16,40,128]{2,1,0:T(8,128)S(1)} %broadcast_in_dim.6), channel_id=1, replica_groups=mesh['row'=32,'col'=16] {'col'}, dimensions={0} | all-to-all | bytes 655360 | tf_op jit(solution)/shard_map/all_to_all | solution.py:190
  143.4 0.9 broadcast_in_dim.7
  144.3 6.6 %all-to-all-start.3 = ((f32[32,40,128]{2,1,0:T(8,128)}), f32[32,40,128]{2,1,0:T(8,128)S(1)}, u32[]{:S(2)}, u32[]{:S(2)}) async-start(f32[32,40,128]{2,1,0:T(8,128)} %broadcast_in_dim.7), calls=%async_computation.3 | async-start | bytes 1310720 | tf_op jit(solution)/shard_map/all_to_all | solution.py:192
  150.9 0.2 copy.41
  151.1 29.5 %all_gather.7.value_ref = f32[512,448]{1,0:T(8,128)S(1)} all-gather(f32[16,448]{1,0:T(8,128)S(1)} %slice.56), channel_id=1, replica_groups=mesh['row'=32,'col'=16] {'row'}, dimensions={0}, use_global_device_ids=true | all-gather | bytes 946176 | tf_op jit(solution)/shard_map/all_gather | solution.py:171
  180.6 2.4 %reshape.23 = f32[576,512]{1,0:T(8,128)} reshape(f32[16,36,512]{2,1,0:T(8,128)} %all-gather.3.cloned.1.call-done) | data formatting | bytes 2359296
  183.0 35.4 %shard_map.55 = f32[512,448]{1,0:T(8,128)S(1)} custom-call(f32[1280,128]{1,0:T(8,128)S(1)} %bitcast.29, bf16[512,448]{1,0:T(8,128)(2,1)S(1)} %bitcast.30, f32[512,448]{1,0:T(8,128)S(1)} %all_gather.7.value_ref), custom_call_target="tpu_custom_call" | custom-call | tf_op jit(solution)/shard_map/pallas_call | solution.py:116
  218.5 3.2 %fusion.3 = bf16[576,448]{0,1:T(8,128)(2,1)} fusion(f32[576,512]{1,0:T(8,128)S(1)} %copy-done.4, f32[512,448]{1,0:T(8,128)S(1)} %shard_map.55), kind=kOutput, calls=%fused_computation.10 | convolution fusion | flops 1585963008 | bytes 2613248 | tf_op jit(solution)/shard_map/dot_general | solution.py:195
  (24 shorter events, 0.4 us)
Async XLA Ops:
  6.5 1.3 copy-start
  7.8 1.7 copy-start.1
  9.6 1.2 copy-start.2
  19.1 1.1 copy-start.3
  19.1 1.2 copy-start.5
  21.6 12.0 %collective-permute-start = (f32[16,52,512]{2,0,1:T(8,128)S(1)}, f32[16,52,512]{2,0,1:T(8,128)S(1)}, u32[]{:S(2)}, u32[]{:S(2)}) collective-permute-start(f32[16,52,512]{2,0,1:T(8,128)S(1)} %pad_maximum_fusion), channel_id=1, source_target_pairs={{0,16},{16,0},{32,48},{48,32},{64,80},{80,64},{96,112},{112,96},{1... | collective-permute-start | bytes 5111816 | tf_op jit(solution)/shard_map/ppermute | solution.py:166
  36.4 33.1 %all-to-all-start = ((f32[16,52,512]{2,1,0:T(8,128)}), f32[16,52,512]{2,1,0:T(8,128)S(1)}, u32[]{:S(2)}, u32[]{:S(2)}) async-start(f32[16,52,512]{2,1,0:T(8,128)} %copy.40), calls=%async_computation | async-start | bytes 3670016 | tf_op jit(solution)/shard_map/all_to_all | solution.py:167
  41.0 28.7 %collective-permute-start.2 = (bf16[36,512]{1,0:T(8,128)(2,1)S(1)}, bf16[36,512]{1,0:T(8,128)(2,1)S(1)}, u32[]{:S(2)}, u32[]{:S(2)}) collective-permute-start(bf16[36,512]{1,0:T(8,128)(2,1)S(1)} %dynamic-slice_bitcast_fusion.2), channel_id=1, source_target_pairs={{0,0},{16,16},{1,32},{17,48},{2,64},{18,80},{3,96},{19,112},{4,128... | collective-permute-start | bytes 110600 | tf_op jit(solution)/shard_map/ppermute | solution.py:150
  76.0 17.8 %all-to-all-start.1 = ((f32[32,40,128]{2,1,0:T(8,128)}), f32[32,40,128]{2,1,0:T(8,128)S(1)}, u32[]{:S(2)}, u32[]{:S(2)}) async-start(f32[32,40,128]{2,1,0:T(8,128)} %bitcast.8), calls=%async_computation.1 | async-start | bytes 1310720 | tf_op jit(solution)/shard_map/all_to_all | solution.py:188
  80.7 99.9 %all-gather.3.cloned.1.call-start = ((), (), s32[]{:S(2)}) async-start(), calls=%async_computation.4 | async-start | bytes 1392640 | tf_op jit(solution)/shard_map/all_gather | solution.py:173
  80.8 0.7 collective-permute-start.1
  81.5 0.6 copy-start.7
  93.8 57.0 %copy-start.6 = (bf16[2,256,448]{1,2,0:T(8,128)(2,1)S(1)}, bf16[2,256,448]{1,2,0:T(8,128)(2,1)}, u32[]{:S(2)}) copy-start(bf16[2,256,448]{1,2,0:T(8,128)(2,1)} %param.9) | copy-start | bytes 1376260
  144.3 38.8 %all-to-all-start.3 = ((f32[32,40,128]{2,1,0:T(8,128)}), f32[32,40,128]{2,1,0:T(8,128)S(1)}, u32[]{:S(2)}, u32[]{:S(2)}) async-start(f32[32,40,128]{2,1,0:T(8,128)} %broadcast_in_dim.7), calls=%async_computation.3 | async-start | bytes 1310720 | tf_op jit(solution)/shard_map/all_to_all | solution.py:192
  183.0 35.4 %copy-start.4 = (f32[576,512]{1,0:T(8,128)S(1)}, f32[576,512]{1,0:T(8,128)}, u32[]{:S(2)}) copy-start(f32[576,512]{1,0:T(8,128)} %reshape.23) | copy-start | bytes 3538948
Sparse Core Ops, SparseCore 0:
  83.7 93.1 all-gather.2

commit v2 on v1

--- a/solution.py
+++ b/solution.py
@@ -9,6 +9,10 @@
 
 F = 18432
 LANES = 128
+VMEM_LIMIT = 48 * 2**20
+TALL, SHORT, PADDED = 40, 32, 48
+STRIDE = 4
+SHIFTS = (0, 1, 2, -1)
 HIGHEST = lax.Precision.HIGHEST
 
 
@@ -39,7 +43,7 @@
                 a_ref[j * LANES:(j + 1) * LANES, i * LANES:(i + 1) * LANES] = block.T
     a = a_ref[...]
     top = jnp.maximum(jnp.max(jnp.sum(jnp.abs(a), axis=0)), 1.0)
-    r_ref[...] = target_ref[...].astype(jnp.float32) - value_ref[...]
+    r_ref[...] = target_ref[...].astype(jnp.float32) - value_ref[:, :r_ref.shape[1]]
     big_rows = lax.broadcasted_iota(jnp.int32, (n, n), 0)
     big_cols = lax.broadcasted_iota(jnp.int32, (n, n), 1)
     one = jnp.where(big_rows == big_cols, 1.0, 0.0).astype(jnp.float32)
@@ -119,80 +123,178 @@
         in_specs=[pl.BlockSpec(memory_space=pltpu.VMEM)] * 3,
         out_specs=pl.BlockSpec(memory_space=pltpu.VMEM),
         scratch_shapes=[square, half, half, square, square, pltpu.VMEM((n, width), jnp.float32)],
-        compiler_params=pltpu.CompilerParams(vmem_limit_bytes=48 * 2**20),
+        compiler_params=pltpu.CompilerParams(vmem_limit_bytes=VMEM_LIMIT),
+        cost_estimate=pl.CostEstimate(flops=40 * n * n * n, bytes_accessed=4 * 2**20, transcendentals=0),
     )(gram_packed, targets, values)
 
 
-def dot_exact_right(a, b16, dims):
-    high = lax.reduce_precision(a, 8, 7)
-    low = a - high
-    out = lax.dot_general(high.astype(jnp.bfloat16), b16, dims, preferred_element_type=jnp.float32)
-    return out + lax.dot_general(low.astype(jnp.bfloat16), b16, dims, preferred_element_type=jnp.float32)
+def contract_first(a, b):
+    return lax.dot_general(a, b, (((0,), (0,)), ((), ())), preferred_element_type=jnp.float32)
+
+
+def piece_start(index, here, chips):
+    return index // 2 * (2 * here // chips) + index % 2 * TALL
+
+
+def front_kernel(place_ref, index_ref, table_ref, cov_ref, weight_ref, mine_ref, other_ref, slice_ref, part_ref, value_ref):
+    here, n = table_ref.shape[1], index_ref.shape[1]
+    chips = mine_ref.shape[0]
+    width = weight_ref.shape[1]
+    core, col = place_ref[0], place_ref[1]
+    picked = lax.broadcasted_iota(jnp.int32, (table_ref.shape[0], n), 0) == index_ref[...]
+    picked = jnp.where(picked, 1.0, 0.0).astype(jnp.bfloat16)
+    keys = contract_first(table_ref[...], picked).astype(jnp.bfloat16)
+    padded = slice_ref.shape[0]
+    slot = lax.broadcasted_iota(jnp.int32, (padded, here), 0)
+    spot = lax.broadcasted_iota(jnp.int32, (padded, here), 1)
+    used = TALL - lax.rem(col, 2) * (TALL - SHORT)
+    first = lax.div(col, 2) * (TALL + SHORT) + lax.rem(col, 2) * TALL
+    taken = jnp.logical_and(slot + first == spot, slot < used)
+    taken = jnp.where(taken, 1.0, 0.0).astype(jnp.bfloat16)
+    slice_ref[...] = dot16(taken, keys).astype(jnp.bfloat16)
+    high, low = split(cov_ref[...])
+    part_ref[...] = contract_first(high, keys) + contract_first(low, keys)
+    value_ref[...] = contract_first(keys, weight_ref[...])
+    for which, ref in ((core, mine_ref), (1 - core, other_ref)):
+        for j in range(chips):
+            begin = pl.multiple_of(which * here + piece_start(j, here, chips), 8)
+            tall = TALL if j % 2 == 0 else SHORT
+            ref[j, :tall, :] = part_ref[pl.ds(begin, tall), :]
+            if tall < TALL:
+                ref[j, tall:TALL, :] = jnp.zeros((TALL - tall, n), jnp.float32)
+            share = ref.shape[1] - TALL
+            at = pl.multiple_of((2 * j + which) * share, 8)
+            ref[j, TALL:, :width] = value_ref[pl.ds(at, share), :]
+            ref[j, TALL:, width:] = jnp.zeros((share, n - width), jnp.float32)
+
+
+def front(place, index, table, cov, weight, chips):
+    here, n = table.shape[1], index.shape[1]
+    share = n // (2 * chips)
+    payload = jax.ShapeDtypeStruct((chips, TALL + share, n), jnp.float32)
+    vmem = pl.BlockSpec(memory_space=pltpu.VMEM)
+    return pl.pallas_call(
+        front_kernel,
+        out_shape=(payload, payload, jax.ShapeDtypeStruct((PADDED, n), jnp.bfloat16)),
+        in_specs=[pl.BlockSpec(memory_space=pltpu.SMEM)] + [vmem] * 4,
+        out_specs=(vmem, vmem, vmem),
+        scratch_shapes=[
+            pltpu.VMEM((cov.shape[1], n), jnp.float32),
+            pltpu.VMEM((n, weight.shape[1]), jnp.float32),
+        ],
+        compiler_params=pltpu.CompilerParams(vmem_limit_bytes=VMEM_LIMIT),
+    )(place, index, table, cov, weight)
+
+
+def gram_kernel(received_ref, key_ref, panel_ref, value_ref, packed_ref):
+    total = received_ref[0]
+    for j in range(1, received_ref.shape[0]):
+        total = total + received_ref[j]
+    panel = total[:TALL]
+    panel_ref[...] = panel
+    value_ref[...] = total[TALL:]
+    n = panel.shape[1]
+    padded = jnp.concatenate([panel, jnp.zeros((PADDED - TALL, n), jnp.float32)], axis=0)
+    high = padded.astype(jnp.bfloat16)
+    rest = padded - high.astype(jnp.float32)
+    middle, low = split(rest)
+    keys = key_ref[...]
+    gram = contract_first(keys, high) + (contract_first(keys, middle) + contract_first(keys, low))
+    place = 0
+    for i in range(n // LANES):
+        for j in range(i + 1):
+            packed_ref[place * LANES:(place + 1) * LANES, :] = gram[
+                i * LANES:(i + 1) * LANES, j * LANES:(j + 1) * LANES
+            ]
+            place += 1
+
+
+def gram_share(received, key_piece):
+    n = received.shape[2]
+    blocks = n // LANES
+    vmem = pl.BlockSpec(memory_space=pltpu.VMEM)
+    return pl.pallas_call(
+        gram_kernel,
+        out_shape=(
+            jax.ShapeDtypeStruct((TALL, n), jnp.float32),
+            jax.ShapeDtypeStruct((received.shape[1] - TALL, n), jnp.float32),
+            jax.ShapeDtypeStruct((blocks * (blocks + 1) // 2 * LANES, LANES), jnp.float32),
+        ),
+        in_specs=[vmem] * 2,
+        out_specs=(vmem, vmem, vmem),
+        compiler_params=pltpu.CompilerParams(vmem_limit_bytes=VMEM_LIMIT),
+    )(received, key_piece)
+
+
+def change_kernel(place_ref, *refs):
+    *bundle_refs, solved_ref, out_ref, panel_ref = refs
+    cols = len(bundle_refs) * STRIDE
+    for shift, ref in zip(SHIFTS, bundle_refs):
+        for t in range(cols // STRIDE):
+            piece = lax.rem(place_ref[1] - shift - STRIDE * t + 2 * cols, cols)
+            odd = lax.rem(piece, 2)
+            begin = pl.multiple_of(lax.div(piece, 2) * (TALL + SHORT) + odd * TALL, 8)
+            panel_ref[pl.ds(begin, SHORT), :] = ref[t * TALL:t * TALL + SHORT, :]
+
+            @pl.when(odd == 0)
+            def _(ref=ref, t=t, begin=begin):
+                panel_ref[pl.ds(begin + SHORT, TALL - SHORT), :] = ref[t * TALL + SHORT:(t + 1) * TALL, :]
+
+    high, low = split(panel_ref[...])
+    solved_high, solved_low = split(solved_ref[...] * math.sqrt(F))
+    out = dot16(high, solved_high) + (dot16(high, solved_low) + dot16(low, solved_high))
+    out_ref[...] = out.astype(jnp.bfloat16)
+
+
+def change(place, bundles, solved, here):
+    n, width = solved.shape
+    vmem = pl.BlockSpec(memory_space=pltpu.VMEM)
+    return pl.pallas_call(
+        change_kernel,
+        out_shape=jax.ShapeDtypeStruct((here, width), jnp.bfloat16),
+        in_specs=[pl.BlockSpec(memory_space=pltpu.SMEM)] + [vmem] * (len(bundles) + 1),
+        out_specs=vmem,
+        scratch_shapes=[pltpu.VMEM((here, n), jnp.float32)],
+        compiler_params=pltpu.CompilerParams(vmem_limit_bytes=VMEM_LIMIT),
+    )(place, *bundles, solved)
+
+
+def moved(value, axis, shift):
+    size = lax.axis_size(axis)
+    return lax.ppermute(value, axis, [(i, (i + shift) % size) for i in range(size)])
 
 
 def shards(inverse_cov, key_table, weight, edit_index, targets):
     rows = lax.axis_size("row")
     cols = lax.axis_size("col")
     chips = rows // 2
-    here, depth = inverse_cov.shape[0], inverse_cov.shape[1]
+    here = inverse_cov.shape[0]
     n = edit_index.size
     width = weight.shape[1]
-    piece = here // chips
-    core = lax.axis_index("row") % 2
-    table_rows = key_table.shape[0]
+    place = jnp.stack([lax.axis_index("row") % 2, lax.axis_index("col")]).astype(jnp.int32)
     turned = [((2 * a + h) * cols + b, (2 * b + h) * cols + a) for a in range(chips) for b in range(cols) for h in range(2)]
     same_core = [[2 * k + h for k in range(chips)] for h in range(2)]
     other_core = [(r, r ^ 1) for r in range(rows)]
 
-    picked = (lax.broadcasted_iota(jnp.int32, (table_rows, n), 0) == edit_index.reshape(1, n)).astype(jnp.bfloat16)
-    keys = lax.dot_general(key_table, picked, (((0,), (0,)), ((), ()))).astype(jnp.bfloat16)
-    key_slice = lax.dynamic_slice_in_dim(keys, lax.axis_index("col") * piece, piece, 0)
+    mine, other, key_slice = front(place, edit_index.reshape(1, n), key_table, inverse_cov, weight, chips)
     key_piece = lax.ppermute(key_slice, ("row", "col"), turned)
-
-    part = dot_exact_right(inverse_cov, keys, (((0,), (0,)), ((), ())))
-    value = lax.dot_general(keys, weight, (((0,), (0,)), ((), ())), preferred_element_type=jnp.float32)
-    part = part.reshape(2, chips, piece, n)
-    value = jnp.pad(value, ((0, 0), (0, n - width))).reshape(chips, 2, n // rows, n)
-
-    def half(which):
-        return jnp.concatenate(
-            [
-                lax.dynamic_index_in_dim(part, which, 0, keepdims=False),
-                lax.dynamic_index_in_dim(value, which, 1, keepdims=False),
-            ],
-            axis=1,
-        )
-
-    half_sum = half(core) + lax.ppermute(half(1 - core), "row", other_core)
+    half_sum = mine + lax.ppermute(other, "row", other_core)
     received = lax.all_to_all(half_sum, "row", 0, 0, axis_index_groups=same_core, tiled=True)
-    summed = jnp.sum(received, axis=0)
-    panel_piece = summed[:piece]
-    value_piece = summed[piece:, :width]
+    panel_piece, value_piece, packed = gram_share(received, key_piece)
     values = lax.all_gather(value_piece, "row", axis=0, tiled=True)
-    panel_turned = lax.ppermute(panel_piece, ("row", "col"), turned)
-    panel = lax.all_gather(panel_turned, "col", axis=0, tiled=True)
-
-    gram_part = lax.dot_general(
-        key_piece.astype(jnp.float32), panel_piece, (((0,), (0,)), ((), ())), precision=HIGHEST
-    )
-    blocks = n // LANES
-    packed = jnp.concatenate(
-        [
-            gram_part[i * LANES:(i + 1) * LANES, j * LANES:(j + 1) * LANES]
-            for i in range(blocks)
-            for j in range(i + 1)
-        ],
-        axis=0,
-    )
+
+    near = lax.ppermute(panel_piece, ("row", "col"), turned)
     share = packed.shape[0] // rows
-    gram_share = jnp.sum(lax.all_to_all(packed.reshape(rows, share, LANES), "row", 0, 0, tiled=True), axis=0)
-    gram_share = jnp.sum(
-        lax.all_to_all(jnp.broadcast_to(gram_share, (cols, share, LANES)), "col", 0, 0, tiled=True), axis=0
-    )
-    gram = lax.all_to_all(jnp.broadcast_to(gram_share, (rows, share, LANES)), "row", 0, 0, tiled=True)
-    gram = gram.reshape(rows * share, LANES)
-    solved = solve(gram, targets.reshape(n, width), values)
-    return (math.sqrt(F) * jnp.dot(panel, solved, precision=HIGHEST)).astype(jnp.bfloat16)
+    part = jnp.sum(lax.all_to_all(packed.reshape(rows, share, LANES), "row", 0, 0, tiled=True), axis=0)
+    part, near = lax.optimization_barrier((part, near))
+    far = [moved(near, "col", STRIDE * t) for t in range(1, cols // STRIDE)]
+    part = jnp.sum(lax.all_to_all(jnp.broadcast_to(part, (cols, share, LANES)), "col", 0, 0, tiled=True), axis=0)
+    part, *far = lax.optimization_barrier((part, *far))
+    far = jnp.concatenate([near] + far, axis=0)
+    bundles = [far] + [moved(far, "col", shift) for shift in SHIFTS[1:]]
+    gram = lax.all_to_all(jnp.broadcast_to(part, (rows, share, LANES)), "row", 0, 0, tiled=True)
+    solved = solve(gram.reshape(rows * share, LANES), targets.reshape(n, width), values)
+    return change(place, bundles, solved, here)
 
 
 def solution(mesh):

time: 232 us -> 215 us (0.927); the launches traced: 229 us -> 214 us
  blocking collectives: 79 us -> 0 us
  starting transfers between devices: 25.2 us -> 81.9 us
  waiting for transfers between devices: 41.7 us -> 66.2 us
  local copies, waits for them, and re-layouts: 23.4 us -> 6.17 us
  matrix products: 9.18 us -> 0 us
  Pallas kernels: 35.4 us -> 44.4 us
    all_to_all x1 -> x0, blocking collectives: 49.5 us -> none  [shards(): lax.all_to_all(jnp.broadcast_to(gram_share, (cols, share, LANES)), 'col',...]
    ppermute x2 -> x8, starting transfers between devices: 9.45 us -> 39 us  [the longest x6 29.6 us: moved(): lax.ppermute(value, axis, [(i, (i + shift) % size) for i in range(size)])]
    all_gather x1 -> x0, blocking collectives: 29.5 us -> none  [shards(): values = lax.all_gather(value_piece, 'row', axis=0, tiled=True)]
    all_to_all x1 -> x2, starting transfers between devices: 6.59 us -> 32.2 us  [the longest x1 26.7 us: shards(): lax.all_to_all(jnp.broadcast_to(part, (cols, share, LANES)), 'col', 0, 0,...]
    ppermute x2 -> x8, waiting for transfers between devices: 2.2 us -> 19.9 us  [the longest x6 16.6 us: moved(): lax.ppermute(value, axis, [(i, (i + shift) % size) for i in range(size)])]
    pallas_call x0 -> x3, Pallas kernels: none -> 8.74 us  [the longest x1 5.32 us: front(): pl.pallas_call(front_kernel, out_shape=(payload, payload, jax.ShapeDtypeS...]
    dot_general x5 -> x0, matrix products: 8.57 us -> none  [the longest x1 3.22 us: shards(): jnp.dot(panel, solved, precision=HIGHEST)]
    unnamed x27 -> x15, local copies, waits for them, and re-layouts: 11 us -> 3.45 us
  transfers between devices with their start and end apart: 7 -> 14, of which waited for: 3 -> 7; matrix products, arithmetic and copies ran while one was open for 2% -> 1% of each run, Pallas kernels for 0% -> 17%
where the time goes in v2:
time: 215 us; the launch traced here: 214 us
  starting transfers between devices  81.9 us (38%)
  waiting for transfers between devices  66.2 us (31%)
  Pallas kernels  44.4 us (21%)
  between operations  13.7 us (6%)
  local copies, waits for them, and re-layouts  6.17 us (3%)
    pallas_call x1, Pallas kernels, solve(): pl.pallas_call(solve_kernel, out_shape=jax.ShapeDtypeStruct((n, width), j...  35.6 us
    ppermute x6, starting transfers between devices, moved(): lax.ppermute(value, axis, [(i, (i + shift) % size) for i in range(size)])  29.6 us
    all_to_all x1, waiting for transfers between devices, shards(): lax.all_to_all(half_sum, 'row', 0, 0, axis_index_groups=same_core, tiled=...  29 us
    all_to_all x1, starting transfers between devices, shards(): lax.all_to_all(jnp.broadcast_to(part, (cols, share, LANES)), 'col', 0, 0,...  26.7 us
    ppermute x6, waiting for transfers between devices, moved(): lax.ppermute(value, axis, [(i, (i + shift) % size) for i in range(size)])  16.6 us
    all_to_all x1, waiting for transfers between devices, shards(): lax.all_to_all(packed.reshape(rows, share, LANES), 'row', 0, 0, tiled=True)  11.5 us
    ppermute x1, starting transfers between devices, shards(): half_sum = mine + lax.ppermute(other, 'row', other_core)  8.79 us
    all_to_all x1, starting transfers between devices, shards(): lax.all_to_all(packed.reshape(rows, share, LANES), 'row', 0, 0, tiled=True)  6.19 us
  transfers between devices with their start and end apart: 14, of which 7 were waited for; matrix products, arithmetic and copies ran while one was open for 1% of the time, Pallas kernels for 17%

profile of v2, /device:TPU:1, one launch (start us, length us, event | category | flops | bytes accessed | tf_op | source)
XLA Modules:
  0.0 214.1 jit_solution(6146824535770901840)
XLA Ops:
  6.5 0.0 copy-start.1
  6.5 0.0 copy-start.3
  6.5 1.7 copy.10.table_ref
  8.3 0.0 copy-done.1
  8.3 0.2 copy.11.weight_ref
  8.5 0.0 copy-done.3
  8.6 0.1 pad_add_fusion.place_ref
  8.7 5.3 %shard_map.55 = (f32[16,56,512]{2,1,0:T(8,128)S(1)}, f32[16,56,512]{2,1,0:T(8,128)S(1)}, bf16[48,512]{1,0:T(8,128)(2,1)S(1)}) custom-call(s32[2]{0:T(128)S(1)} %pad_add_fusion.place_ref, s32[1,512]{1,0:T(1,128)S(1)} %bitcast.10, bf16[1024,576]{1,0:T(8,128)(2,1)S(1)} %copy.10.table_ref, f32[576,1152]{1,0:T(8,128)} %cov_ref.1, ...), custom_call_target="tpu_custom_call" | custom-call | tf_op jit(solution)/shard_map/pallas_call | solution.py:176
  14.0 8.8 %collective-permute-start = (f32[16,56,512]{2,1,0:T(8,128)S(1)}, f32[16,56,512]{2,1,0:T(8,128)S(1)}, u32[]{:S(2)}, u32[]{:S(2)}) collective-permute-start(f32[16,56,512]{2,1,0:T(8,128)S(1)} %get-tuple-element.18), channel_id=1, source_target_pairs={{0,16},{16,0},{32,48},{48,32},{64,80},{80,64},{96,112},{112,96},{1... | collective-permute-start | bytes 5505032 | tf_op jit(solution)/shard_map/ppermute | solution.py:281
  22.8 3.4 %collective-permute-done = f32[16,56,512]{2,1,0:T(8,128)S(1)} collective-permute-done((f32[16,56,512]{2,1,0:T(8,128)S(1)}, f32[16,56,512]{2,1,0:T(8,128)S(1)}, u32[]{:S(2)}, u32[]{:S(2)}) %collective-permute-start) | collective-permute-done | bytes 1835040 | tf_op jit(solution)/shard_map/ppermute | solution.py:281
  26.2 1.7 add.8
  27.8 3.7 %all-to-all-start = ((f32[16,56,512]{2,1,0:T(8,128)}), f32[16,56,512]{2,1,0:T(8,128)S(1)}, u32[]{:S(2)}, u32[]{:S(2)}) async-start(f32[16,56,512]{2,1,0:T(8,128)} %add.8), calls=%async_computation | async-start | bytes 3670016 | tf_op jit(solution)/shard_map/all_to_all | solution.py:282
  31.5 0.7 collective-permute-start.1
  32.2 0.0 collective-permute-done.1.key_ref
  32.2 29.0 %all-to-all-done.received_ref = f32[16,56,512]{2,1,0:T(8,128)S(1)} async-done(((f32[16,56,512]{2,1,0:T(8,128)}), f32[16,56,512]{2,1,0:T(8,128)S(1)}, u32[]{:S(2)}, u32[]{:S(2)}) %all-to-all-start) | async-done | bytes 1835040 | tf_op jit(solution)/shard_map/all_to_all | solution.py:282
  61.2 1.5 shard_map.56
  62.7 6.2 %all-to-all-start.1 = ((f32[32,40,128]{2,1,0:T(8,128)}), f32[32,40,128]{2,1,0:T(8,128)S(1)}, u32[]{:S(2)}, u32[]{:S(2)}) async-start(f32[32,40,128]{2,1,0:T(8,128)} %bitcast.2), calls=%async_computation.1 | async-start | bytes 1310720 | tf_op jit(solution)/shard_map/all_to_all | solution.py:288
  68.9 0.0 all-gather.2.cloned.1.call-start
  69.0 0.7 all-gather.2.cloned.1.call-update
  69.7 0.7 collective-permute-start.2
  70.3 11.5 %all-to-all-done.1 = f32[32,40,128]{2,1,0:T(8,128)S(1)} async-done(((f32[32,40,128]{2,1,0:T(8,128)}), f32[32,40,128]{2,1,0:T(8,128)S(1)}, u32[]{:S(2)}, u32[]{:S(2)}) %all-to-all-start.1) | async-done | bytes 655392 | tf_op jit(solution)/shard_map/all_to_all | solution.py:288
  81.8 0.1 reduce_sum.18
  81.9 0.0 collective-permute-done.2
  81.9 0.7 broadcast_in_dim.6
  82.6 26.7 %all-to-all-start.2 = ((f32[16,40,128]{2,1,0:T(8,128)}), f32[16,40,128]{2,1,0:T(8,128)S(1)}, u32[]{:S(2)}, u32[]{:S(2)}) async-start(f32[16,40,128]{2,1,0:T(8,128)} %broadcast_in_dim.6), calls=%async_computation.2 | async-start | bytes 655360 | tf_op jit(solution)/shard_map/all_to_all | solution.py:291
  109.4 7.2 %collective-permute-start.3 = (f32[40,512]{1,0:T(8,128)S(1)}, f32[40,512]{1,0:T(8,128)S(1)}, u32[]{:S(2)}, u32[]{:S(2)}) collective-permute-start(f32[40,512]{1,0:T(8,128)S(1)} %collective-permute-done.2), channel_id=1, source_target_pairs={{0,4},{1,5},{2,6},{3,7},{4,8},{5,9},{6,10},{7,11},{8,12},{9,13},{1... | collective-permute-start | bytes 245768 | tf_op jit(solution)/shard_map/ppermute | solution.py:264
  116.5 7.0 %collective-permute-start.4 = (f32[40,512]{1,0:T(8,128)S(1)}, f32[40,512]{1,0:T(8,128)S(1)}, u32[]{:S(2)}, u32[]{:S(2)}) collective-permute-start(f32[40,512]{1,0:T(8,128)S(1)} %collective-permute-done.2), channel_id=1, source_target_pairs={{0,8},{1,9},{2,10},{3,11},{4,12},{5,13},{6,14},{7,15},{8,0},{9,1},... | collective-permute-start | bytes 245768 | tf_op jit(solution)/shard_map/ppermute | solution.py:264
  123.6 7.0 %collective-permute-start.5 = (f32[40,512]{1,0:T(8,128)S(1)}, f32[40,512]{1,0:T(8,128)S(1)}, u32[]{:S(2)}, u32[]{:S(2)}) collective-permute-start(f32[40,512]{1,0:T(8,128)S(1)} %collective-permute-done.2), channel_id=1, source_target_pairs={{0,12},{1,13},{2,14},{3,15},{4,0},{5,1},{6,2},{7,3},{8,4},{9,5},{1... | collective-permute-start | bytes 245768 | tf_op jit(solution)/shard_map/ppermute | solution.py:264
  130.6 0.9 all-to-all-done.2
  131.5 1.6 collective-permute-done.3
  133.1 15.0 %collective-permute-done.4 = f32[40,512]{1,0:T(8,128)S(1)} collective-permute-done((f32[40,512]{1,0:T(8,128)S(1)}, f32[40,512]{1,0:T(8,128)S(1)}, u32[]{:S(2)}, u32[]{:S(2)}) %collective-permute-start.4) | collective-permute-done | bytes 81952 | tf_op jit(solution)/shard_map/ppermute | solution.py:264
  148.1 0.0 collective-permute-done.5
  148.1 0.9 broadcast_in_dim.7
  149.0 5.5 %all-to-all-start.3 = ((f32[32,40,128]{2,1,0:T(8,128)}), f32[32,40,128]{2,1,0:T(8,128)S(1)}, u32[]{:S(2)}, u32[]{:S(2)}) async-start(f32[32,40,128]{2,1,0:T(8,128)} %broadcast_in_dim.7), calls=%async_computation.3 | async-start | bytes 1310720 | tf_op jit(solution)/shard_map/all_to_all | solution.py:295
  154.5 0.0 copy-done.2
  154.5 0.2 copy.12
  154.8 1.9 collective-permute-start.6
  156.7 1.9 collective-permute-start.7
  158.6 4.6 %collective-permute-start.8 = (f32[160,512]{1,0:T(8,128)S(1)}, f32[160,512]{1,0:T(8,128)S(1)}, u32[]{:S(2)}, u32[]{:S(2)}) collective-permute-start(f32[160,512]{1,0:T(8,128)S(1)} %constant_dynamic-update-slice_fusion.refs_0_), channel_id=1, source_target_pairs={{0,15},{1,0},{2,1},{3,2},{4,3},{5,4},{6,5},{7,6},{8,7},{9,8},{10,9... | collective-permute-start | bytes 983048 | tf_op jit(solution)/shard_map/ppermute | solution.py:264
  163.2 0.0 all-gather.2.cloned.1.call-done.value_ref
  163.2 4.2 %all-to-all-done.3 = f32[32,40,128]{2,1,0:T(8,128)S(1)} async-done(((f32[32,40,128]{2,1,0:T(8,128)}), f32[32,40,128]{2,1,0:T(8,128)S(1)}, u32[]{:S(2)}, u32[]{:S(2)}) %all-to-all-start.3) | async-done | bytes 655392 | tf_op jit(solution)/shard_map/all_to_all | solution.py:295
  167.4 1.2 copy-done
  168.6 35.6 %shard_map.57.refs_4_ = f32[512,448]{1,0:T(8,128)S(1)} custom-call(f32[1280,128]{1,0:T(8,128)S(1)} %bitcast.8, bf16[512,448]{1,0:T(8,128)(2,1)S(1)} %bitcast.9, f32[512,512]{1,0:T(8,128)S(1)} %copy-done), custom_call_target="tpu_custom_call" | custom-call | flops 5368709120 | bytes 4194304 | tf_op jit(solution)/shard_map/pallas_call | solution.py:120
  204.2 0.0 collective-permute-done.6.refs_1_
  204.2 0.0 collective-permute-done.7.refs_2_
  204.2 0.0 collective-permute-done.8.refs_3_
  204.3 1.9 shard_map.58
  206.2 1.1 copy.13
  (8 shorter events, 0.1 us)
Async XLA Ops:
  6.5 1.8 copy-start.1
  6.5 2.0 copy-start.3
  14.0 12.2 %collective-permute-start = (f32[16,56,512]{2,1,0:T(8,128)S(1)}, f32[16,56,512]{2,1,0:T(8,128)S(1)}, u32[]{:S(2)}, u32[]{:S(2)}) collective-permute-start(f32[16,56,512]{2,1,0:T(8,128)S(1)} %get-tuple-element.18), channel_id=1, source_target_pairs={{0,16},{16,0},{32,48},{48,32},{64,80},{80,64},{96,112},{112,96},{1... | collective-permute-start | bytes 5505032 | tf_op jit(solution)/shard_map/ppermute | solution.py:281
  27.8 33.4 %all-to-all-start = ((f32[16,56,512]{2,1,0:T(8,128)}), f32[16,56,512]{2,1,0:T(8,128)S(1)}, u32[]{:S(2)}, u32[]{:S(2)}) async-start(f32[16,56,512]{2,1,0:T(8,128)} %add.8), calls=%async_computation | async-start | bytes 3670016 | tf_op jit(solution)/shard_map/all_to_all | solution.py:282
  31.5 0.7 collective-permute-start.1
  62.7 19.1 %all-to-all-start.1 = ((f32[32,40,128]{2,1,0:T(8,128)}), f32[32,40,128]{2,1,0:T(8,128)S(1)}, u32[]{:S(2)}, u32[]{:S(2)}) async-start(f32[32,40,128]{2,1,0:T(8,128)} %bitcast.2), calls=%async_computation.1 | async-start | bytes 1310720 | tf_op jit(solution)/shard_map/all_to_all | solution.py:288
  68.9 94.3 %all-gather.2.cloned.1.call-start = ((), (), s32[]{:S(2)}) async-start(), calls=%async_computation.4 | async-start | bytes 1081344 | tf_op jit(solution)/shard_map/all_gather | solution.py:284
  69.7 12.2 %collective-permute-start.2 = (f32[40,512]{1,0:T(8,128)S(1)}, f32[40,512]{1,0:T(8,128)S(1)}, u32[]{:S(2)}, u32[]{:S(2)}) collective-permute-start(f32[40,512]{1,0:T(8,128)S(1)} %get-tuple-element.21), channel_id=1, source_target_pairs={{0,0},{16,16},{1,32},{17,48},{2,64},{18,80},{3,96},{19,112},{4,128... | collective-permute-start | bytes 245768 | tf_op jit(solution)/shard_map/ppermute | solution.py:286
  81.9 72.6 %copy-start.2 = (bf16[2,256,448]{1,2,0:T(8,128)(2,1)S(1)}, bf16[2,256,448]{1,2,0:T(8,128)(2,1)}, u32[]{:S(2)}) copy-start(bf16[2,256,448]{1,2,0:T(8,128)(2,1)} %param.9) | copy-start | bytes 1376260
  82.6 48.8 %all-to-all-start.2 = ((f32[16,40,128]{2,1,0:T(8,128)}), f32[16,40,128]{2,1,0:T(8,128)S(1)}, u32[]{:S(2)}, u32[]{:S(2)}) async-start(f32[16,40,128]{2,1,0:T(8,128)} %broadcast_in_dim.6), calls=%async_computation.2 | async-start | bytes 655360 | tf_op jit(solution)/shard_map/all_to_all | solution.py:291
  109.4 23.7 %collective-permute-start.3 = (f32[40,512]{1,0:T(8,128)S(1)}, f32[40,512]{1,0:T(8,128)S(1)}, u32[]{:S(2)}, u32[]{:S(2)}) collective-permute-start(f32[40,512]{1,0:T(8,128)S(1)} %collective-permute-done.2), channel_id=1, source_target_pairs={{0,4},{1,5},{2,6},{3,7},{4,8},{5,9},{6,10},{7,11},{8,12},{9,13},{1... | collective-permute-start | bytes 245768 | tf_op jit(solution)/shard_map/ppermute | solution.py:264
  116.5 31.5 %collective-permute-start.4 = (f32[40,512]{1,0:T(8,128)S(1)}, f32[40,512]{1,0:T(8,128)S(1)}, u32[]{:S(2)}, u32[]{:S(2)}) collective-permute-start(f32[40,512]{1,0:T(8,128)S(1)} %collective-permute-done.2), channel_id=1, source_target_pairs={{0,8},{1,9},{2,10},{3,11},{4,12},{5,13},{6,14},{7,15},{8,0},{9,1},... | collective-permute-start | bytes 245768 | tf_op jit(solution)/shard_map/ppermute | solution.py:264
  123.6 24.5 %collective-permute-start.5 = (f32[40,512]{1,0:T(8,128)S(1)}, f32[40,512]{1,0:T(8,128)S(1)}, u32[]{:S(2)}, u32[]{:S(2)}) collective-permute-start(f32[40,512]{1,0:T(8,128)S(1)} %collective-permute-done.2), channel_id=1, source_target_pairs={{0,12},{1,13},{2,14},{3,15},{4,0},{5,1},{6,2},{7,3},{8,4},{9,5},{1... | collective-permute-start | bytes 245768 | tf_op jit(solution)/shard_map/ppermute | solution.py:264
  149.0 18.4 %all-to-all-start.3 = ((f32[32,40,128]{2,1,0:T(8,128)}), f32[32,40,128]{2,1,0:T(8,128)S(1)}, u32[]{:S(2)}, u32[]{:S(2)}) async-start(f32[32,40,128]{2,1,0:T(8,128)} %broadcast_in_dim.7), calls=%async_computation.3 | async-start | bytes 1310720 | tf_op jit(solution)/shard_map/all_to_all | solution.py:295
  154.8 49.5 %collective-permute-start.6 = (f32[160,512]{1,0:T(8,128)S(1)}, f32[160,512]{1,0:T(8,128)S(1)}, u32[]{:S(2)}, u32[]{:S(2)}) collective-permute-start(f32[160,512]{1,0:T(8,128)S(1)} %constant_dynamic-update-slice_fusion.refs_0_), channel_id=1, source_target_pairs={{0,1},{1,2},{2,3},{3,4},{4,5},{5,6},{6,7},{7,8},{8,9},{9,10},{10,1... | collective-permute-start | bytes 983048 | tf_op jit(solution)/shard_map/ppermute | solution.py:264
  156.7 47.6 %collective-permute-start.7 = (f32[160,512]{1,0:T(8,128)S(1)}, f32[160,512]{1,0:T(8,128)S(1)}, u32[]{:S(2)}, u32[]{:S(2)}) collective-permute-start(f32[160,512]{1,0:T(8,128)S(1)} %constant_dynamic-update-slice_fusion.refs_0_), channel_id=1, source_target_pairs={{0,2},{1,3},{2,4},{3,5},{4,6},{5,7},{6,8},{7,9},{8,10},{9,11},{10,... | collective-permute-start | bytes 983048 | tf_op jit(solution)/shard_map/ppermute | solution.py:264
  158.6 45.6 %collective-permute-start.8 = (f32[160,512]{1,0:T(8,128)S(1)}, f32[160,512]{1,0:T(8,128)S(1)}, u32[]{:S(2)}, u32[]{:S(2)}) collective-permute-start(f32[160,512]{1,0:T(8,128)S(1)} %constant_dynamic-update-slice_fusion.refs_0_), channel_id=1, source_target_pairs={{0,15},{1,0},{2,1},{3,2},{4,3},{5,4},{6,5},{7,6},{8,7},{9,8},{10,9... | collective-permute-start | bytes 983048 | tf_op jit(solution)/shard_map/ppermute | solution.py:264
  167.4 1.2 copy-start
Sparse Core Ops, SparseCore 0:
  72.9 63.3 all-gather.1

commit v3 on v2

v3 whole, which is shorter than its diff:
```python
import math

import jax
import jax.numpy as jnp
from jax import lax
from jax.experimental import pallas as pl
from jax.experimental.pallas import tpu as pltpu
from jax.sharding import PartitionSpec as P

F = 18432
LANES = 128
HIGHEST = lax.Precision.HIGHEST
VMEM_LIMIT = 48 * 2**20
TALL, SHORT, PADDED = 40, 32, 48
V_SHORT = 24
STRIDE = 4
SHIFTS = (0, 1, 2, -1)


def split(value):
    high = value.astype(jnp.bfloat16)
    return high, (value - high.astype(jnp.float32)).astype(jnp.bfloat16)


def dot16(a, b):
    return jnp.dot(a, b, preferred_element_type=jnp.float32)


def solve_kernel(gram_ref, target_hbm, value_hbm, high_out, low_out, a_ref, a16_ref, z_ref, s_ref, r_ref, y_ref, target_ref, value_ref, sems):
    n = a_ref.shape[0]
    width = r_ref.shape[0]
    target_copy = pltpu.make_async_copy(target_hbm, target_ref, sems.at[0])
    value_copy = pltpu.make_async_copy(value_hbm, value_ref, sems.at[1])
    target_copy.start()
    value_copy.start()
    blocks = n // LANES
    rows = lax.broadcasted_iota(jnp.int32, (LANES, LANES), 0)
    cols = lax.broadcasted_iota(jnp.int32, (LANES, LANES), 1)
    eye = jnp.where(rows == cols, 1.0, 0.0).astype(jnp.float32)
    place = 0
    for i in range(blocks):
        for j in range(i + 1):
            block = gram_ref[place * LANES:(place + 1) * LANES, :]
            place += 1
            if i == j:
                a_ref[i * LANES:(i + 1) * LANES, j * LANES:(j + 1) * LANES] = block + eye
            else:
                a_ref[i * LANES:(i + 1) * LANES, j * LANES:(j + 1) * LANES] = block
                a_ref[j * LANES:(j + 1) * LANES, i * LANES:(i + 1) * LANES] = block.T
    a = a_ref[...]
    top = jnp.maximum(jnp.max(jnp.sum(jnp.abs(a), axis=0)), 1.0)
    high = a.astype(jnp.bfloat16)
    a16_ref[0] = high
    a16_ref[1] = (a - high.astype(jnp.float32)).astype(jnp.bfloat16)
    middle = top + 1.0
    span = top - 1.0
    scale = 2.0 * middle * middle - span * span
    first, second = 8.0 * middle / scale, 8.0 / scale
    rho = span * span / scale

    def add_eye(ref, times):
        for i in range(blocks):
            at = slice(i * LANES, (i + 1) * LANES)
            ref[at, at] += eye * times

    def load_residual():
        target_copy.wait()
        value_copy.wait()
        per_batch = target_ref.shape[2]
        share = value_ref.shape[1]
        for b in range(target_ref.shape[0]):
            r_ref[:, b * per_batch:(b + 1) * per_batch] = target_ref[b].astype(jnp.float32)
        half = n // 2
        for r in range(value_ref.shape[0]):
            k, h = r // 2, r % 2
            tall = 2 * share if k % 2 == 0 else V_SHORT
            begin = k // 2 * (2 * share + V_SHORT) + k % 2 * 2 * share
            at = slice(h * half, (h + 1) * half)
            r_ref[begin:begin + share, at] -= value_ref[r, :, :half]
            r_ref[begin + share:begin + tall, at] -= value_ref[r, :tall - share, half:]

    def more(carry):
        step, before, worst, limit = carry
        return jnp.logical_and(step < 12, worst * worst > limit * before)

    def finish():
        result = y_ref[...] * math.sqrt(F)
        high, low = split(result)
        high_out[...] = high
        low_out[...] = low

    @pl.when(top <= 32.0)
    def _():
        z_ref[...] = -second * a_ref[...]
        add_eye(z_ref, first)
        s_ref[...] = second * dot16(a16_ref[0], a16_ref[0]) - first * a_ref[...]
        add_eye(s_ref, 1.0)

        def body(rho):
            s16 = s_ref[...].astype(jnp.bfloat16)
            both = dot16(jnp.concatenate([z_ref[...].astype(jnp.bfloat16), s16], axis=0), s16)
            z_ref[...] += both[:n]
            s_ref[...] = both[n:]
            return rho * rho

        lax.while_loop(lambda rho: rho * rho > 0.004, body, rho)
        z = z_ref[...]
        z16 = (z + dot16(z.astype(jnp.bfloat16), s_ref[...].astype(jnp.bfloat16))).astype(jnp.bfloat16)
        s_ref[...] = z16.astype(jnp.float32)
        load_residual()
        r = r_ref[...]
        start = dot16(r.astype(jnp.bfloat16), z16).astype(jnp.bfloat16)
        residual = r - (dot16(start, a16_ref[0]) + dot16(start, a16_ref[1]))
        y_ref[...] = start.astype(jnp.float32) + dot16(residual.astype(jnp.bfloat16), z16)
        limit = jnp.max(jnp.abs(r)) * 2e-6

        def refine(carry):
            step, _, before, limit = carry
            y = y_ref[...]
            y_high, y_low = split(y)
            residual = r_ref[...] - (
                dot16(y_high, a16_ref[0]) + (dot16(y_low, a16_ref[0]) + dot16(y_high, a16_ref[1]))
            )
            y_ref[...] = y + dot16(residual.astype(jnp.bfloat16), s_ref[...].astype(jnp.bfloat16))
            return step + 1, before, jnp.max(jnp.abs(residual)), limit

        worst = jnp.max(jnp.abs(residual))
        lax.while_loop(more, refine, (jnp.int32(0), worst, jnp.maximum(worst, 1e-30), limit))
        finish()

    @pl.when(top > 32.0)
    def _():
        def full(x, y):
            return jnp.dot(x, y, precision=HIGHEST, preferred_element_type=jnp.float32)

        z_ref[...] = -second * a_ref[...]
        add_eye(z_ref, first)

        def body(carry):
            rho, extra = carry
            s_ref[...] = -full(a_ref[...], z_ref[...])
            add_eye(s_ref, 1.0)
            z_ref[...] += full(z_ref[...], s_ref[...])
            return rho * rho, jnp.where(rho < 0.01, extra + 1, extra)

        lax.while_loop(lambda carry: carry[1] < 2, body, (rho, jnp.int32(0)))
        load_residual()
        y_ref[...] = full(r_ref[...], z_ref[...])
        size = jnp.max(jnp.abs(r_ref[...]))

        def refine(carry):
            step, _, before, limit = carry
            residual = r_ref[...] - full(y_ref[...], a_ref[...])
            y_ref[...] += full(residual, z_ref[...])
            return step + 1, before, jnp.max(jnp.abs(residual)), limit

        lax.while_loop(more, refine, (jnp.int32(0), size, jnp.maximum(size, 1e-30), size * 2e-6))
        finish()


def solve(gram_packed, targets, values):
    batches, width, per_batch = targets.shape
    n = batches * per_batch
    square = pltpu.VMEM((n, n), jnp.float32)
    wide = pltpu.VMEM((width, n), jnp.float32)
    vmem = pl.BlockSpec(memory_space=pltpu.VMEM)
    out = jax.ShapeDtypeStruct((width, n), jnp.bfloat16)
    return pl.pallas_call(
        solve_kernel,
        out_shape=(out, out),
        in_specs=[vmem, pl.BlockSpec(memory_space=pl.ANY), pl.BlockSpec(memory_space=pl.ANY)],
        out_specs=(vmem, vmem),
        scratch_shapes=[
            square,
            pltpu.VMEM((2, n, n), jnp.bfloat16),
            square,
            square,
            wide,
            wide,
            pltpu.VMEM(targets.shape, targets.dtype),
            pltpu.VMEM(values.shape, values.dtype),
            pltpu.SemaphoreType.DMA((2,)),
        ],
        compiler_params=pltpu.CompilerParams(vmem_limit_bytes=VMEM_LIMIT),
        cost_estimate=pl.CostEstimate(flops=40 * n * n * n, bytes_accessed=4 * 2**20, transcendentals=0),
    )(gram_packed, targets, values)


def contract_first(a, b):
    return lax.dot_general(a, b, (((0,), (0,)), ((), ())), preferred_element_type=jnp.float32)


def piece_start(index):
    return index // 2 * (TALL + SHORT) + index % 2 * TALL


def key_kernel(place_ref, index_ref, table_ref, keys_ref, slice_ref):
    here, n = keys_ref.shape
    col = place_ref[1]
    picked = lax.broadcasted_iota(jnp.int32, (table_ref.shape[1], n), 0) == index_ref[...]
    picked = jnp.where(picked, 1.0, 0.0).astype(jnp.bfloat16)
    keys = dot16(table_ref[...], picked).astype(jnp.bfloat16)
    keys_ref[...] = keys
    padded = slice_ref.shape[0]
    slot = lax.broadcasted_iota(jnp.int32, (padded, here), 0)
    spot = lax.broadcasted_iota(jnp.int32, (padded, here), 1)
    odd = lax.rem(col, 2)
    first = lax.div(col, 2) * (TALL + SHORT) + odd * TALL
    taken = jnp.logical_and(slot + first == spot, slot < TALL - odd * (TALL - SHORT))
    taken = jnp.where(taken, 1.0, 0.0).astype(jnp.bfloat16)
    slice_ref[...] = dot16(taken, keys).astype(jnp.bfloat16)


def select_keys(place, index, table):
    n = index.shape[1]
    vmem = pl.BlockSpec(memory_space=pltpu.VMEM)
    return pl.pallas_call(
        key_kernel,
        out_shape=(
            jax.ShapeDtypeStruct((table.shape[0], n), jnp.bfloat16),
            jax.ShapeDtypeStruct((PADDED, n), jnp.bfloat16),
        ),
        in_specs=[pl.BlockSpec(memory_space=pltpu.SMEM)] + [vmem] * 2,
        out_specs=(vmem, vmem),
        compiler_params=pltpu.CompilerParams(vmem_limit_bytes=VMEM_LIMIT),
    )(place, index, table)


def front_kernel(place_ref, keys_ref, cov_ref, weight_ref, mine_ref, other_ref, part_ref, value_ref):
    here, n = keys_ref.shape
    chips = mine_ref.shape[0]
    share = mine_ref.shape[1] - TALL
    core = place_ref[0]
    keys = keys_ref[...]
    high, low = split(cov_ref[...])
    part_ref[...] = contract_first(high, keys) + contract_first(low, keys)
    value_ref[...] = dot16(weight_ref[...], keys)
    for which, ref in ((core, mine_ref), (1 - core, other_ref)):
        lanes = pl.ds(pl.multiple_of(which * (n // 2), LANES), n // 2)
        for j in range(chips):
            begin = pl.multiple_of(which * here + piece_start(j), 8)
            tall = TALL if j % 2 == 0 else SHORT
            ref[j, :tall, :] = part_ref[pl.ds(begin, tall), :]
            if tall < TALL:
                ref[j, tall:TALL, :] = jnp.zeros((TALL - tall, n), jnp.float32)
            at = j // 2 * (2 * share + V_SHORT) + j % 2 * 2 * share
            second = share if j % 2 == 0 else V_SHORT - share
            ref[j, TALL:, :n // 2] = value_ref[at:at + share, lanes]
            ref[j, TALL:TALL + second, n // 2:] = value_ref[at + share:at + share + second, lanes]
            if second < share:
                ref[j, TALL + second:, n // 2:] = jnp.zeros((share - second, n // 2), jnp.float32)


def front(place, keys, cov, weight, chips):
    n = keys.shape[1]
    width = weight.shape[0]
    share = width // (2 * chips) + 2
    payload = jax.ShapeDtypeStruct((chips, TALL + share, n), jnp.float32)
    vmem = pl.BlockSpec(memory_space=pltpu.VMEM)
    return pl.pallas_call(
        front_kernel,
        out_shape=(payload, payload),
        in_specs=[pl.BlockSpec(memory_space=pltpu.SMEM)] + [vmem] * 3,
        out_specs=(vmem, vmem),
        scratch_shapes=[pltpu.VMEM((cov.shape[1], n), jnp.float32), pltpu.VMEM((width, n), jnp.float32)],
        compiler_params=pltpu.CompilerParams(vmem_limit_bytes=VMEM_LIMIT),
        cost_estimate=pl.CostEstimate(flops=4 * cov.size * n, bytes_accessed=8 * 2**20, transcendentals=0),
    )(place, keys, cov, weight)


def gram_kernel(received_ref, key_ref, panel_ref, value_ref, packed_ref):
    total = received_ref[0]
    for j in range(1, received_ref.shape[0]):
        total = total + received_ref[j]
    panel = total[:TALL]
    panel_ref[...] = panel
    value_ref[...] = total[TALL:]
    n = panel.shape[1]
    padded = jnp.concatenate([panel, jnp.zeros((PADDED - TALL, n), jnp.float32)], axis=0)
    high = padded.astype(jnp.bfloat16)
    rest = padded - high.astype(jnp.float32)
    middle, low = split(rest)
    keys = key_ref[...]
    gram = contract_first(keys, high) + (contract_first(keys, middle) + contract_first(keys, low))
    place = 0
    for i in range(n // LANES):
        for j in range(i + 1):
            packed_ref[place * LANES:(place + 1) * LANES, :] = gram[
                i * LANES:(i + 1) * LANES, j * LANES:(j + 1) * LANES
            ]
            place += 1


def gram_share(received, key_piece):
    n = received.shape[2]
    blocks = n // LANES
    vmem = pl.BlockSpec(memory_space=pltpu.VMEM)
    return pl.pallas_call(
        gram_kernel,
        out_shape=(
            jax.ShapeDtypeStruct((TALL, n), jnp.float32),
            jax.ShapeDtypeStruct((received.shape[1] - TALL, n), jnp.float32),
            jax.ShapeDtypeStruct((blocks * (blocks + 1) // 2 * LANES, LANES), jnp.float32),
        ),
        in_specs=[vmem] * 2,
        out_specs=(vmem, vmem, vmem),
        compiler_params=pltpu.CompilerParams(vmem_limit_bytes=VMEM_LIMIT),
    )(received, key_piece)


def change_kernel(place_ref, *refs):
    *bundle_refs, high_ref, low_ref, out_ref, panel_ref = refs
    cols = len(bundle_refs) * STRIDE
    for shift, ref in zip(SHIFTS, bundle_refs):
        for t in range(cols // STRIDE):
            piece = lax.rem(place_ref[1] - shift - STRIDE * t + 2 * cols, cols)
            odd = lax.rem(piece, 2)
            begin = pl.multiple_of(lax.div(piece, 2) * (TALL + SHORT) + odd * TALL, 8)
            panel_ref[pl.ds(begin, SHORT), :] = ref[t * TALL:t * TALL + SHORT, :]

            @pl.when(odd == 0)
            def _(ref=ref, t=t, begin=begin):
                panel_ref[pl.ds(begin + SHORT, TALL - SHORT), :] = ref[t * TALL + SHORT:(t + 1) * TALL, :]

    high, low = split(panel_ref[...])
    last = (((1,), (1,)), ((), ()))
    out = lax.dot_general(high_ref[...], high, last, preferred_element_type=jnp.float32)
    out += lax.dot_general(low_ref[...], high, last, preferred_element_type=jnp.float32)
    out += lax.dot_general(high_ref[...], low, last, preferred_element_type=jnp.float32)
    out_ref[...] = out.astype(jnp.bfloat16)


def change(place, bundles, solved, here):
    width, n = solved[0].shape
    vmem = pl.BlockSpec(memory_space=pltpu.VMEM)
    return pl.pallas_call(
        change_kernel,
        out_shape=jax.ShapeDtypeStruct((width, here), jnp.bfloat16),
        in_specs=[pl.BlockSpec(memory_space=pltpu.SMEM)] + [vmem] * (len(bundles) + 2),
        out_specs=vmem,
        scratch_shapes=[pltpu.VMEM((here, n), jnp.float32)],
        compiler_params=pltpu.CompilerParams(vmem_limit_bytes=VMEM_LIMIT),
    )(place, *bundles, *solved)


def moved(value, axis, shift):
    size = lax.axis_size(axis)
    return lax.ppermute(value, axis, [(i, (i + shift) % size) for i in range(size)])


def swapped(value, axis, groups=None):
    return lax.all_to_all(value, axis, 0, 0, axis_index_groups=groups, tiled=True)


def copies(value, count):
    return jnp.broadcast_to(value, (count, *value.shape))


def shards(inverse_cov, key_table, weight, edit_index, targets):
    rows = lax.axis_size("row")
    cols = lax.axis_size("col")
    chips = rows // 2
    here = inverse_cov.shape[0]
    n = edit_index.size
    place = jnp.stack([lax.axis_index("row") % 2, lax.axis_index("col")]).astype(jnp.int32)
    turned = [((2 * a + h) * cols + b, (2 * b + h) * cols + a) for a in range(chips) for b in range(cols) for h in range(2)]
    same_core = [[2 * k + h for k in range(chips)] for h in range(2)]
    other_core = [(r, r ^ 1) for r in range(rows)]

    keys, key_slice = select_keys(place, edit_index.reshape(1, n), key_table.T)
    key_piece = lax.ppermute(key_slice, ("row", "col"), turned)
    mine, other = front(place, keys, inverse_cov, weight.T, chips)
    half_sum = mine + lax.ppermute(other, "row", other_core)
    received = swapped(half_sum, "row", same_core)
    panel_piece, value_piece, packed = gram_share(received, key_piece)
    near = lax.ppermute(panel_piece, ("row", "col"), turned)
    share = packed.shape[0] // rows
    neighbours = [[STRIDE * g + i for i in range(STRIDE)] for g in range(cols // STRIDE)]
    part = jnp.sum(swapped(packed.reshape(rows, share, LANES), "row"), axis=0)
    part, near = lax.optimization_barrier((part, near))
    part = jnp.sum(swapped(copies(part, STRIDE), "col", neighbours), axis=0)
    part, value_piece = lax.optimization_barrier((part, value_piece))
    values = swapped(copies(value_piece, rows), "row")
    part = part + sum(moved(part, "col", STRIDE * t) for t in range(1, cols // STRIDE))
    part, near, values = lax.optimization_barrier((part, near, values))
    far = [near] + [moved(near, "col", STRIDE * t) for t in range(1, cols // STRIDE)]
    gram = swapped(copies(part, rows), "row")
    gram, *far = lax.optimization_barrier((gram, *far))
    far = jnp.concatenate(far, axis=0)
    bundles = [far] + [moved(far, "col", shift) for shift in SHIFTS[1:]]
    solved = solve(gram.reshape(rows * share, LANES), jnp.swapaxes(targets, 1, 2), values)
    return change(place, bundles, solved, here).T


def solution(mesh):
    in_specs = (P("row", "col"), P(None, "row"), P("row", "col"), P(), P(None, None, "col"))
    out_specs = P("row", "col")
    return jax.shard_map(shards, mesh=mesh, in_specs=in_specs, out_specs=out_specs, check_vma=False)
```

time: 215 us -> 218 us (1.014)
  starting transfers between devices: 81.9 us -> 97.2 us
  between operations: 13.7 us -> 0.29 us
  blocking collectives: 0 us -> 9.05 us
  waiting for transfers between devices: 66.2 us -> 58.1 us
    ppermute x6 -> x9, starting transfers between devices: 29.6 us -> 50.5 us  [moved(): lax.ppermute(value, axis, [(i, (i + shift) % size) for i in range(size)])]
    all_to_all x0 -> x1, blocking collectives: none -> 9.05 us  [swapped(): lax.all_to_all(value, axis, 0, 0, axis_index_groups=groups, tiled=True)]
    all_to_all x4, starting transfers between devices: 42.1 us -> 36.6 us  [swapped(): lax.all_to_all(value, axis, 0, 0, axis_index_groups=groups, tiled=True)]
    all_to_all x4, waiting for transfers between devices: 45.6 us -> 41.3 us  [swapped(): lax.all_to_all(value, axis, 0, 0, axis_index_groups=groups, tiled=True)]
    ppermute x6 -> x9, waiting for transfers between devices: 16.6 us -> 13.4 us  [moved(): lax.ppermute(value, axis, [(i, (i + shift) % size) for i in range(size)])]
    pallas_call x3 -> x4, Pallas kernels: 42.9 us -> 44.2 us  [the longest x1 35.5 us: solve(): pl.pallas_call(solve_kernel, out_shape=(out, out), in_specs=[vmem, pl.Blo...]
  transfers between devices with their start and end apart: 14 -> 16, of which waited for: 7 -> 6; matrix products, arithmetic and copies ran while one was open for 1% -> 0% of each run, Pallas kernels for 17% -> 16%
where the time goes in v3:
time: 218 us; the launch traced here: 217 us
  starting transfers between devices  97.2 us (45%)
  waiting for transfers between devices  58.1 us (27%)
  Pallas kernels  45.7 us (21%)
  blocking collectives  9.05 us (4%)
  local copies, waits for them, and re-layouts  5.07 us (2%)
    ppermute x9, starting transfers between devices, moved(): lax.ppermute(value, axis, [(i, (i + shift) % size) for i in range(size)])  50.5 us
    all_to_all x4, waiting for transfers between devices, swapped(): lax.all_to_all(value, axis, 0, 0, axis_index_groups=groups, tiled=True)  41.3 us
    all_to_all x4, starting transfers between devices, swapped(): lax.all_to_all(value, axis, 0, 0, axis_index_groups=groups, tiled=True)  36.6 us
    pallas_call x1, Pallas kernels, solve(): pl.pallas_call(solve_kernel, out_shape=(out, out), in_specs=[vmem, pl.Blo...  35.5 us
    ppermute x9, waiting for transfers between devices, moved(): lax.ppermute(value, axis, [(i, (i + shift) % size) for i in range(size)])  13.4 us
    all_to_all x1, blocking collectives, swapped(): lax.all_to_all(value, axis, 0, 0, axis_index_groups=groups, tiled=True)  9.05 us
    ppermute x1, starting transfers between devices, shards(): half_sum = mine + lax.ppermute(other, 'row', other_core)  8.79 us
    pallas_call x1, Pallas kernels, front(): pl.pallas_call(front_kernel, out_shape=(payload, payload), in_specs=[pl.B...  4.37 us
  transfers between devices with their start and end apart: 16, of which 6 were waited for; matrix products, arithmetic and copies ran while one was open for 0% of the time, Pallas kernels for 16%

profile of v3, /device:TPU:1, one launch (start us, length us, event | category | flops | bytes accessed | tf_op | source)
XLA Modules:
  0.0 217.1 jit_solution(9778586367161352960)
XLA Ops:
  0.0 0.7 copy.6
  0.7 0.1 pad_add_fusion.place_ref
  0.8 1.3 copy-done
  2.0 1.5 shard_map.55
  3.5 0.0 copy-start.1
  3.5 1.1 copy-done.1
  4.6 4.4 %shard_map.56 = (f32[16,56,512]{2,1,0:T(8,128)S(1)}, f32[16,56,512]{2,1,0:T(8,128)S(1)}) custom-call(s32[2]{0:T(128)S(1)} %pad_add_fusion.place_ref, bf16[576,512]{1,0:T(8,128)(2,1)S(1)} %get-tuple-element.26.keys_ref, f32[576,1152]{1,0:T(8,128)} %cov_ref.1, bf16[448,576]{1,0:T(8,128)(2,1)S(1)} %bitcast.14), custom_call_target="tpu_custom_call" | custom-call | flops 1358954496 | bytes 8388608 | tf_op jit(solution)/shard_map/pallas_call | solution.py:260
  8.9 8.8 %collective-permute-start = (f32[16,56,512]{2,1,0:T(8,128)S(1)}, f32[16,56,512]{2,1,0:T(8,128)S(1)}, u32[]{:S(2)}, u32[]{:S(2)}) collective-permute-start(f32[16,56,512]{2,1,0:T(8,128)S(1)} %get-tuple-element.28), channel_id=1, source_target_pairs={{0,16},{16,0},{32,48},{48,32},{64,80},{80,64},{96,112},{112,96},{1... | collective-permute-start | bytes 5505032 | tf_op jit(solution)/shard_map/ppermute | solution.py:373
  17.7 3.4 %collective-permute-done = f32[16,56,512]{2,1,0:T(8,128)S(1)} collective-permute-done((f32[16,56,512]{2,1,0:T(8,128)S(1)}, f32[16,56,512]{2,1,0:T(8,128)S(1)}, u32[]{:S(2)}, u32[]{:S(2)}) %collective-permute-start) | collective-permute-done | bytes 1835040 | tf_op jit(solution)/shard_map/ppermute | solution.py:373
  21.1 1.7 add.17
  22.8 3.7 %all-to-all-start = ((f32[16,56,512]{2,1,0:T(8,128)}), f32[16,56,512]{2,1,0:T(8,128)S(1)}, u32[]{:S(2)}, u32[]{:S(2)}) async-start(f32[16,56,512]{2,1,0:T(8,128)} %add.17), calls=%async_computation | async-start | bytes 3670016 | tf_op jit(solution)/shard_map/all_to_all | solution.py:352
  26.5 0.7 collective-permute-start.1
  27.2 0.0 collective-permute-done.1.key_ref
  27.2 29.0 %all-to-all-done.received_ref = f32[16,56,512]{2,1,0:T(8,128)S(1)} async-done(((f32[16,56,512]{2,1,0:T(8,128)}), f32[16,56,512]{2,1,0:T(8,128)S(1)}, u32[]{:S(2)}, u32[]{:S(2)}) %all-to-all-start) | async-done | bytes 1835040 | tf_op jit(solution)/shard_map/all_to_all | solution.py:352
  56.2 1.5 shard_map.57
  57.7 6.2 %all-to-all-start.1 = ((f32[32,40,128]{2,1,0:T(8,128)}), f32[32,40,128]{2,1,0:T(8,128)S(1)}, u32[]{:S(2)}, u32[]{:S(2)}) async-start(f32[32,40,128]{2,1,0:T(8,128)} %bitcast.4), calls=%async_computation.1 | async-start | bytes 1310720 | tf_op jit(solution)/shard_map/all_to_all | solution.py:352
  63.9 0.7 collective-permute-start.2
  64.6 12.2 %all-to-all-done.1 = f32[32,40,128]{2,1,0:T(8,128)S(1)} async-done(((f32[32,40,128]{2,1,0:T(8,128)}), f32[32,40,128]{2,1,0:T(8,128)S(1)}, u32[]{:S(2)}, u32[]{:S(2)}) %all-to-all-start.1) | async-done | bytes 655392 | tf_op jit(solution)/shard_map/all_to_all | solution.py:352
  76.8 0.1 reduce_sum.18
  76.9 0.0 collective-permute-done.2
  76.9 9.0 %all_to_all.25 = f32[4,40,128]{2,1,0:T(8,128)S(1)} all-to-all(f32[4,40,128]{2,1,0:T(8,128)S(1)} %broadcast_in_dim.9), channel_id=1, replica_groups={{0,1,2,3},{4,5,6,7},{8,9,10,11},{12,13,14,15},{16,17,18,19},{20,21,22,2..., dimensions={0} | all-to-all | bytes 163840 | tf_op jit(solution)/shard_map/all_to_all | solution.py:352
  86.0 1.1 broadcast_in_dim.10
  87.1 18.9 %all-to-all-start.3 = ((f32[32,16,512]{2,1,0:T(8,128)}), f32[32,16,512]{2,1,0:T(8,128)S(1)}, u32[]{:S(2)}, u32[]{:S(2)}) async-start(f32[32,16,512]{2,1,0:T(8,128)} %broadcast_in_dim.10), calls=%async_computation.3 | async-start | bytes 2097152 | tf_op jit(solution)/shard_map/all_to_all | solution.py:352
  106.0 0.0 copy-start.2
  106.0 11.5 %collective-permute-start.5 = (f32[40,128]{1,0:T(8,128)S(1)}, f32[40,128]{1,0:T(8,128)S(1)}, u32[]{:S(2)}, u32[]{:S(2)}) collective-permute-start(f32[40,128]{1,0:T(8,128)S(1)} %reduce_sum.19), channel_id=1, source_target_pairs={{0,12},{1,13},{2,14},{3,15},{4,0},{5,1},{6,2},{7,3},{8,4},{9,5},{1... | collective-permute-start | bytes 61448 | tf_op jit(solution)/shard_map/ppermute | solution.py:348
  117.5 5.2 %collective-permute-start.4 = (f32[40,128]{1,0:T(8,128)S(1)}, f32[40,128]{1,0:T(8,128)S(1)}, u32[]{:S(2)}, u32[]{:S(2)}) collective-permute-start(f32[40,128]{1,0:T(8,128)S(1)} %reduce_sum.19), channel_id=1, source_target_pairs={{0,8},{1,9},{2,10},{3,11},{4,12},{5,13},{6,14},{7,15},{8,0},{9,1},... | collective-permute-start | bytes 61448 | tf_op jit(solution)/shard_map/ppermute | solution.py:348
  122.8 5.7 %collective-permute-start.3 = (f32[40,128]{1,0:T(8,128)S(1)}, f32[40,128]{1,0:T(8,128)S(1)}, u32[]{:S(2)}, u32[]{:S(2)}) collective-permute-start(f32[40,128]{1,0:T(8,128)S(1)} %reduce_sum.19), channel_id=1, source_target_pairs={{0,4},{1,5},{2,6},{3,7},{4,8},{5,9},{6,10},{7,11},{8,12},{9,13},{1... | collective-permute-start | bytes 61448 | tf_op jit(solution)/shard_map/ppermute | solution.py:348
  128.5 0.0 collective-permute-done.5
  128.5 2.4 %collective-permute-done.4 = f32[40,128]{1,0:T(8,128)S(1)} collective-permute-done((f32[40,128]{1,0:T(8,128)S(1)}, f32[40,128]{1,0:T(8,128)S(1)}, u32[]{:S(2)}, u32[]{:S(2)}) %collective-permute-start.4) | collective-permute-done | bytes 20512 | tf_op jit(solution)/shard_map/ppermute | solution.py:348
  130.9 1.7 collective-permute-done.3
  132.6 0.0 all-to-all-done.3.value_hbm
  132.6 0.9 broadcast_in_dim.11
  133.6 7.8 %all-to-all-start.4 = ((f32[32,40,128]{2,1,0:T(8,128)}), f32[32,40,128]{2,1,0:T(8,128)S(1)}, u32[]{:S(2)}, u32[]{:S(2)}) async-start(f32[32,40,128]{2,1,0:T(8,128)} %broadcast_in_dim.11), calls=%async_computation.4 | async-start | bytes 1310720 | tf_op jit(solution)/shard_map/all_to_all | solution.py:352
  141.4 3.3 %collective-permute-start.8 = (f32[40,512]{1,0:T(8,128)S(1)}, f32[40,512]{1,0:T(8,128)S(1)}, u32[]{:S(2)}, u32[]{:S(2)}) collective-permute-start(f32[40,512]{1,0:T(8,128)S(1)} %collective-permute-done.2), channel_id=1, source_target_pairs={{0,12},{1,13},{2,14},{3,15},{4,0},{5,1},{6,2},{7,3},{8,4},{9,5},{1... | collective-permute-start | bytes 245768 | tf_op jit(solution)/shard_map/ppermute | solution.py:348
  144.7 9.2 %collective-permute-start.7 = (f32[40,512]{1,0:T(8,128)S(1)}, f32[40,512]{1,0:T(8,128)S(1)}, u32[]{:S(2)}, u32[]{:S(2)}) collective-permute-start(f32[40,512]{1,0:T(8,128)S(1)} %collective-permute-done.2), channel_id=1, source_target_pairs={{0,8},{1,9},{2,10},{3,11},{4,12},{5,13},{6,14},{7,15},{8,0},{9,1},... | collective-permute-start | bytes 245768 | tf_op jit(solution)/shard_map/ppermute | solution.py:348
  154.0 5.6 %collective-permute-start.6 = (f32[40,512]{1,0:T(8,128)S(1)}, f32[40,512]{1,0:T(8,128)S(1)}, u32[]{:S(2)}, u32[]{:S(2)}) collective-permute-start(f32[40,512]{1,0:T(8,128)S(1)} %collective-permute-done.2), channel_id=1, source_target_pairs={{0,4},{1,5},{2,6},{3,7},{4,8},{5,9},{6,10},{7,11},{8,12},{9,13},{1... | collective-permute-start | bytes 245768 | tf_op jit(solution)/shard_map/ppermute | solution.py:348
  159.6 0.0 collective-permute-done.8
  159.6 0.0 collective-permute-done.7
  159.6 9.3 %collective-permute-done.6 = f32[40,512]{1,0:T(8,128)S(1)} collective-permute-done((f32[40,512]{1,0:T(8,128)S(1)}, f32[40,512]{1,0:T(8,128)S(1)}, u32[]{:S(2)}, u32[]{:S(2)}) %collective-permute-start.6) | collective-permute-done | bytes 81952 | tf_op jit(solution)/shard_map/ppermute | solution.py:348
  168.9 0.0 all-to-all-done.4
  169.0 1.9 collective-permute-start.11
  170.9 5.9 %collective-permute-start.10 = (f32[160,512]{1,0:T(8,128)S(1)}, f32[160,512]{1,0:T(8,128)S(1)}, u32[]{:S(2)}, u32[]{:S(2)}) collective-permute-start(f32[160,512]{1,0:T(8,128)S(1)} %constant_dynamic-update-slice_fusion.refs_0_), channel_id=1, source_target_pairs={{0,2},{1,3},{2,4},{3,5},{4,6},{5,7},{6,8},{7,9},{8,10},{9,11},{10,... | collective-permute-start | bytes 983048 | tf_op jit(solution)/shard_map/ppermute | solution.py:348
  176.8 1.9 collective-permute-start.9
  178.8 35.5 %shard_map.58 = (bf16[448,512]{1,0:T(8,128)(2,1)S(1)}, bf16[448,512]{1,0:T(8,128)(2,1)S(1)}) custom-call(f32[1280,128]{1,0:T(8,128)S(1)} %bitcast.12, bf16[2,448,256]{2,1,0:T(8,128)(2,1)S(1)} %bitcast.15, f32[32,16,512]{2,1,0:T(8,128)S(1)} %all-to-all-done.3.value_hbm), custom_call_target="tpu_custom_call" | custom-call | flops 5368709120 | bytes 4194304 | tf_op jit(solution)/shard_map/pallas_call | solution.py:168
  214.3 0.0 collective-permute-done.11.refs_3_
  214.3 0.0 collective-permute-done.10.refs_2_
  214.3 0.0 collective-permute-done.9.refs_1_
  214.3 2.9 %shard_map.59 = bf16[448,576]{1,0:T(8,128)(2,1)} custom-call(s32[2]{0:T(128)S(1)} %pad_add_fusion.place_ref, f32[160,512]{1,0:T(8,128)S(1)} %constant_dynamic-update-slice_fusion.refs_0_, f32[160,512]{1,0:T(8,128)S(1)} %collective-permute-done.9.refs_1_, f32[160,512]{1,0:T(8,128)S(1)} %collective-permute-done.10.refs_2_, ...), custom_call_target="tpu_custom_call" | custom-call | tf_op jit(solution)/shard_map/pallas_call | solution.py:336
  (9 shorter events, 0.1 us)
Async XLA Ops:
  0.8 1.3 copy-start
  3.5 1.1 copy-start.1
  8.9 12.2 %collective-permute-start = (f32[16,56,512]{2,1,0:T(8,128)S(1)}, f32[16,56,512]{2,1,0:T(8,128)S(1)}, u32[]{:S(2)}, u32[]{:S(2)}) collective-permute-start(f32[16,56,512]{2,1,0:T(8,128)S(1)} %get-tuple-element.28), channel_id=1, source_target_pairs={{0,16},{16,0},{32,48},{48,32},{64,80},{80,64},{96,112},{112,96},{1... | collective-permute-start | bytes 5505032 | tf_op jit(solution)/shard_map/ppermute | solution.py:373
  22.8 33.4 %all-to-all-start = ((f32[16,56,512]{2,1,0:T(8,128)}), f32[16,56,512]{2,1,0:T(8,128)S(1)}, u32[]{:S(2)}, u32[]{:S(2)}) async-start(f32[16,56,512]{2,1,0:T(8,128)} %add.17), calls=%async_computation | async-start | bytes 3670016 | tf_op jit(solution)/shard_map/all_to_all | solution.py:352
  26.5 0.7 collective-permute-start.1
  57.7 19.1 %all-to-all-start.1 = ((f32[32,40,128]{2,1,0:T(8,128)}), f32[32,40,128]{2,1,0:T(8,128)S(1)}, u32[]{:S(2)}, u32[]{:S(2)}) async-start(f32[32,40,128]{2,1,0:T(8,128)} %bitcast.4), calls=%async_computation.1 | async-start | bytes 1310720 | tf_op jit(solution)/shard_map/all_to_all | solution.py:352
  63.9 13.0 %collective-permute-start.2 = (f32[40,512]{1,0:T(8,128)S(1)}, f32[40,512]{1,0:T(8,128)S(1)}, u32[]{:S(2)}, u32[]{:S(2)}) collective-permute-start(f32[40,512]{1,0:T(8,128)S(1)} %get-tuple-element.31), channel_id=1, source_target_pairs={{0,0},{16,16},{1,32},{17,48},{2,64},{18,80},{3,96},{19,112},{4,128... | collective-permute-start | bytes 245768 | tf_op jit(solution)/shard_map/ppermute | solution.py:376
  87.1 45.6 %all-to-all-start.3 = ((f32[32,16,512]{2,1,0:T(8,128)}), f32[32,16,512]{2,1,0:T(8,128)S(1)}, u32[]{:S(2)}, u32[]{:S(2)}) async-start(f32[32,16,512]{2,1,0:T(8,128)} %broadcast_in_dim.10), calls=%async_computation.3 | async-start | bytes 2097152 | tf_op jit(solution)/shard_map/all_to_all | solution.py:352
  106.0 72.8 %copy-start.2 = (bf16[2,256,448]{1,2,0:T(8,128)(2,1)S(1)}, bf16[2,256,448]{1,2,0:T(8,128)(2,1)}, u32[]{:S(2)}) copy-start(bf16[2,256,448]{1,2,0:T(8,128)(2,1)} %param.9) | copy-start | bytes 1376260
  106.0 22.5 %collective-permute-start.5 = (f32[40,128]{1,0:T(8,128)S(1)}, f32[40,128]{1,0:T(8,128)S(1)}, u32[]{:S(2)}, u32[]{:S(2)}) collective-permute-start(f32[40,128]{1,0:T(8,128)S(1)} %reduce_sum.19), channel_id=1, source_target_pairs={{0,12},{1,13},{2,14},{3,15},{4,0},{5,1},{6,2},{7,3},{8,4},{9,5},{1... | collective-permute-start | bytes 61448 | tf_op jit(solution)/shard_map/ppermute | solution.py:348
  117.5 13.4 %collective-permute-start.4 = (f32[40,128]{1,0:T(8,128)S(1)}, f32[40,128]{1,0:T(8,128)S(1)}, u32[]{:S(2)}, u32[]{:S(2)}) collective-permute-start(f32[40,128]{1,0:T(8,128)S(1)} %reduce_sum.19), channel_id=1, source_target_pairs={{0,8},{1,9},{2,10},{3,11},{4,12},{5,13},{6,14},{7,15},{8,0},{9,1},... | collective-permute-start | bytes 61448 | tf_op jit(solution)/shard_map/ppermute | solution.py:348
  122.8 9.9 %collective-permute-start.3 = (f32[40,128]{1,0:T(8,128)S(1)}, f32[40,128]{1,0:T(8,128)S(1)}, u32[]{:S(2)}, u32[]{:S(2)}) collective-permute-start(f32[40,128]{1,0:T(8,128)S(1)} %reduce_sum.19), channel_id=1, source_target_pairs={{0,4},{1,5},{2,6},{3,7},{4,8},{5,9},{6,10},{7,11},{8,12},{9,13},{1... | collective-permute-start | bytes 61448 | tf_op jit(solution)/shard_map/ppermute | solution.py:348
  133.6 35.4 %all-to-all-start.4 = ((f32[32,40,128]{2,1,0:T(8,128)}), f32[32,40,128]{2,1,0:T(8,128)S(1)}, u32[]{:S(2)}, u32[]{:S(2)}) async-start(f32[32,40,128]{2,1,0:T(8,128)} %broadcast_in_dim.11), calls=%async_computation.4 | async-start | bytes 1310720 | tf_op jit(solution)/shard_map/all_to_all | solution.py:352
  141.4 18.2 %collective-permute-start.8 = (f32[40,512]{1,0:T(8,128)S(1)}, f32[40,512]{1,0:T(8,128)S(1)}, u32[]{:S(2)}, u32[]{:S(2)}) collective-permute-start(f32[40,512]{1,0:T(8,128)S(1)} %collective-permute-done.2), channel_id=1, source_target_pairs={{0,12},{1,13},{2,14},{3,15},{4,0},{5,1},{6,2},{7,3},{8,4},{9,5},{1... | collective-permute-start | bytes 245768 | tf_op jit(solution)/shard_map/ppermute | solution.py:348
  144.7 14.9 %collective-permute-start.7 = (f32[40,512]{1,0:T(8,128)S(1)}, f32[40,512]{1,0:T(8,128)S(1)}, u32[]{:S(2)}, u32[]{:S(2)}) collective-permute-start(f32[40,512]{1,0:T(8,128)S(1)} %collective-permute-done.2), channel_id=1, source_target_pairs={{0,8},{1,9},{2,10},{3,11},{4,12},{5,13},{6,14},{7,15},{8,0},{9,1},... | collective-permute-start | bytes 245768 | tf_op jit(solution)/shard_map/ppermute | solution.py:348
  154.0 14.9 %collective-permute-start.6 = (f32[40,512]{1,0:T(8,128)S(1)}, f32[40,512]{1,0:T(8,128)S(1)}, u32[]{:S(2)}, u32[]{:S(2)}) collective-permute-start(f32[40,512]{1,0:T(8,128)S(1)} %collective-permute-done.2), channel_id=1, source_target_pairs={{0,4},{1,5},{2,6},{3,7},{4,8},{5,9},{6,10},{7,11},{8,12},{9,13},{1... | collective-permute-start | bytes 245768 | tf_op jit(solution)/shard_map/ppermute | solution.py:348
  169.0 45.3 %collective-permute-start.11 = (f32[160,512]{1,0:T(8,128)S(1)}, f32[160,512]{1,0:T(8,128)S(1)}, u32[]{:S(2)}, u32[]{:S(2)}) collective-permute-start(f32[160,512]{1,0:T(8,128)S(1)} %constant_dynamic-update-slice_fusion.refs_0_), channel_id=1, source_target_pairs={{0,15},{1,0},{2,1},{3,2},{4,3},{5,4},{6,5},{7,6},{8,7},{9,8},{10,9... | collective-permute-start | bytes 983048 | tf_op jit(solution)/shard_map/ppermute | solution.py:348
  170.9 43.4 %collective-permute-start.10 = (f32[160,512]{1,0:T(8,128)S(1)}, f32[160,512]{1,0:T(8,128)S(1)}, u32[]{:S(2)}, u32[]{:S(2)}) collective-permute-start(f32[160,512]{1,0:T(8,128)S(1)} %constant_dynamic-update-slice_fusion.refs_0_), channel_id=1, source_target_pairs={{0,2},{1,3},{2,4},{3,5},{4,6},{5,7},{6,8},{7,9},{8,10},{9,11},{10,... | collective-permute-start | bytes 983048 | tf_op jit(solution)/shard_map/ppermute | solution.py:348
  176.8 37.4 %collective-permute-start.9 = (f32[160,512]{1,0:T(8,128)S(1)}, f32[160,512]{1,0:T(8,128)S(1)}, u32[]{:S(2)}, u32[]{:S(2)}) collective-permute-start(f32[160,512]{1,0:T(8,128)S(1)} %constant_dynamic-update-slice_fusion.refs_0_), channel_id=1, source_target_pairs={{0,1},{1,2},{2,3},{3,4},{4,5},{5,6},{6,7},{7,8},{8,9},{9,10},{10,1... | collective-permute-start | bytes 983048 | tf_op jit(solution)/shard_map/ppermute | solution.py:348

commit v4 on v3

--- a/solution.py
+++ b/solution.py
@@ -194,13 +194,24 @@
     return index // 2 * (TALL + SHORT) + index % 2 * TALL
 
 
-def key_kernel(place_ref, index_ref, table_ref, keys_ref, slice_ref):
-    here, n = keys_ref.shape
-    col = place_ref[1]
-    picked = lax.broadcasted_iota(jnp.int32, (table_ref.shape[1], n), 0) == index_ref[...]
-    picked = jnp.where(picked, 1.0, 0.0).astype(jnp.bfloat16)
+def front_kernel(place_ref, index_ref, table_hbm, cov_hbm, weight_hbm, other_ref, mine_ref, slice_ref, table_ref, cov_ref, weight_ref, part_ref, value_ref, sems):
+    loads = [
+        pltpu.make_async_copy(src, dst, sems.at[i])
+        for i, (src, dst) in enumerate(((table_hbm, table_ref), (cov_hbm, cov_ref), (weight_hbm, weight_ref)))
+    ]
+    for load in loads:
+        load.start()
+    here, n = table_ref.shape[0], slice_ref.shape[1]
+    chips = mine_ref.shape[0]
+    share = mine_ref.shape[1] - TALL
+    core, col = place_ref[0], place_ref[1]
+    batches, per_batch = index_ref.shape
+    spot = lax.broadcasted_iota(jnp.int32, (table_ref.shape[1], per_batch), 0)
+    picked = jnp.concatenate(
+        [jnp.where(spot == index_ref[b:b + 1, :], 1.0, 0.0).astype(jnp.bfloat16) for b in range(batches)], axis=1
+    )
+    loads[0].wait()
     keys = dot16(table_ref[...], picked).astype(jnp.bfloat16)
-    keys_ref[...] = keys
     padded = slice_ref.shape[0]
     slot = lax.broadcasted_iota(jnp.int32, (padded, here), 0)
     spot = lax.broadcasted_iota(jnp.int32, (padded, here), 1)
@@ -209,32 +220,11 @@
     taken = jnp.logical_and(slot + first == spot, slot < TALL - odd * (TALL - SHORT))
     taken = jnp.where(taken, 1.0, 0.0).astype(jnp.bfloat16)
     slice_ref[...] = dot16(taken, keys).astype(jnp.bfloat16)
-
-
-def select_keys(place, index, table):
-    n = index.shape[1]
-    vmem = pl.BlockSpec(memory_space=pltpu.VMEM)
-    return pl.pallas_call(
-        key_kernel,
-        out_shape=(
-            jax.ShapeDtypeStruct((table.shape[0], n), jnp.bfloat16),
-            jax.ShapeDtypeStruct((PADDED, n), jnp.bfloat16),
-        ),
-        in_specs=[pl.BlockSpec(memory_space=pltpu.SMEM)] + [vmem] * 2,
-        out_specs=(vmem, vmem),
-        compiler_params=pltpu.CompilerParams(vmem_limit_bytes=VMEM_LIMIT),
-    )(place, index, table)
-
-
-def front_kernel(place_ref, keys_ref, cov_ref, weight_ref, mine_ref, other_ref, part_ref, value_ref):
-    here, n = keys_ref.shape
-    chips = mine_ref.shape[0]
-    share = mine_ref.shape[1] - TALL
-    core = place_ref[0]
-    keys = keys_ref[...]
+    loads[2].wait()
+    value_ref[...] = dot16(weight_ref[...], keys)
+    loads[1].wait()
     high, low = split(cov_ref[...])
     part_ref[...] = contract_first(high, keys) + contract_first(low, keys)
-    value_ref[...] = dot16(weight_ref[...], keys)
     for which, ref in ((core, mine_ref), (1 - core, other_ref)):
         lanes = pl.ds(pl.multiple_of(which * (n // 2), LANES), n // 2)
         for j in range(chips):
@@ -251,30 +241,31 @@
                 ref[j, TALL + second:, n // 2:] = jnp.zeros((share - second, n // 2), jnp.float32)
 
 
-def front(place, keys, cov, weight, chips):
-    n = keys.shape[1]
+def front(place, index, table, cov, weight, chips):
+    n = index.size
     width = weight.shape[0]
     share = width // (2 * chips) + 2
     payload = jax.ShapeDtypeStruct((chips, TALL + share, n), jnp.float32)
     vmem = pl.BlockSpec(memory_space=pltpu.VMEM)
     return pl.pallas_call(
         front_kernel,
-        out_shape=(payload, payload),
-        in_specs=[pl.BlockSpec(memory_space=pltpu.SMEM)] + [vmem] * 3,
-        out_specs=(vmem, vmem),
-        scratch_shapes=[pltpu.VMEM((cov.shape[1], n), jnp.float32), pltpu.VMEM((width, n), jnp.float32)],
-        compiler_params=pltpu.CompilerParams(vmem_limit_bytes=VMEM_LIMIT),
-        cost_estimate=pl.CostEstimate(flops=4 * cov.size * n, bytes_accessed=8 * 2**20, transcendentals=0),
-    )(place, keys, cov, weight)
-
-
-def gram_kernel(received_ref, key_ref, panel_ref, value_ref, packed_ref):
-    total = received_ref[0]
-    for j in range(1, received_ref.shape[0]):
-        total = total + received_ref[j]
-    panel = total[:TALL]
-    panel_ref[...] = panel
-    value_ref[...] = total[TALL:]
+        out_shape=(payload, payload, jax.ShapeDtypeStruct((PADDED, n), jnp.bfloat16)),
+        in_specs=[pl.BlockSpec(memory_space=pltpu.SMEM), vmem] + [pl.BlockSpec(memory_space=pl.ANY)] * 3,
+        out_specs=(vmem, vmem, vmem),
+        scratch_shapes=[
+            pltpu.VMEM(table.shape, table.dtype),
+            pltpu.VMEM(cov.shape, cov.dtype),
+            pltpu.VMEM(weight.shape, weight.dtype),
+            pltpu.VMEM((cov.shape[1], n), jnp.float32),
+            pltpu.VMEM((width, n), jnp.float32),
+            pltpu.SemaphoreType.DMA((3,)),
+        ],
+        compiler_params=pltpu.CompilerParams(vmem_limit_bytes=60 * 2**20),
+    )(place, index, table, cov, weight)
+
+
+def gram_kernel(panel_ref, key_ref, packed_ref):
+    panel = panel_ref[...]
     n = panel.shape[1]
     padded = jnp.concatenate([panel, jnp.zeros((PADDED - TALL, n), jnp.float32)], axis=0)
     high = padded.astype(jnp.bfloat16)
@@ -291,21 +282,16 @@
             place += 1
 
 
-def gram_share(received, key_piece):
-    n = received.shape[2]
-    blocks = n // LANES
+def gram_share(panel, key_piece):
+    blocks = panel.shape[1] // LANES
     vmem = pl.BlockSpec(memory_space=pltpu.VMEM)
     return pl.pallas_call(
         gram_kernel,
-        out_shape=(
-            jax.ShapeDtypeStruct((TALL, n), jnp.float32),
-            jax.ShapeDtypeStruct((received.shape[1] - TALL, n), jnp.float32),
-            jax.ShapeDtypeStruct((blocks * (blocks + 1) // 2 * LANES, LANES), jnp.float32),
-        ),
+        out_shape=jax.ShapeDtypeStruct((blocks * (blocks + 1) // 2 * LANES, LANES), jnp.float32),
         in_specs=[vmem] * 2,
-        out_specs=(vmem, vmem, vmem),
+        out_specs=vmem,
         compiler_params=pltpu.CompilerParams(vmem_limit_bytes=VMEM_LIMIT),
-    )(received, key_piece)
+    )(panel, key_piece)
 
 
 def change_kernel(place_ref, *refs):
@@ -367,25 +353,26 @@
     same_core = [[2 * k + h for k in range(chips)] for h in range(2)]
     other_core = [(r, r ^ 1) for r in range(rows)]
 
-    keys, key_slice = select_keys(place, edit_index.reshape(1, n), key_table.T)
-    key_piece = lax.ppermute(key_slice, ("row", "col"), turned)
-    mine, other = front(place, keys, inverse_cov, weight.T, chips)
+    other, mine, key_piece = front(place, edit_index, key_table.T, inverse_cov, weight.T, chips)
     half_sum = mine + lax.ppermute(other, "row", other_core)
-    received = swapped(half_sum, "row", same_core)
-    panel_piece, value_piece, packed = gram_share(received, key_piece)
-    near = lax.ppermute(panel_piece, ("row", "col"), turned)
+    panel_piece = jnp.sum(swapped(half_sum[:, :TALL], "row", same_core), axis=0)
+    own = lax.ppermute(panel_piece, ("row", "col"), turned)
+    value_parts, _ = lax.optimization_barrier((half_sum[:, TALL:], panel_piece))
+    value_piece = jnp.sum(swapped(value_parts, "row", same_core), axis=0)
+    own, value_piece = lax.optimization_barrier((own, value_piece))
+    packed = gram_share(own, key_piece)
+
+    neighbours = [[STRIDE * g + i for i in range(STRIDE)] for g in range(cols // STRIDE)]
     share = packed.shape[0] // rows
-    neighbours = [[STRIDE * g + i for i in range(STRIDE)] for g in range(cols // STRIDE)]
+    far = [own] + [moved(own, "col", STRIDE * t) for t in range(1, cols // STRIDE)]
     part = jnp.sum(swapped(packed.reshape(rows, share, LANES), "row"), axis=0)
-    part, near = lax.optimization_barrier((part, near))
+    part, *far = lax.optimization_barrier((part, *far))
     part = jnp.sum(swapped(copies(part, STRIDE), "col", neighbours), axis=0)
     part, value_piece = lax.optimization_barrier((part, value_piece))
     values = swapped(copies(value_piece, rows), "row")
     part = part + sum(moved(part, "col", STRIDE * t) for t in range(1, cols // STRIDE))
-    part, near, values = lax.optimization_barrier((part, near, values))
-    far = [near] + [moved(near, "col", STRIDE * t) for t in range(1, cols // STRIDE)]
+    part, values, *far = lax.optimization_barrier((part, values, *far))
     gram = swapped(copies(part, rows), "row")
-    gram, *far = lax.optimization_barrier((gram, *far))
     far = jnp.concatenate(far, axis=0)
     bundles = [far] + [moved(far, "col", shift) for shift in SHIFTS[1:]]
     solved = solve(gram.reshape(rows * share, LANES), jnp.swapaxes(targets, 1, 2), values)

time: 218 us -> 217 us (level)
  waiting for transfers between devices: 58.1 us -> 48.2 us
  blocking collectives: 9.05 us -> 13.9 us
  starting transfers between devices: 97.2 us -> 99.5 us
    all_to_all x4 -> x5, starting transfers between devices: 36.6 us -> 45.5 us  [swapped(): lax.all_to_all(value, axis, 0, 0, axis_index_groups=groups, tiled=True)]
    ppermute x9, starting transfers between devices: 50.5 us -> 44.6 us  [moved(): lax.ppermute(value, axis, [(i, (i + shift) % size) for i in range(size)])]
    all_to_all x4 -> x5, waiting for transfers between devices: 41.3 us -> 35.5 us  [swapped(): lax.all_to_all(value, axis, 0, 0, axis_index_groups=groups, tiled=True)]
    all_to_all x1, blocking collectives: 9.05 us -> 13.9 us  [swapped(): lax.all_to_all(value, axis, 0, 0, axis_index_groups=groups, tiled=True)]
    ppermute x9, waiting for transfers between devices: 13.4 us -> 9.13 us  [moved(): lax.ppermute(value, axis, [(i, (i + shift) % size) for i in range(size)])]
    unnamed x10 -> x9, local copies, waits for them, and re-layouts: 3.04 us -> 0.04 us
    pallas_call x3 -> x2, Pallas kernels: 7.34 us -> 8.89 us  [the longest x1 7.45 us: front(): pl.pallas_call(front_kernel, out_shape=(payload, payload, jax.ShapeDtypeS...]
  transfers between devices with their start and end apart: 16 -> 16, of which waited for: 6 -> 7; matrix products, arithmetic and copies ran while one was open for 0% -> 0% of each run, Pallas kernels for 16% -> 16%
where the time goes in v4:
time: 217 us; the launch traced here: 216 us
  starting transfers between devices  99.5 us (46%)
  waiting for transfers between devices  48.2 us (22%)
  Pallas kernels  47.2 us (22%)
  blocking collectives  13.9 us (6%)
  local copies, waits for them, and re-layouts  4.07 us (2%)
  other arithmetic  2.71 us (1%)
    all_to_all x5, starting transfers between devices, swapped(): lax.all_to_all(value, axis, 0, 0, axis_index_groups=groups, tiled=True)  45.5 us
    ppermute x9, starting transfers between devices, moved(): lax.ppermute(value, axis, [(i, (i + shift) % size) for i in range(size)])  44.6 us
    all_to_all x5, waiting for transfers between devices, swapped(): lax.all_to_all(value, axis, 0, 0, axis_index_groups=groups, tiled=True)  35.5 us
    pallas_call x1, Pallas kernels, solve(): pl.pallas_call(solve_kernel, out_shape=(out, out), in_specs=[vmem, pl.Blo...  35.5 us
    all_to_all x1, blocking collectives, swapped(): lax.all_to_all(value, axis, 0, 0, axis_index_groups=groups, tiled=True)  13.9 us
    ppermute x9, waiting for transfers between devices, moved(): lax.ppermute(value, axis, [(i, (i + shift) % size) for i in range(size)])  9.13 us
    ppermute x1, starting transfers between devices, shards(): half_sum = mine + lax.ppermute(other, 'row', other_core)  8.77 us
    pallas_call x1, Pallas kernels, front(): pl.pallas_call(front_kernel, out_shape=(payload, payload, jax.ShapeDtypeS...  7.45 us
  transfers between devices with their start and end apart: 16, of which 7 were waited for; matrix products, arithmetic and copies ran while one was open for 0% of the time, Pallas kernels for 16%

profile of v4, /device:TPU:1, one launch (start us, length us, event | category | flops | bytes accessed | tf_op | source)
XLA Modules:
  0.0 215.9 jit_solution(15612322710203946346)
XLA Ops:
  0.0 0.6 pad_add_fusion.place_ref
  0.6 7.4 %shard_map.55 = (f32[16,56,512]{2,1,0:T(8,128)}, f32[16,56,512]{2,1,0:T(8,128)}, bf16[48,512]{1,0:T(8,128)(2,1)}) custom-call(s32[2]{0:T(128)} %pad_add_fusion.place_ref, s32[2,256]{1,0:T(2,128)} %index_ref.1, bf16[576,1024]{1,0:T(8,128)(2,1)} %bitcast.10, f32[576,1152]{1,0:T(8,128)} %cov_hbm.1, bf16[448,576]{1,0:T(8,128)(2,1)} %bitcast.11), custom_call_target="tpu_custom_call" | custom-call | tf_op jit(solution)/shard_map/pallas_call | solution.py:250
  8.1 8.8 %collective-permute-start = (f32[16,56,512]{2,1,0:T(8,128)}, f32[16,56,512]{2,1,0:T(8,128)S(1)}, u32[]{:S(2)}, u32[]{:S(2)}) collective-permute-start(f32[16,56,512]{2,1,0:T(8,128)} %get-tuple-element.27), channel_id=1, source_target_pairs={{0,16},{16,0},{32,48},{48,32},{64,80},{80,64},{96,112},{112,96},{1... | collective-permute-start | bytes 5505032 | tf_op jit(solution)/shard_map/ppermute | solution.py:357
  16.8 3.6 %collective-permute-done = f32[16,56,512]{2,1,0:T(8,128)S(1)} collective-permute-done((f32[16,56,512]{2,1,0:T(8,128)}, f32[16,56,512]{2,1,0:T(8,128)S(1)}, u32[]{:S(2)}, u32[]{:S(2)}) %collective-permute-start) | collective-permute-done | bytes 1835040 | tf_op jit(solution)/shard_map/ppermute | solution.py:357
  20.4 1.9 add.17
  22.4 1.2 slice.8
  23.5 3.7 %all-to-all-start = ((f32[16,40,512]{2,1,0:T(8,128)}), f32[16,40,512]{2,1,0:T(8,128)S(1)}, u32[]{:S(2)}, u32[]{:S(2)}) async-start(f32[16,40,512]{2,1,0:T(8,128)} %slice.8), calls=%async_computation | async-start | bytes 2621440 | tf_op jit(solution)/shard_map/all_to_all | solution.py:338
  27.2 0.0 copy-start
  27.2 0.8 slice.9
  28.1 20.5 %all-to-all-done = f32[16,40,512]{2,1,0:T(8,128)S(1)} async-done(((f32[16,40,512]{2,1,0:T(8,128)}), f32[16,40,512]{2,1,0:T(8,128)S(1)}, u32[]{:S(2)}, u32[]{:S(2)}) %all-to-all-start) | async-done | bytes 1310752 | tf_op jit(solution)/shard_map/all_to_all | solution.py:338
  48.6 0.1 reduce_sum.36
  48.7 3.6 %all-to-all-start.1 = ((f32[16,16,512]{2,1,0:T(8,128)}), f32[16,16,512]{2,1,0:T(8,128)S(1)}, u32[]{:S(2)}, u32[]{:S(2)}) async-start(f32[16,16,512]{2,1,0:T(8,128)} %slice.9), calls=%async_computation.1 | async-start | bytes 1048576 | tf_op jit(solution)/shard_map/all_to_all | solution.py:338
  52.3 0.7 collective-permute-start.1
  53.0 9.7 %all-to-all-done.1 = f32[16,16,512]{2,1,0:T(8,128)S(1)} async-done(((f32[16,16,512]{2,1,0:T(8,128)}), f32[16,16,512]{2,1,0:T(8,128)S(1)}, u32[]{:S(2)}, u32[]{:S(2)}) %all-to-all-start.1) | async-done | bytes 524320 | tf_op jit(solution)/shard_map/all_to_all | solution.py:338
  62.7 0.0 collective-permute-done.1.panel_ref
  62.7 0.0 copy-done
  62.7 1.4 shard_map.56
  64.2 20.4 %all-to-all-start.2 = ((f32[32,40,128]{2,1,0:T(8,128)}), f32[32,40,128]{2,1,0:T(8,128)S(1)}, u32[]{:S(2)}, u32[]{:S(2)}) async-start(f32[32,40,128]{2,1,0:T(8,128)} %bitcast.4), calls=%async_computation.2 | async-start | bytes 1310720 | tf_op jit(solution)/shard_map/all_to_all | solution.py:338
  84.6 8.8 %collective-permute-start.4 = (f32[40,512]{1,0:T(8,128)S(1)}, f32[40,512]{1,0:T(8,128)S(1)}, u32[]{:S(2)}, u32[]{:S(2)}) collective-permute-start(f32[40,512]{1,0:T(8,128)S(1)} %collective-permute-done.1.panel_ref), channel_id=1, source_target_pairs={{0,12},{1,13},{2,14},{3,15},{4,0},{5,1},{6,2},{7,3},{8,4},{9,5},{1... | collective-permute-start | bytes 245768 | tf_op jit(solution)/shard_map/ppermute | solution.py:334
  93.3 3.4 %collective-permute-start.3 = (f32[40,512]{1,0:T(8,128)S(1)}, f32[40,512]{1,0:T(8,128)S(1)}, u32[]{:S(2)}, u32[]{:S(2)}) collective-permute-start(f32[40,512]{1,0:T(8,128)S(1)} %collective-permute-done.1.panel_ref), channel_id=1, source_target_pairs={{0,8},{1,9},{2,10},{3,11},{4,12},{5,13},{6,14},{7,15},{8,0},{9,1},... | collective-permute-start | bytes 245768 | tf_op jit(solution)/shard_map/ppermute | solution.py:334
  96.8 7.3 %collective-permute-start.2 = (f32[40,512]{1,0:T(8,128)S(1)}, f32[40,512]{1,0:T(8,128)S(1)}, u32[]{:S(2)}, u32[]{:S(2)}) collective-permute-start(f32[40,512]{1,0:T(8,128)S(1)} %collective-permute-done.1.panel_ref), channel_id=1, source_target_pairs={{0,4},{1,5},{2,6},{3,7},{4,8},{5,9},{6,10},{7,11},{8,12},{9,13},{1... | collective-permute-start | bytes 245768 | tf_op jit(solution)/shard_map/ppermute | solution.py:334
  104.1 0.0 all-to-all-done.2
  104.1 0.1 reduce_sum.38
  104.1 0.0 collective-permute-done.4
  104.1 3.6 %collective-permute-done.3 = f32[40,512]{1,0:T(8,128)S(1)} collective-permute-done((f32[40,512]{1,0:T(8,128)S(1)}, f32[40,512]{1,0:T(8,128)S(1)}, u32[]{:S(2)}, u32[]{:S(2)}) %collective-permute-start.3) | collective-permute-done | bytes 81952 | tf_op jit(solution)/shard_map/ppermute | solution.py:334
  107.7 2.5 %collective-permute-done.2 = f32[40,512]{1,0:T(8,128)S(1)} collective-permute-done((f32[40,512]{1,0:T(8,128)S(1)}, f32[40,512]{1,0:T(8,128)S(1)}, u32[]{:S(2)}, u32[]{:S(2)}) %collective-permute-start.2) | collective-permute-done | bytes 81952 | tf_op jit(solution)/shard_map/ppermute | solution.py:334
  110.3 13.9 %all_to_all.30 = f32[4,40,128]{2,1,0:T(8,128)S(1)} all-to-all(f32[4,40,128]{2,1,0:T(8,128)S(1)} %broadcast_in_dim.9), channel_id=1, replica_groups={{0,1,2,3},{4,5,6,7},{8,9,10,11},{12,13,14,15},{16,17,18,19},{20,21,22,2..., dimensions={0} | all-to-all | bytes 163840 | tf_op jit(solution)/shard_map/all_to_all | solution.py:338
  124.1 1.1 broadcast_in_dim.10
  125.3 8.9 %all-to-all-start.4 = ((f32[32,16,512]{2,1,0:T(8,128)}), f32[32,16,512]{2,1,0:T(8,128)S(1)}, u32[]{:S(2)}, u32[]{:S(2)}) async-start(f32[32,16,512]{2,1,0:T(8,128)} %broadcast_in_dim.10), calls=%async_computation.4 | async-start | bytes 2097152 | tf_op jit(solution)/shard_map/all_to_all | solution.py:338
  134.2 0.0 copy-start.2
  134.2 6.9 %collective-permute-start.7 = (f32[40,128]{1,0:T(8,128)S(1)}, f32[40,128]{1,0:T(8,128)S(1)}, u32[]{:S(2)}, u32[]{:S(2)}) collective-permute-start(f32[40,128]{1,0:T(8,128)S(1)} %reduce_sum.39), channel_id=1, source_target_pairs={{0,12},{1,13},{2,14},{3,15},{4,0},{5,1},{6,2},{7,3},{8,4},{9,5},{1... | collective-permute-start | bytes 61448 | tf_op jit(solution)/shard_map/ppermute | solution.py:334
  141.1 3.7 %collective-permute-start.6 = (f32[40,128]{1,0:T(8,128)S(1)}, f32[40,128]{1,0:T(8,128)S(1)}, u32[]{:S(2)}, u32[]{:S(2)}) collective-permute-start(f32[40,128]{1,0:T(8,128)S(1)} %reduce_sum.39), channel_id=1, source_target_pairs={{0,8},{1,9},{2,10},{3,11},{4,12},{5,13},{6,14},{7,15},{8,0},{9,1},... | collective-permute-start | bytes 61448 | tf_op jit(solution)/shard_map/ppermute | solution.py:334
  144.8 7.0 %collective-permute-start.5 = (f32[40,128]{1,0:T(8,128)S(1)}, f32[40,128]{1,0:T(8,128)S(1)}, u32[]{:S(2)}, u32[]{:S(2)}) collective-permute-start(f32[40,128]{1,0:T(8,128)S(1)} %reduce_sum.39), channel_id=1, source_target_pairs={{0,4},{1,5},{2,6},{3,7},{4,8},{5,9},{6,10},{7,11},{8,12},{9,13},{1... | collective-permute-start | bytes 61448 | tf_op jit(solution)/shard_map/ppermute | solution.py:334
  151.8 0.0 collective-permute-done.7
  151.8 3.0 %collective-permute-done.6 = f32[40,128]{1,0:T(8,128)S(1)} collective-permute-done((f32[40,128]{1,0:T(8,128)S(1)}, f32[40,128]{1,0:T(8,128)S(1)}, u32[]{:S(2)}, u32[]{:S(2)}) %collective-permute-start.6) | collective-permute-done | bytes 20512 | tf_op jit(solution)/shard_map/ppermute | solution.py:334
  154.8 0.0 collective-permute-done.5
  154.8 0.0 all-to-all-done.4.value_hbm
  154.8 0.9 broadcast_in_dim.11
  155.7 8.8 %all-to-all-start.5 = ((f32[32,40,128]{2,1,0:T(8,128)}), f32[32,40,128]{2,1,0:T(8,128)S(1)}, u32[]{:S(2)}, u32[]{:S(2)}) async-start(f32[32,40,128]{2,1,0:T(8,128)} %broadcast_in_dim.11), calls=%async_computation.5 | async-start | bytes 1310720 | tf_op jit(solution)/shard_map/all_to_all | solution.py:338
  164.6 3.3 %collective-permute-start.10 = (f32[160,512]{1,0:T(8,128)S(1)}, f32[160,512]{1,0:T(8,128)S(1)}, u32[]{:S(2)}, u32[]{:S(2)}) collective-permute-start(f32[160,512]{1,0:T(8,128)S(1)} %constant_dynamic-update-slice_fusion.refs_0_), channel_id=1, source_target_pairs={{0,15},{1,0},{2,1},{3,2},{4,3},{5,4},{6,5},{7,6},{8,7},{9,8},{10,9... | collective-permute-start | bytes 983048 | tf_op jit(solution)/shard_map/ppermute | solution.py:334
  167.9 2.4 %collective-permute-start.9 = (f32[160,512]{1,0:T(8,128)S(1)}, f32[160,512]{1,0:T(8,128)S(1)}, u32[]{:S(2)}, u32[]{:S(2)}) collective-permute-start(f32[160,512]{1,0:T(8,128)S(1)} %constant_dynamic-update-slice_fusion.refs_0_), channel_id=1, source_target_pairs={{0,2},{1,3},{2,4},{3,5},{4,6},{5,7},{6,8},{7,9},{8,10},{9,11},{10,... | collective-permute-start | bytes 983048 | tf_op jit(solution)/shard_map/ppermute | solution.py:334
  170.3 1.9 collective-permute-start.8
  172.2 5.3 %all-to-all-done.5 = f32[32,40,128]{2,1,0:T(8,128)S(1)} async-done(((f32[32,40,128]{2,1,0:T(8,128)}), f32[32,40,128]{2,1,0:T(8,128)S(1)}, u32[]{:S(2)}, u32[]{:S(2)}) %all-to-all-start.5) | async-done | bytes 655392 | tf_op jit(solution)/shard_map/all_to_all | solution.py:338
  177.5 35.5 %shard_map.57 = (bf16[448,512]{1,0:T(8,128)(2,1)S(1)}, bf16[448,512]{1,0:T(8,128)(2,1)S(1)}) custom-call(f32[1280,128]{1,0:T(8,128)S(1)} %bitcast.8, bf16[2,448,256]{2,1,0:T(8,128)(2,1)S(1)} %bitcast.9, f32[32,16,512]{2,1,0:T(8,128)S(1)} %all-to-all-done.4.value_hbm), custom_call_target="tpu_custom_call" | custom-call | flops 5368709120 | bytes 4194304 | tf_op jit(solution)/shard_map/pallas_call | solution.py:168
  212.9 0.0 collective-permute-done.10.refs_3_
  213.0 0.0 collective-permute-done.9.refs_2_
  213.0 0.0 collective-permute-done.8.refs_1_
  213.0 2.9 %shard_map.58 = bf16[448,576]{1,0:T(8,128)(2,1)} custom-call(s32[2]{0:T(128)S(1)} %copy-done.1, f32[160,512]{1,0:T(8,128)S(1)} %constant_dynamic-update-slice_fusion.refs_0_, f32[160,512]{1,0:T(8,128)S(1)} %collective-permute-done.8.refs_1_, f32[160,512]{1,0:T(8,128)S(1)} %collective-permute-done.9.refs_2_, f32[160,512]{1,0:T(8,128)S(1)} %collective-permute-done.10.refs_3_, ...), custom_call_target="tpu_custom_call" | custom-call | tf_op jit(solution)/shard_map/pallas_call | solution.py:322
  (11 shorter events, 0.1 us)
Async XLA Ops:
  8.1 12.4 %collective-permute-start = (f32[16,56,512]{2,1,0:T(8,128)}, f32[16,56,512]{2,1,0:T(8,128)S(1)}, u32[]{:S(2)}, u32[]{:S(2)}) collective-permute-start(f32[16,56,512]{2,1,0:T(8,128)} %get-tuple-element.27), channel_id=1, source_target_pairs={{0,16},{16,0},{32,48},{48,32},{64,80},{80,64},{96,112},{112,96},{1... | collective-permute-start | bytes 5505032 | tf_op jit(solution)/shard_map/ppermute | solution.py:357
  23.5 25.1 %all-to-all-start = ((f32[16,40,512]{2,1,0:T(8,128)}), f32[16,40,512]{2,1,0:T(8,128)S(1)}, u32[]{:S(2)}, u32[]{:S(2)}) async-start(f32[16,40,512]{2,1,0:T(8,128)} %slice.8), calls=%async_computation | async-start | bytes 2621440 | tf_op jit(solution)/shard_map/all_to_all | solution.py:338
  27.2 35.5 %copy-start = (bf16[48,512]{1,0:T(8,128)(2,1)S(1)}, bf16[48,512]{1,0:T(8,128)(2,1)}, u32[]{:S(2)}) copy-start(bf16[48,512]{1,0:T(8,128)(2,1)} %get-tuple-element.30.key_ref) | copy-start | bytes 147460
  48.7 14.0 %all-to-all-start.1 = ((f32[16,16,512]{2,1,0:T(8,128)}), f32[16,16,512]{2,1,0:T(8,128)S(1)}, u32[]{:S(2)}, u32[]{:S(2)}) async-start(f32[16,16,512]{2,1,0:T(8,128)} %slice.9), calls=%async_computation.1 | async-start | bytes 1048576 | tf_op jit(solution)/shard_map/all_to_all | solution.py:338
  52.3 10.4 %collective-permute-start.1 = (f32[40,512]{1,0:T(8,128)S(1)}, f32[40,512]{1,0:T(8,128)S(1)}, u32[]{:S(2)}, u32[]{:S(2)}) collective-permute-start(f32[40,512]{1,0:T(8,128)S(1)} %reduce_sum.36), channel_id=1, source_target_pairs={{0,0},{16,16},{1,32},{17,48},{2,64},{18,80},{3,96},{19,112},{4,128... | collective-permute-start | bytes 245768 | tf_op jit(solution)/shard_map/ppermute | solution.py:359
  64.2 39.9 %all-to-all-start.2 = ((f32[32,40,128]{2,1,0:T(8,128)}), f32[32,40,128]{2,1,0:T(8,128)S(1)}, u32[]{:S(2)}, u32[]{:S(2)}) async-start(f32[32,40,128]{2,1,0:T(8,128)} %bitcast.4), calls=%async_computation.2 | async-start | bytes 1310720 | tf_op jit(solution)/shard_map/all_to_all | solution.py:338
  84.6 19.6 %collective-permute-start.4 = (f32[40,512]{1,0:T(8,128)S(1)}, f32[40,512]{1,0:T(8,128)S(1)}, u32[]{:S(2)}, u32[]{:S(2)}) collective-permute-start(f32[40,512]{1,0:T(8,128)S(1)} %collective-permute-done.1.panel_ref), channel_id=1, source_target_pairs={{0,12},{1,13},{2,14},{3,15},{4,0},{5,1},{6,2},{7,3},{8,4},{9,5},{1... | collective-permute-start | bytes 245768 | tf_op jit(solution)/shard_map/ppermute | solution.py:334
  93.3 14.4 %collective-permute-start.3 = (f32[40,512]{1,0:T(8,128)S(1)}, f32[40,512]{1,0:T(8,128)S(1)}, u32[]{:S(2)}, u32[]{:S(2)}) collective-permute-start(f32[40,512]{1,0:T(8,128)S(1)} %collective-permute-done.1.panel_ref), channel_id=1, source_target_pairs={{0,8},{1,9},{2,10},{3,11},{4,12},{5,13},{6,14},{7,15},{8,0},{9,1},... | collective-permute-start | bytes 245768 | tf_op jit(solution)/shard_map/ppermute | solution.py:334
  96.8 13.5 %collective-permute-start.2 = (f32[40,512]{1,0:T(8,128)S(1)}, f32[40,512]{1,0:T(8,128)S(1)}, u32[]{:S(2)}, u32[]{:S(2)}) collective-permute-start(f32[40,512]{1,0:T(8,128)S(1)} %collective-permute-done.1.panel_ref), channel_id=1, source_target_pairs={{0,4},{1,5},{2,6},{3,7},{4,8},{5,9},{6,10},{7,11},{8,12},{9,13},{1... | collective-permute-start | bytes 245768 | tf_op jit(solution)/shard_map/ppermute | solution.py:334
  125.3 29.6 %all-to-all-start.4 = ((f32[32,16,512]{2,1,0:T(8,128)}), f32[32,16,512]{2,1,0:T(8,128)S(1)}, u32[]{:S(2)}, u32[]{:S(2)}) async-start(f32[32,16,512]{2,1,0:T(8,128)} %broadcast_in_dim.10), calls=%async_computation.4 | async-start | bytes 2097152 | tf_op jit(solution)/shard_map/all_to_all | solution.py:338
  134.2 43.3 %copy-start.2 = (bf16[2,256,448]{1,2,0:T(8,128)(2,1)S(1)}, bf16[2,256,448]{1,2,0:T(8,128)(2,1)}, u32[]{:S(2)}) copy-start(bf16[2,256,448]{1,2,0:T(8,128)(2,1)} %param.9) | copy-start | bytes 1376260
  134.2 17.6 %collective-permute-start.7 = (f32[40,128]{1,0:T(8,128)S(1)}, f32[40,128]{1,0:T(8,128)S(1)}, u32[]{:S(2)}, u32[]{:S(2)}) collective-permute-start(f32[40,128]{1,0:T(8,128)S(1)} %reduce_sum.39), channel_id=1, source_target_pairs={{0,12},{1,13},{2,14},{3,15},{4,0},{5,1},{6,2},{7,3},{8,4},{9,5},{1... | collective-permute-start | bytes 61448 | tf_op jit(solution)/shard_map/ppermute | solution.py:334
  141.1 13.7 %collective-permute-start.6 = (f32[40,128]{1,0:T(8,128)S(1)}, f32[40,128]{1,0:T(8,128)S(1)}, u32[]{:S(2)}, u32[]{:S(2)}) collective-permute-start(f32[40,128]{1,0:T(8,128)S(1)} %reduce_sum.39), channel_id=1, source_target_pairs={{0,8},{1,9},{2,10},{3,11},{4,12},{5,13},{6,14},{7,15},{8,0},{9,1},... | collective-permute-start | bytes 61448 | tf_op jit(solution)/shard_map/ppermute | solution.py:334
  144.8 10.0 %collective-permute-start.5 = (f32[40,128]{1,0:T(8,128)S(1)}, f32[40,128]{1,0:T(8,128)S(1)}, u32[]{:S(2)}, u32[]{:S(2)}) collective-permute-start(f32[40,128]{1,0:T(8,128)S(1)} %reduce_sum.39), channel_id=1, source_target_pairs={{0,4},{1,5},{2,6},{3,7},{4,8},{5,9},{6,10},{7,11},{8,12},{9,13},{1... | collective-permute-start | bytes 61448 | tf_op jit(solution)/shard_map/ppermute | solution.py:334
  155.7 21.8 %all-to-all-start.5 = ((f32[32,40,128]{2,1,0:T(8,128)}), f32[32,40,128]{2,1,0:T(8,128)S(1)}, u32[]{:S(2)}, u32[]{:S(2)}) async-start(f32[32,40,128]{2,1,0:T(8,128)} %broadcast_in_dim.11), calls=%async_computation.5 | async-start | bytes 1310720 | tf_op jit(solution)/shard_map/all_to_all | solution.py:338
  164.6 48.3 %collective-permute-start.10 = (f32[160,512]{1,0:T(8,128)S(1)}, f32[160,512]{1,0:T(8,128)S(1)}, u32[]{:S(2)}, u32[]{:S(2)}) collective-permute-start(f32[160,512]{1,0:T(8,128)S(1)} %constant_dynamic-update-slice_fusion.refs_0_), channel_id=1, source_target_pairs={{0,15},{1,0},{2,1},{3,2},{4,3},{5,4},{6,5},{7,6},{8,7},{9,8},{10,9... | collective-permute-start | bytes 983048 | tf_op jit(solution)/shard_map/ppermute | solution.py:334
  167.9 45.1 %collective-permute-start.9 = (f32[160,512]{1,0:T(8,128)S(1)}, f32[160,512]{1,0:T(8,128)S(1)}, u32[]{:S(2)}, u32[]{:S(2)}) collective-permute-start(f32[160,512]{1,0:T(8,128)S(1)} %constant_dynamic-update-slice_fusion.refs_0_), channel_id=1, source_target_pairs={{0,2},{1,3},{2,4},{3,5},{4,6},{5,7},{6,8},{7,9},{8,10},{9,11},{10,... | collective-permute-start | bytes 983048 | tf_op jit(solution)/shard_map/ppermute | solution.py:334
  170.3 42.7 %collective-permute-start.8 = (f32[160,512]{1,0:T(8,128)S(1)}, f32[160,512]{1,0:T(8,128)S(1)}, u32[]{:S(2)}, u32[]{:S(2)}) collective-permute-start(f32[160,512]{1,0:T(8,128)S(1)} %constant_dynamic-update-slice_fusion.refs_0_), channel_id=1, source_target_pairs={{0,1},{1,2},{2,3},{3,4},{4,5},{5,6},{6,7},{7,8},{8,9},{9,10},{10,1... | collective-permute-start | bytes 983048 | tf_op jit(solution)/shard_map/ppermute | solution.py:334
  177.5 35.5 %copy-start.1 = (s32[2]{0:T(128)S(1)}, s32[2]{0:T(128)}, u32[]{:S(2)}) copy-start(s32[2]{0:T(128)} %pad_add_fusion.place_ref) | copy-start | bytes 28

commit v5 on v4

--- a/solution.py
+++ b/solution.py
@@ -264,8 +264,13 @@
     )(place, index, table, cov, weight)
 
 
-def gram_kernel(panel_ref, key_ref, packed_ref):
-    panel = panel_ref[...]
+def gram_kernel(received_ref, key_ref, panel_ref, value_ref, packed_ref):
+    total = received_ref[0]
+    for j in range(1, received_ref.shape[0]):
+        total = total + received_ref[j]
+    panel = total[:TALL]
+    panel_ref[...] = panel
+    value_ref[...] = total[TALL:]
     n = panel.shape[1]
     padded = jnp.concatenate([panel, jnp.zeros((PADDED - TALL, n), jnp.float32)], axis=0)
     high = padded.astype(jnp.bfloat16)
@@ -282,16 +287,21 @@
             place += 1
 
 
-def gram_share(panel, key_piece):
-    blocks = panel.shape[1] // LANES
+def gram_share(received, key_piece):
+    n = received.shape[2]
+    blocks = n // LANES
     vmem = pl.BlockSpec(memory_space=pltpu.VMEM)
     return pl.pallas_call(
         gram_kernel,
-        out_shape=jax.ShapeDtypeStruct((blocks * (blocks + 1) // 2 * LANES, LANES), jnp.float32),
+        out_shape=(
+            jax.ShapeDtypeStruct((TALL, n), jnp.float32),
+            jax.ShapeDtypeStruct((received.shape[1] - TALL, n), jnp.float32),
+            jax.ShapeDtypeStruct((blocks * (blocks + 1) // 2 * LANES, LANES), jnp.float32),
+        ),
         in_specs=[vmem] * 2,
-        out_specs=vmem,
+        out_specs=(vmem, vmem, vmem),
         compiler_params=pltpu.CompilerParams(vmem_limit_bytes=VMEM_LIMIT),
-    )(panel, key_piece)
+    )(received, key_piece)
 
 
 def change_kernel(place_ref, *refs):
@@ -353,25 +363,23 @@
     same_core = [[2 * k + h for k in range(chips)] for h in range(2)]
     other_core = [(r, r ^ 1) for r in range(rows)]
 
-    other, mine, key_piece = front(place, edit_index, key_table.T, inverse_cov, weight.T, chips)
+    other, mine, key_slice = front(place, edit_index, key_table.T, inverse_cov, weight.T, chips)
     half_sum = mine + lax.ppermute(other, "row", other_core)
-    panel_piece = jnp.sum(swapped(half_sum[:, :TALL], "row", same_core), axis=0)
+    key_piece = lax.ppermute(key_slice, ("row", "col"), turned)
+    panel_piece, value_piece, packed = gram_share(swapped(half_sum, "row", same_core), key_piece)
+
     own = lax.ppermute(panel_piece, ("row", "col"), turned)
-    value_parts, _ = lax.optimization_barrier((half_sum[:, TALL:], panel_piece))
-    value_piece = jnp.sum(swapped(value_parts, "row", same_core), axis=0)
-    own, value_piece = lax.optimization_barrier((own, value_piece))
-    packed = gram_share(own, key_piece)
-
+    share = packed.shape[0] // rows
+    part = jnp.sum(swapped(packed.reshape(rows, share, LANES), "row"), axis=0)
     neighbours = [[STRIDE * g + i for i in range(STRIDE)] for g in range(cols // STRIDE)]
-    share = packed.shape[0] // rows
-    far = [own] + [moved(own, "col", STRIDE * t) for t in range(1, cols // STRIDE)]
-    part = jnp.sum(swapped(packed.reshape(rows, share, LANES), "row"), axis=0)
-    part, *far = lax.optimization_barrier((part, *far))
+    joined = jnp.concatenate([own, part.reshape(-1, n)], axis=0)
+    joined, value_piece = lax.optimization_barrier((joined, value_piece))
+    values = swapped(copies(value_piece, rows), "row")
+    joined = [joined] + [moved(joined, "col", STRIDE * t) for t in range(1, cols // STRIDE)]
+    values, *joined = lax.optimization_barrier((values, *joined))
+    far = [item[:TALL] for item in joined]
+    part = sum(item[TALL:] for item in joined).reshape(share, LANES)
     part = jnp.sum(swapped(copies(part, STRIDE), "col", neighbours), axis=0)
-    part, value_piece = lax.optimization_barrier((part, value_piece))
-    values = swapped(copies(value_piece, rows), "row")
-    part = part + sum(moved(part, "col", STRIDE * t) for t in range(1, cols // STRIDE))
-    part, values, *far = lax.optimization_barrier((part, values, *far))
     gram = swapped(copies(part, rows), "row")
     far = jnp.concatenate(far, axis=0)
     bundles = [far] + [moved(far, "col", shift) for shift in SHIFTS[1:]]

time: 217 us -> 205 us (0.945)
  starting transfers between devices: 99.5 us -> 79.9 us
  waiting for transfers between devices: 48.2 us -> 54.8 us
  blocking collectives: 13.9 us -> 16.5 us
    ppermute x9 -> x6, starting transfers between devices: 44.6 us -> 31.5 us  [moved(): lax.ppermute(value, axis, [(i, (i + shift) % size) for i in range(size)])]
    all_to_all x5 -> x4, waiting for transfers between devices: 35.5 us -> 45 us  [swapped(): lax.all_to_all(value, axis, 0, 0, axis_index_groups=groups, tiled=True)]
    all_to_all x5 -> x4, starting transfers between devices: 45.5 us -> 38.3 us  [swapped(): lax.all_to_all(value, axis, 0, 0, axis_index_groups=groups, tiled=True)]
    ppermute x9 -> x6, waiting for transfers between devices: 9.13 us -> 6.21 us  [moved(): lax.ppermute(value, axis, [(i, (i + shift) % size) for i in range(size)])]
    all_to_all x1, blocking collectives: 13.9 us -> 16.5 us  [swapped(): lax.all_to_all(value, axis, 0, 0, axis_index_groups=groups, tiled=True)]
  transfers between devices with their start and end apart: 16 -> 13, of which waited for: 7 -> 6; matrix products, arithmetic and copies ran while one was open for 0% -> 0% of each run, Pallas kernels for 16% -> 17%
where the time goes in v5:
time: 205 us
  starting transfers between devices  79.9 us (39%)
  waiting for transfers between devices  54.8 us (27%)
  Pallas kernels  47.2 us (23%)
  blocking collectives  16.5 us (8%)
  other arithmetic  3.85 us (2%)
  local copies, waits for them, and re-layouts  2.06 us (1%)
    all_to_all x4, waiting for transfers between devices, swapped(): lax.all_to_all(value, axis, 0, 0, axis_index_groups=groups, tiled=True)  45 us
    all_to_all x4, starting transfers between devices, swapped(): lax.all_to_all(value, axis, 0, 0, axis_index_groups=groups, tiled=True)  38.3 us
    pallas_call x1, Pallas kernels, solve(): pl.pallas_call(solve_kernel, out_shape=(out, out), in_specs=[vmem, pl.Blo...  35.4 us
    ppermute x6, starting transfers between devices, moved(): lax.ppermute(value, axis, [(i, (i + shift) % size) for i in range(size)])  31.5 us
    all_to_all x1, blocking collectives, swapped(): lax.all_to_all(value, axis, 0, 0, axis_index_groups=groups, tiled=True)  16.5 us
    ppermute x1, starting transfers between devices, shards(): half_sum = mine + lax.ppermute(other, 'row', other_core)  8.77 us
    pallas_call x1, Pallas kernels, front(): pl.pallas_call(front_kernel, out_shape=(payload, payload, jax.ShapeDtypeS...  7.46 us
    ppermute x6, waiting for transfers between devices, moved(): lax.ppermute(value, axis, [(i, (i + shift) % size) for i in range(size)])  6.21 us
  transfers between devices with their start and end apart: 13, of which 6 were waited for; matrix products, arithmetic and copies ran while one was open for 0% of the time, Pallas kernels for 17%

profile of v5, /device:TPU:1, one launch (start us, length us, event | category | flops | bytes accessed | tf_op | source)
XLA Modules:
  0.0 204.6 jit_solution(7724990446942994296)
XLA Ops:
  0.0 0.6 pad_add_fusion.place_ref
  0.6 7.5 %shard_map.55 = (f32[16,56,512]{2,1,0:T(8,128)}, f32[16,56,512]{2,1,0:T(8,128)}, bf16[48,512]{1,0:T(8,128)(2,1)}) custom-call(s32[2]{0:T(128)} %pad_add_fusion.place_ref, s32[2,256]{1,0:T(2,128)} %index_ref.1, bf16[576,1024]{1,0:T(8,128)(2,1)} %bitcast.10, f32[576,1152]{1,0:T(8,128)} %cov_hbm.1, bf16[448,576]{1,0:T(8,128)(2,1)} %bitcast.11), custom_call_target="tpu_custom_call" | custom-call | tf_op jit(solution)/shard_map/pallas_call | solution.py:250
  8.1 8.8 %collective-permute-start = (f32[16,56,512]{2,1,0:T(8,128)}, f32[16,56,512]{2,1,0:T(8,128)S(1)}, u32[]{:S(2)}, u32[]{:S(2)}) collective-permute-start(f32[16,56,512]{2,1,0:T(8,128)} %get-tuple-element.21), channel_id=1, source_target_pairs={{0,16},{16,0},{32,48},{48,32},{64,80},{80,64},{96,112},{112,96},{1... | collective-permute-start | bytes 5505032 | tf_op jit(solution)/shard_map/ppermute | solution.py:367
  16.9 3.6 %collective-permute-done = f32[16,56,512]{2,1,0:T(8,128)S(1)} collective-permute-done((f32[16,56,512]{2,1,0:T(8,128)}, f32[16,56,512]{2,1,0:T(8,128)S(1)}, u32[]{:S(2)}, u32[]{:S(2)}) %collective-permute-start) | collective-permute-done | bytes 1835040 | tf_op jit(solution)/shard_map/ppermute | solution.py:367
  20.5 3.1 %add.17 = f32[16,56,512]{2,1,0:T(8,128)} add(f32[16,56,512]{2,1,0:T(8,128)} %get-tuple-element.20, f32[16,56,512]{2,1,0:T(8,128)S(1)} %collective-permute-done) | non-fusion elementwise | flops 458752 | bytes 5505024 | tf_op jit(solution)/shard_map/add | solution.py:367
  23.6 0.0 copy-start.2
  23.6 3.8 %all-to-all-start = ((f32[16,56,512]{2,1,0:T(8,128)}), f32[16,56,512]{2,1,0:T(8,128)S(1)}, u32[]{:S(2)}, u32[]{:S(2)}) async-start(f32[16,56,512]{2,1,0:T(8,128)} %add.17), calls=%async_computation | async-start | bytes 3670016 | tf_op jit(solution)/shard_map/all_to_all | solution.py:348
  27.4 0.0 copy-done.2
  27.5 0.7 collective-permute-start.1
  28.1 0.0 collective-permute-done.1.key_ref
  28.1 29.0 %all-to-all-done.received_ref = f32[16,56,512]{2,1,0:T(8,128)S(1)} async-done(((f32[16,56,512]{2,1,0:T(8,128)}), f32[16,56,512]{2,1,0:T(8,128)S(1)}, u32[]{:S(2)}, u32[]{:S(2)}) %all-to-all-start) | async-done | bytes 1835040 | tf_op jit(solution)/shard_map/all_to_all | solution.py:348
  57.2 1.5 shard_map.56
  58.6 6.2 %all-to-all-start.1 = ((f32[32,40,128]{2,1,0:T(8,128)}), f32[32,40,128]{2,1,0:T(8,128)S(1)}, u32[]{:S(2)}, u32[]{:S(2)}) async-start(f32[32,40,128]{2,1,0:T(8,128)} %bitcast.4), calls=%async_computation.1 | async-start | bytes 1310720 | tf_op jit(solution)/shard_map/all_to_all | solution.py:348
  64.8 0.7 collective-permute-start.2
  65.5 12.2 %all-to-all-done.1 = f32[32,40,128]{2,1,0:T(8,128)S(1)} async-done(((f32[32,40,128]{2,1,0:T(8,128)}), f32[32,40,128]{2,1,0:T(8,128)S(1)}, u32[]{:S(2)}, u32[]{:S(2)}) %all-to-all-start.1) | async-done | bytes 655392 | tf_op jit(solution)/shard_map/all_to_all | solution.py:348
  77.8 0.1 reduce_sum.18
  77.8 0.0 collective-permute-done.2
  77.8 1.1 broadcast_in_dim.9
  79.0 19.7 %all-to-all-start.2 = ((f32[32,16,512]{2,1,0:T(8,128)}), f32[32,16,512]{2,1,0:T(8,128)S(1)}, u32[]{:S(2)}, u32[]{:S(2)}) async-start(f32[32,16,512]{2,1,0:T(8,128)} %broadcast_in_dim.9), calls=%async_computation.2 | async-start | bytes 2097152 | tf_op jit(solution)/shard_map/all_to_all | solution.py:348
  98.7 8.5 %collective-permute-start.5 = (f32[50,512]{1,0:T(8,128)S(1)}, f32[50,512]{1,0:T(8,128)S(1)}, u32[]{:S(2)}, u32[]{:S(2)}) collective-permute-start(f32[50,512]{1,0:T(8,128)S(1)} %pad_maximum_fusion.1), channel_id=1, source_target_pairs={{0,12},{1,13},{2,14},{3,15},{4,0},{5,1},{6,2},{7,3},{8,4},{9,5},{1... | collective-permute-start | bytes 307208 | tf_op jit(solution)/shard_map/ppermute | solution.py:344
  107.2 6.7 %collective-permute-start.4 = (f32[50,512]{1,0:T(8,128)S(1)}, f32[50,512]{1,0:T(8,128)S(1)}, u32[]{:S(2)}, u32[]{:S(2)}) collective-permute-start(f32[50,512]{1,0:T(8,128)S(1)} %pad_maximum_fusion.1), channel_id=1, source_target_pairs={{0,8},{1,9},{2,10},{3,11},{4,12},{5,13},{6,14},{7,15},{8,0},{9,1},... | collective-permute-start | bytes 307208 | tf_op jit(solution)/shard_map/ppermute | solution.py:344
  113.8 7.3 %collective-permute-start.3 = (f32[50,512]{1,0:T(8,128)S(1)}, f32[50,512]{1,0:T(8,128)S(1)}, u32[]{:S(2)}, u32[]{:S(2)}) collective-permute-start(f32[50,512]{1,0:T(8,128)S(1)} %pad_maximum_fusion.1), channel_id=1, source_target_pairs={{0,4},{1,5},{2,6},{3,7},{4,8},{5,9},{6,10},{7,11},{8,12},{9,13},{1... | collective-permute-start | bytes 307208 | tf_op jit(solution)/shard_map/ppermute | solution.py:344
  121.1 0.0 collective-permute-done.5
  121.1 0.8 collective-permute-done.4
  122.0 5.4 %collective-permute-done.3 = f32[50,512]{1,0:T(8,128)S(1)} collective-permute-done((f32[50,512]{1,0:T(8,128)S(1)}, f32[50,512]{1,0:T(8,128)S(1)}, u32[]{:S(2)}, u32[]{:S(2)}) %collective-permute-start.3) | collective-permute-done | bytes 102432 | tf_op jit(solution)/shard_map/ppermute | solution.py:344
  127.3 0.0 all-to-all-done.2.value_hbm
  127.3 0.0 copy-start.1
  127.4 16.5 %all_to_all.25 = f32[4,40,128]{2,1,0:T(8,128)S(1)} all-to-all(f32[4,40,128]{2,1,0:T(8,128)S(1)} %broadcast_in_dim.10), channel_id=1, replica_groups={{0,1,2,3},{4,5,6,7},{8,9,10,11},{12,13,14,15},{16,17,18,19},{20,21,22,2..., dimensions={0} | all-to-all | bytes 163840 | tf_op jit(solution)/shard_map/all_to_all | solution.py:348
  143.9 0.9 broadcast_in_dim.11
  144.8 8.6 %all-to-all-start.4 = ((f32[32,40,128]{2,1,0:T(8,128)}), f32[32,40,128]{2,1,0:T(8,128)S(1)}, u32[]{:S(2)}, u32[]{:S(2)}) async-start(f32[32,40,128]{2,1,0:T(8,128)} %broadcast_in_dim.11), calls=%async_computation.4 | async-start | bytes 1310720 | tf_op jit(solution)/shard_map/all_to_all | solution.py:348
  153.4 5.2 %collective-permute-start.8 = (f32[160,512]{1,0:T(8,128)S(1)}, f32[160,512]{1,0:T(8,128)S(1)}, u32[]{:S(2)}, u32[]{:S(2)}) collective-permute-start(f32[160,512]{1,0:T(8,128)S(1)} %pad_maximum_fusion.refs_0_), channel_id=1, source_target_pairs={{0,15},{1,0},{2,1},{3,2},{4,3},{5,4},{6,5},{7,6},{8,7},{9,8},{10,9... | collective-permute-start | bytes 983048 | tf_op jit(solution)/shard_map/ppermute | solution.py:344
  158.7 1.9 collective-permute-start.7
  160.6 1.9 collective-permute-start.6
  162.5 3.7 %all-to-all-done.4 = f32[32,40,128]{2,1,0:T(8,128)S(1)} async-done(((f32[32,40,128]{2,1,0:T(8,128)}), f32[32,40,128]{2,1,0:T(8,128)S(1)}, u32[]{:S(2)}, u32[]{:S(2)}) %all-to-all-start.4) | async-done | bytes 655392 | tf_op jit(solution)/shard_map/all_to_all | solution.py:348
  166.3 0.0 copy-done.1
  166.3 0.0 copy-start
  166.3 35.4 %shard_map.57 = (bf16[448,512]{1,0:T(8,128)(2,1)S(1)}, bf16[448,512]{1,0:T(8,128)(2,1)S(1)}) custom-call(f32[1280,128]{1,0:T(8,128)S(1)} %bitcast.8, bf16[2,448,256]{2,1,0:T(8,128)(2,1)S(1)} %bitcast.9, f32[32,16,512]{2,1,0:T(8,128)S(1)} %all-to-all-done.2.value_hbm), custom_call_target="tpu_custom_call" | custom-call | flops 5368709120 | bytes 4194304 | tf_op jit(solution)/shard_map/pallas_call | solution.py:168
  201.7 0.0 collective-permute-done.8.refs_3_
  201.7 0.0 collective-permute-done.7.refs_2_
  201.7 0.0 collective-permute-done.6.refs_1_
  201.7 0.0 copy-done
  201.7 2.9 %shard_map.58 = bf16[448,576]{1,0:T(8,128)(2,1)} custom-call(s32[2]{0:T(128)S(1)} %copy-done, f32[160,512]{1,0:T(8,128)S(1)} %pad_maximum_fusion.refs_0_, f32[160,512]{1,0:T(8,128)S(1)} %collective-permute-done.6.refs_1_, f32[160,512]{1,0:T(8,128)S(1)} %collective-permute-done.7.refs_2_, f32[160,512]{1,0:T(8,128)S(1)} %collective-permute-done.8.refs_3_, ...), custom_call_target="tpu_custom_call" | custom-call | tf_op jit(solution)/shard_map/pallas_call | solution.py:332
  (11 shorter events, 0.1 us)
Async XLA Ops:
  8.1 12.4 %collective-permute-start = (f32[16,56,512]{2,1,0:T(8,128)}, f32[16,56,512]{2,1,0:T(8,128)S(1)}, u32[]{:S(2)}, u32[]{:S(2)}) collective-permute-start(f32[16,56,512]{2,1,0:T(8,128)} %get-tuple-element.21), channel_id=1, source_target_pairs={{0,16},{16,0},{32,48},{48,32},{64,80},{80,64},{96,112},{112,96},{1... | collective-permute-start | bytes 5505032 | tf_op jit(solution)/shard_map/ppermute | solution.py:367
  23.6 3.9 %copy-start.2 = (bf16[48,512]{1,0:T(8,128)(2,1)S(1)}, bf16[48,512]{1,0:T(8,128)(2,1)}, u32[]{:S(2)}) copy-start(bf16[48,512]{1,0:T(8,128)(2,1)} %get-tuple-element.22) | copy-start | bytes 147460
  23.6 33.6 %all-to-all-start = ((f32[16,56,512]{2,1,0:T(8,128)}), f32[16,56,512]{2,1,0:T(8,128)S(1)}, u32[]{:S(2)}, u32[]{:S(2)}) async-start(f32[16,56,512]{2,1,0:T(8,128)} %add.17), calls=%async_computation | async-start | bytes 3670016 | tf_op jit(solution)/shard_map/all_to_all | solution.py:348
  27.5 0.7 collective-permute-start.1
  58.6 19.1 %all-to-all-start.1 = ((f32[32,40,128]{2,1,0:T(8,128)}), f32[32,40,128]{2,1,0:T(8,128)S(1)}, u32[]{:S(2)}, u32[]{:S(2)}) async-start(f32[32,40,128]{2,1,0:T(8,128)} %bitcast.4), calls=%async_computation.1 | async-start | bytes 1310720 | tf_op jit(solution)/shard_map/all_to_all | solution.py:348
  64.8 13.0 %collective-permute-start.2 = (f32[40,512]{1,0:T(8,128)S(1)}, f32[40,512]{1,0:T(8,128)S(1)}, u32[]{:S(2)}, u32[]{:S(2)}) collective-permute-start(f32[40,512]{1,0:T(8,128)S(1)} %get-tuple-element.23), channel_id=1, source_target_pairs={{0,0},{16,16},{1,32},{17,48},{2,64},{18,80},{3,96},{19,112},{4,128... | collective-permute-start | bytes 245768 | tf_op jit(solution)/shard_map/ppermute | solution.py:371
  79.0 48.4 %all-to-all-start.2 = ((f32[32,16,512]{2,1,0:T(8,128)}), f32[32,16,512]{2,1,0:T(8,128)S(1)}, u32[]{:S(2)}, u32[]{:S(2)}) async-start(f32[32,16,512]{2,1,0:T(8,128)} %broadcast_in_dim.9), calls=%async_computation.2 | async-start | bytes 2097152 | tf_op jit(solution)/shard_map/all_to_all | solution.py:348
  98.7 22.4 %collective-permute-start.5 = (f32[50,512]{1,0:T(8,128)S(1)}, f32[50,512]{1,0:T(8,128)S(1)}, u32[]{:S(2)}, u32[]{:S(2)}) collective-permute-start(f32[50,512]{1,0:T(8,128)S(1)} %pad_maximum_fusion.1), channel_id=1, source_target_pairs={{0,12},{1,13},{2,14},{3,15},{4,0},{5,1},{6,2},{7,3},{8,4},{9,5},{1... | collective-permute-start | bytes 307208 | tf_op jit(solution)/shard_map/ppermute | solution.py:344
  107.2 14.8 %collective-permute-start.4 = (f32[50,512]{1,0:T(8,128)S(1)}, f32[50,512]{1,0:T(8,128)S(1)}, u32[]{:S(2)}, u32[]{:S(2)}) collective-permute-start(f32[50,512]{1,0:T(8,128)S(1)} %pad_maximum_fusion.1), channel_id=1, source_target_pairs={{0,8},{1,9},{2,10},{3,11},{4,12},{5,13},{6,14},{7,15},{8,0},{9,1},... | collective-permute-start | bytes 307208 | tf_op jit(solution)/shard_map/ppermute | solution.py:344
  113.8 13.5 %collective-permute-start.3 = (f32[50,512]{1,0:T(8,128)S(1)}, f32[50,512]{1,0:T(8,128)S(1)}, u32[]{:S(2)}, u32[]{:S(2)}) collective-permute-start(f32[50,512]{1,0:T(8,128)S(1)} %pad_maximum_fusion.1), channel_id=1, source_target_pairs={{0,4},{1,5},{2,6},{3,7},{4,8},{5,9},{6,10},{7,11},{8,12},{9,13},{1... | collective-permute-start | bytes 307208 | tf_op jit(solution)/shard_map/ppermute | solution.py:344
  127.3 38.9 %copy-start.1 = (bf16[2,256,448]{1,2,0:T(8,128)(2,1)S(1)}, bf16[2,256,448]{1,2,0:T(8,128)(2,1)}, u32[]{:S(2)}) copy-start(bf16[2,256,448]{1,2,0:T(8,128)(2,1)} %param.9) | copy-start | bytes 1376260
  144.8 21.5 %all-to-all-start.4 = ((f32[32,40,128]{2,1,0:T(8,128)}), f32[32,40,128]{2,1,0:T(8,128)S(1)}, u32[]{:S(2)}, u32[]{:S(2)}) async-start(f32[32,40,128]{2,1,0:T(8,128)} %broadcast_in_dim.11), calls=%async_computation.4 | async-start | bytes 1310720 | tf_op jit(solution)/shard_map/all_to_all | solution.py:348
  153.4 48.3 %collective-permute-start.8 = (f32[160,512]{1,0:T(8,128)S(1)}, f32[160,512]{1,0:T(8,128)S(1)}, u32[]{:S(2)}, u32[]{:S(2)}) collective-permute-start(f32[160,512]{1,0:T(8,128)S(1)} %pad_maximum_fusion.refs_0_), channel_id=1, source_target_pairs={{0,15},{1,0},{2,1},{3,2},{4,3},{5,4},{6,5},{7,6},{8,7},{9,8},{10,9... | collective-permute-start | bytes 983048 | tf_op jit(solution)/shard_map/ppermute | solution.py:344
  158.7 43.0 %collective-permute-start.7 = (f32[160,512]{1,0:T(8,128)S(1)}, f32[160,512]{1,0:T(8,128)S(1)}, u32[]{:S(2)}, u32[]{:S(2)}) collective-permute-start(f32[160,512]{1,0:T(8,128)S(1)} %pad_maximum_fusion.refs_0_), channel_id=1, source_target_pairs={{0,2},{1,3},{2,4},{3,5},{4,6},{5,7},{6,8},{7,9},{8,10},{9,11},{10,... | collective-permute-start | bytes 983048 | tf_op jit(solution)/shard_map/ppermute | solution.py:344
  160.6 41.1 %collective-permute-start.6 = (f32[160,512]{1,0:T(8,128)S(1)}, f32[160,512]{1,0:T(8,128)S(1)}, u32[]{:S(2)}, u32[]{:S(2)}) collective-permute-start(f32[160,512]{1,0:T(8,128)S(1)} %pad_maximum_fusion.refs_0_), channel_id=1, source_target_pairs={{0,1},{1,2},{2,3},{3,4},{4,5},{5,6},{6,7},{7,8},{8,9},{9,10},{10,1... | collective-permute-start | bytes 983048 | tf_op jit(solution)/shard_map/ppermute | solution.py:344
  166.3 35.5 %copy-start = (s32[2]{0:T(128)S(1)}, s32[2]{0:T(128)}, u32[]{:S(2)}) copy-start(s32[2]{0:T(128)} %pad_add_fusion.place_ref) | copy-start | bytes 28

commit v6 on v5

--- a/solution.py
+++ b/solution.py
@@ -26,13 +26,18 @@
     return jnp.dot(a, b, preferred_element_type=jnp.float32)
 
 
-def solve_kernel(gram_ref, target_hbm, value_hbm, high_out, low_out, a_ref, a16_ref, z_ref, s_ref, r_ref, y_ref, target_ref, value_ref, sems):
+def solve_kernel(mine_ref, other_ref, target_hbm, high_out, low_out, gram_ref, a_ref, a16_ref, z_ref, s_ref, r_ref, y_ref, target_ref, sem):
     n = a_ref.shape[0]
     width = r_ref.shape[0]
-    target_copy = pltpu.make_async_copy(target_hbm, target_ref, sems.at[0])
-    value_copy = pltpu.make_async_copy(value_hbm, value_ref, sems.at[1])
+    target_copy = pltpu.make_async_copy(target_hbm, target_ref, sem)
     target_copy.start()
-    value_copy.start()
+    core = lax.axis_index("row") % 2
+    chips = mine_ref.shape[0]
+    share = gram_ref.shape[0] // (2 * chips)
+    sources = ((core, mine_ref), (1 - core, other_ref))
+    for h, ref in sources:
+        for k in range(chips):
+            gram_ref[pl.ds(pl.multiple_of((2 * k + h) * share, 8), share), :] = ref[k, :share, :]
     blocks = n // LANES
     rows = lax.broadcasted_iota(jnp.int32, (LANES, LANES), 0)
     cols = lax.broadcasted_iota(jnp.int32, (LANES, LANES), 1)
@@ -65,19 +70,19 @@
 
     def load_residual():
         target_copy.wait()
-        value_copy.wait()
         per_batch = target_ref.shape[2]
-        share = value_ref.shape[1]
         for b in range(target_ref.shape[0]):
             r_ref[:, b * per_batch:(b + 1) * per_batch] = target_ref[b].astype(jnp.float32)
-        half = n // 2
-        for r in range(value_ref.shape[0]):
-            k, h = r // 2, r % 2
-            tall = 2 * share if k % 2 == 0 else V_SHORT
-            begin = k // 2 * (2 * share + V_SHORT) + k % 2 * 2 * share
-            at = slice(h * half, (h + 1) * half)
-            r_ref[begin:begin + share, at] -= value_ref[r, :, :half]
-            r_ref[begin + share:begin + tall, at] -= value_ref[r, :tall - share, half:]
+        tile = (mine_ref.shape[1] - share) * LANES // n
+        for h, ref in sources:
+            for k in range(chips):
+                begin = k // 2 * (2 * tile + V_SHORT) + k % 2 * 2 * tile
+                for q in range(n // LANES):
+                    row = begin + q // 2 * tile
+                    tall = tile if q < 2 or k % 2 == 0 else V_SHORT - tile
+                    lanes = pl.ds(pl.multiple_of(h * (n // 2) + q % 2 * LANES, LANES), LANES)
+                    at = share + q * tile
+                    r_ref[row:row + tall, lanes] -= ref[k, at:at + tall, :]
 
     def more(carry):
         step, before, worst, limit = carry
@@ -158,9 +163,10 @@
         finish()
 
 
-def solve(gram_packed, targets, values):
+def solve(mine, other, targets):
     batches, width, per_batch = targets.shape
     n = batches * per_batch
+    blocks = n // LANES
     square = pltpu.VMEM((n, n), jnp.float32)
     wide = pltpu.VMEM((width, n), jnp.float32)
     vmem = pl.BlockSpec(memory_space=pltpu.VMEM)
@@ -168,9 +174,10 @@
     return pl.pallas_call(
         solve_kernel,
         out_shape=(out, out),
-        in_specs=[vmem, pl.BlockSpec(memory_space=pl.ANY), pl.BlockSpec(memory_space=pl.ANY)],
+        in_specs=[vmem, vmem, pl.BlockSpec(memory_space=pl.ANY)],
         out_specs=(vmem, vmem),
         scratch_shapes=[
+            pltpu.VMEM((blocks * (blocks + 1) // 2 * LANES, LANES), jnp.float32),
             square,
             pltpu.VMEM((2, n, n), jnp.bfloat16),
             square,
@@ -178,12 +185,11 @@
             wide,
             wide,
             pltpu.VMEM(targets.shape, targets.dtype),
-            pltpu.VMEM(values.shape, values.dtype),
-            pltpu.SemaphoreType.DMA((2,)),
+            pltpu.SemaphoreType.DMA,
         ],
         compiler_params=pltpu.CompilerParams(vmem_limit_bytes=VMEM_LIMIT),
         cost_estimate=pl.CostEstimate(flops=40 * n * n * n, bytes_accessed=4 * 2**20, transcendentals=0),
-    )(gram_packed, targets, values)
+    )(mine, other, targets)
 
 
 def contract_first(a, b):
@@ -194,23 +200,16 @@
     return index // 2 * (TALL + SHORT) + index % 2 * TALL
 
 
-def front_kernel(place_ref, index_ref, table_hbm, cov_hbm, weight_hbm, other_ref, mine_ref, slice_ref, table_ref, cov_ref, weight_ref, part_ref, value_ref, sems):
-    loads = [
-        pltpu.make_async_copy(src, dst, sems.at[i])
-        for i, (src, dst) in enumerate(((table_hbm, table_ref), (cov_hbm, cov_ref), (weight_hbm, weight_ref)))
-    ]
-    for load in loads:
-        load.start()
+def front_kernel(index_ref, table_ref, cov_ref, weight_ref, other_ref, mine_ref, slice_ref, part_ref, value_ref):
     here, n = table_ref.shape[0], slice_ref.shape[1]
     chips = mine_ref.shape[0]
     share = mine_ref.shape[1] - TALL
-    core, col = place_ref[0], place_ref[1]
+    core, col = lax.axis_index("row") % 2, lax.axis_index("col")
     batches, per_batch = index_ref.shape
     spot = lax.broadcasted_iota(jnp.int32, (table_ref.shape[1], per_batch), 0)
     picked = jnp.concatenate(
         [jnp.where(spot == index_ref[b:b + 1, :], 1.0, 0.0).astype(jnp.bfloat16) for b in range(batches)], axis=1
     )
-    loads[0].wait()
     keys = dot16(table_ref[...], picked).astype(jnp.bfloat16)
     padded = slice_ref.shape[0]
     slot = lax.broadcasted_iota(jnp.int32, (padded, here), 0)
@@ -220,9 +219,7 @@
     taken = jnp.logical_and(slot + first == spot, slot < TALL - odd * (TALL - SHORT))
     taken = jnp.where(taken, 1.0, 0.0).astype(jnp.bfloat16)
     slice_ref[...] = dot16(taken, keys).astype(jnp.bfloat16)
-    loads[2].wait()
     value_ref[...] = dot16(weight_ref[...], keys)
-    loads[1].wait()
     high, low = split(cov_ref[...])
     part_ref[...] = contract_first(high, keys) + contract_first(low, keys)
     for which, ref in ((core, mine_ref), (1 - core, other_ref)):
@@ -241,7 +238,7 @@
                 ref[j, TALL + second:, n // 2:] = jnp.zeros((share - second, n // 2), jnp.float32)
 
 
-def front(place, index, table, cov, weight, chips):
+def front(index, table, cov, weight, chips):
     n = index.size
     width = weight.shape[0]
     share = width // (2 * chips) + 2
@@ -250,18 +247,14 @@
     return pl.pallas_call(
         front_kernel,
         out_shape=(payload, payload, jax.ShapeDtypeStruct((PADDED, n), jnp.bfloat16)),
-        in_specs=[pl.BlockSpec(memory_space=pltpu.SMEM), vmem] + [pl.BlockSpec(memory_space=pl.ANY)] * 3,
+        in_specs=[vmem] * 4,
         out_specs=(vmem, vmem, vmem),
         scratch_shapes=[
-            pltpu.VMEM(table.shape, table.dtype),
-            pltpu.VMEM(cov.shape, cov.dtype),
-            pltpu.VMEM(weight.shape, weight.dtype),
             pltpu.VMEM((cov.shape[1], n), jnp.float32),
             pltpu.VMEM((width, n), jnp.float32),
-            pltpu.SemaphoreType.DMA((3,)),
         ],
-        compiler_params=pltpu.CompilerParams(vmem_limit_bytes=60 * 2**20),
-    )(place, index, table, cov, weight)
+        compiler_params=pltpu.CompilerParams(vmem_limit_bytes=VMEM_LIMIT),
+    )(index, table, cov, weight)
 
 
 def gram_kernel(received_ref, key_ref, panel_ref, value_ref, packed_ref):
@@ -270,7 +263,9 @@
         total = total + received_ref[j]
     panel = total[:TALL]
     panel_ref[...] = panel
-    value_ref[...] = total[TALL:]
+    tile = total.shape[0] - TALL
+    for q in range(total.shape[1] // LANES):
+        value_ref[q * tile:(q + 1) * tile, :] = total[TALL:, q * LANES:(q + 1) * LANES]
     n = panel.shape[1]
     padded = jnp.concatenate([panel, jnp.zeros((PADDED - TALL, n), jnp.float32)], axis=0)
     high = padded.astype(jnp.bfloat16)
@@ -295,7 +290,7 @@
         gram_kernel,
         out_shape=(
             jax.ShapeDtypeStruct((TALL, n), jnp.float32),
-            jax.ShapeDtypeStruct((received.shape[1] - TALL, n), jnp.float32),
+            jax.ShapeDtypeStruct(((received.shape[1] - TALL) * blocks, LANES), jnp.float32),
             jax.ShapeDtypeStruct((blocks * (blocks + 1) // 2 * LANES, LANES), jnp.float32),
         ),
         in_specs=[vmem] * 2,
@@ -304,12 +299,12 @@
     )(received, key_piece)
 
 
-def change_kernel(place_ref, *refs):
+def change_kernel(*refs):
     *bundle_refs, high_ref, low_ref, out_ref, panel_ref = refs
     cols = len(bundle_refs) * STRIDE
     for shift, ref in zip(SHIFTS, bundle_refs):
         for t in range(cols // STRIDE):
-            piece = lax.rem(place_ref[1] - shift - STRIDE * t + 2 * cols, cols)
+            piece = lax.rem(lax.axis_index("col") - shift - STRIDE * t + 2 * cols, cols)
             odd = lax.rem(piece, 2)
             begin = pl.multiple_of(lax.div(piece, 2) * (TALL + SHORT) + odd * TALL, 8)
             panel_ref[pl.ds(begin, SHORT), :] = ref[t * TALL:t * TALL + SHORT, :]
@@ -326,17 +321,17 @@
     out_ref[...] = out.astype(jnp.bfloat16)
 
 
-def change(place, bundles, solved, here):
+def change(bundles, solved, here):
     width, n = solved[0].shape
     vmem = pl.BlockSpec(memory_space=pltpu.VMEM)
     return pl.pallas_call(
         change_kernel,
         out_shape=jax.ShapeDtypeStruct((width, here), jnp.bfloat16),
-        in_specs=[pl.BlockSpec(memory_space=pltpu.SMEM)] + [vmem] * (len(bundles) + 2),
+        in_specs=[vmem] * (len(bundles) + 2),
         out_specs=vmem,
         scratch_shapes=[pltpu.VMEM((here, n), jnp.float32)],
         compiler_params=pltpu.CompilerParams(vmem_limit_bytes=VMEM_LIMIT),
-    )(place, *bundles, *solved)
+    )(*bundles, *solved)
 
 
 def moved(value, axis, shift):
@@ -358,12 +353,11 @@
     chips = rows // 2
     here = inverse_cov.shape[0]
     n = edit_index.size
-    place = jnp.stack([lax.axis_index("row") % 2, lax.axis_index("col")]).astype(jnp.int32)
     turned = [((2 * a + h) * cols + b, (2 * b + h) * cols + a) for a in range(chips) for b in range(cols) for h in range(2)]
     same_core = [[2 * k + h for k in range(chips)] for h in range(2)]
     other_core = [(r, r ^ 1) for r in range(rows)]
 
-    other, mine, key_slice = front(place, edit_index, key_table.T, inverse_cov, weight.T, chips)
+    other, mine, key_slice = front(edit_index, key_table.T, inverse_cov, weight.T, chips)
     half_sum = mine + lax.ppermute(other, "row", other_core)
     key_piece = lax.ppermute(key_slice, ("row", "col"), turned)
     panel_piece, value_piece, packed = gram_share(swapped(half_sum, "row", same_core), key_piece)
@@ -372,19 +366,20 @@
     share = packed.shape[0] // rows
     part = jnp.sum(swapped(packed.reshape(rows, share, LANES), "row"), axis=0)
     neighbours = [[STRIDE * g + i for i in range(STRIDE)] for g in range(cols // STRIDE)]
-    joined = jnp.concatenate([own, part.reshape(-1, n)], axis=0)
-    joined, value_piece = lax.optimization_barrier((joined, value_piece))
-    values = swapped(copies(value_piece, rows), "row")
+    joined = jnp.concatenate([own, part], axis=1)
     joined = [joined] + [moved(joined, "col", STRIDE * t) for t in range(1, cols // STRIDE)]
-    values, *joined = lax.optimization_barrier((values, *joined))
-    far = [item[:TALL] for item in joined]
-    part = sum(item[TALL:] for item in joined).reshape(share, LANES)
+    joined = lax.optimization_barrier(tuple(joined))
+    far = [item[:, :n] for item in joined]
+    part = sum(item[:, n:] for item in joined)
     part = jnp.sum(swapped(copies(part, STRIDE), "col", neighbours), axis=0)
-    gram = swapped(copies(part, rows), "row")
+    piece = jnp.concatenate([part, value_piece], axis=0)
+    mine = swapped(copies(piece, chips), "row", same_core)
     far = jnp.concatenate(far, axis=0)
     bundles = [far] + [moved(far, "col", shift) for shift in SHIFTS[1:]]
-    solved = solve(gram.reshape(rows * share, LANES), jnp.swapaxes(targets, 1, 2), values)
-    return change(place, bundles, solved, here).T
+    mine, bundles[1], bundles[2] = lax.optimization_barrier((mine, bundles[1], bundles[2]))
+    other = lax.ppermute(mine, "row", other_core)
+    solved = solve(mine, other, jnp.swapaxes(targets, 1, 2))
+    return change(bundles, solved, here).T
 
 
 def solution(mesh):

time: 205 us -> 209 us (1.020)
  waiting for transfers between devices: 54.8 us -> 69.1 us
  starting transfers between devices: 79.9 us -> 70.1 us
  Pallas kernels: 47.2 us -> 44.9 us
    all_to_all x4 -> x3, starting transfers between devices: 38.3 us -> 20 us  [swapped(): lax.all_to_all(value, axis, 0, 0, axis_index_groups=groups, tiled=True)]
    ppermute x6, waiting for transfers between devices: 6.21 us -> 24.4 us  [moved(): lax.ppermute(value, axis, [(i, (i + shift) % size) for i in range(size)])]
    ppermute x6, starting transfers between devices: 31.5 us -> 37.2 us  [moved(): lax.ppermute(value, axis, [(i, (i + shift) % size) for i in range(size)])]
    all_to_all x4 -> x3, waiting for transfers between devices: 45 us -> 41.3 us  [swapped(): lax.all_to_all(value, axis, 0, 0, axis_index_groups=groups, tiled=True)]
    unnamed x6 -> x8, local copies, waits for them, and re-layouts: 0.01 us -> 3.02 us
    ppermute x0 -> x1, starting transfers between devices: none -> 2.82 us  [shards(): other = lax.ppermute(mine, 'row', other_core)]
where the time goes in v6:
time: 209 us; the launch traced here: 208 us
  starting transfers between devices  70.1 us (34%)
  waiting for transfers between devices  69.1 us (33%)
  Pallas kernels  44.9 us (21%)
  blocking collectives  18.1 us (9%)
  local copies, waits for them, and re-layouts  4.01 us (2%)
    all_to_all x3, waiting for transfers between devices, swapped(): lax.all_to_all(value, axis, 0, 0, axis_index_groups=groups, tiled=True)  41.3 us
    ppermute x6, starting transfers between devices, moved(): lax.ppermute(value, axis, [(i, (i + shift) % size) for i in range(size)])  37.2 us
    pallas_call x1, Pallas kernels, solve(): pl.pallas_call(solve_kernel, out_shape=(out, out), in_specs=[vmem, vmem,...  35.8 us
    ppermute x6, waiting for transfers between devices, moved(): lax.ppermute(value, axis, [(i, (i + shift) % size) for i in range(size)])  24.4 us
    all_to_all x3, starting transfers between devices, swapped(): lax.all_to_all(value, axis, 0, 0, axis_index_groups=groups, tiled=True)  20 us
    all_to_all x1, blocking collectives, swapped(): lax.all_to_all(value, axis, 0, 0, axis_index_groups=groups, tiled=True)  18.1 us
    ppermute x1, starting transfers between devices, shards(): half_sum = mine + lax.ppermute(other, 'row', other_core)  8.78 us
    pallas_call x1, Pallas kernels, front(): pl.pallas_call(front_kernel, out_shape=(payload, payload, jax.ShapeDtypeS...  5.39 us
  transfers between devices with their start and end apart: 13, of which 6 were waited for; matrix products, arithmetic and copies ran while one was open for 0% of the time, Pallas kernels for 17%

profile of v6, /device:TPU:1, one launch (start us, length us, event | category | flops | bytes accessed | tf_op | source)
XLA Modules:
  0.0 208.3 jit_solution(14009362298170850990)
XLA Ops:
  0.0 0.0 copy-start
  0.0 1.3 copy-done
  1.3 0.0 copy-start.1
  1.3 1.1 copy-done.1
  2.3 0.0 copy-start.2
  2.3 0.7 copy-done.2
  3.0 5.4 %shard_map.55 = (f32[16,56,512]{2,1,0:T(8,128)S(1)}, f32[16,56,512]{2,1,0:T(8,128)S(1)}, bf16[48,512]{1,0:T(8,128)(2,1)S(1)}) custom-call(s32[2,256]{1,0:T(2,128)S(1)} %copy-done.2, bf16[576,1024]{1,0:T(8,128)(2,1)S(1)} %bitcast.5, f32[576,1152]{1,0:T(8,128)} %cov_ref.1, bf16[448,576]{1,0:T(8,128)(2,1)S(1)} %bitcast.6), custom_call_target="tpu_custom_call" | custom-call | tf_op jit(solution)/shard_map/pallas_call | solution.py:247
  8.4 8.8 %collective-permute-start = (f32[16,56,512]{2,1,0:T(8,128)S(1)}, f32[16,56,512]{2,1,0:T(8,128)S(1)}, u32[]{:S(2)}, u32[]{:S(2)}) collective-permute-start(f32[16,56,512]{2,1,0:T(8,128)S(1)} %get-tuple-element.21), channel_id=1, source_target_pairs={{0,16},{16,0},{32,48},{48,32},{64,80},{80,64},{96,112},{112,96},{1... | collective-permute-start | bytes 5505032 | tf_op jit(solution)/shard_map/ppermute | solution.py:361
  17.2 3.4 %collective-permute-done = f32[16,56,512]{2,1,0:T(8,128)S(1)} collective-permute-done((f32[16,56,512]{2,1,0:T(8,128)S(1)}, f32[16,56,512]{2,1,0:T(8,128)S(1)}, u32[]{:S(2)}, u32[]{:S(2)}) %collective-permute-start) | collective-permute-done | bytes 1835040 | tf_op jit(solution)/shard_map/ppermute | solution.py:361
  20.6 1.7 add.12
  22.3 3.7 %all-to-all-start = ((f32[16,56,512]{2,1,0:T(8,128)}), f32[16,56,512]{2,1,0:T(8,128)S(1)}, u32[]{:S(2)}, u32[]{:S(2)}) async-start(f32[16,56,512]{2,1,0:T(8,128)} %add.12), calls=%async_computation | async-start | bytes 3670016 | tf_op jit(solution)/shard_map/all_to_all | solution.py:343
  26.0 0.7 collective-permute-start.1
  26.7 0.0 collective-permute-done.1.key_ref
  26.7 29.0 %all-to-all-done.received_ref = f32[16,56,512]{2,1,0:T(8,128)S(1)} async-done(((f32[16,56,512]{2,1,0:T(8,128)}), f32[16,56,512]{2,1,0:T(8,128)S(1)}, u32[]{:S(2)}, u32[]{:S(2)}) %all-to-all-start) | async-done | bytes 1835040 | tf_op jit(solution)/shard_map/all_to_all | solution.py:343
  55.7 1.5 shard_map.56
  57.2 6.2 %all-to-all-start.1 = ((f32[32,40,128]{2,1,0:T(8,128)}), f32[32,40,128]{2,1,0:T(8,128)S(1)}, u32[]{:S(2)}, u32[]{:S(2)}) async-start(f32[32,40,128]{2,1,0:T(8,128)} %bitcast.2), calls=%async_computation.1 | async-start | bytes 1310720 | tf_op jit(solution)/shard_map/all_to_all | solution.py:343
  63.4 0.7 collective-permute-start.2
  64.0 12.2 %all-to-all-done.1 = f32[32,40,128]{2,1,0:T(8,128)S(1)} async-done(((f32[32,40,128]{2,1,0:T(8,128)}), f32[32,40,128]{2,1,0:T(8,128)S(1)}, u32[]{:S(2)}, u32[]{:S(2)}) %all-to-all-start.1) | async-done | bytes 655392 | tf_op jit(solution)/shard_map/all_to_all | solution.py:343
  76.3 0.1 reduce_sum.18
  76.3 0.0 collective-permute-done.2
  76.4 11.8 %collective-permute-start.5 = (f32[40,640]{1,0:T(8,128)S(1)}, f32[40,640]{1,0:T(8,128)S(1)}, u32[]{:S(2)}, u32[]{:S(2)}) collective-permute-start(f32[40,640]{1,0:T(8,128)S(1)} %pad_maximum_fusion.1), channel_id=1, source_target_pairs={{0,12},{1,13},{2,14},{3,15},{4,0},{5,1},{6,2},{7,3},{8,4},{9,5},{1... | collective-permute-start | bytes 307208 | tf_op jit(solution)/shard_map/ppermute | solution.py:339
  88.1 10.3 %collective-permute-start.4 = (f32[40,640]{1,0:T(8,128)S(1)}, f32[40,640]{1,0:T(8,128)S(1)}, u32[]{:S(2)}, u32[]{:S(2)}) collective-permute-start(f32[40,640]{1,0:T(8,128)S(1)} %pad_maximum_fusion.1), channel_id=1, source_target_pairs={{0,8},{1,9},{2,10},{3,11},{4,12},{5,13},{6,14},{7,15},{8,0},{9,1},... | collective-permute-start | bytes 307208 | tf_op jit(solution)/shard_map/ppermute | solution.py:339
  98.4 7.3 %collective-permute-start.3 = (f32[40,640]{1,0:T(8,128)S(1)}, f32[40,640]{1,0:T(8,128)S(1)}, u32[]{:S(2)}, u32[]{:S(2)}) collective-permute-start(f32[40,640]{1,0:T(8,128)S(1)} %pad_maximum_fusion.1), channel_id=1, source_target_pairs={{0,4},{1,5},{2,6},{3,7},{4,8},{5,9},{6,10},{7,11},{8,12},{9,13},{1... | collective-permute-start | bytes 307208 | tf_op jit(solution)/shard_map/ppermute | solution.py:339
  105.7 0.0 collective-permute-done.5
  105.7 0.0 collective-permute-done.4
  105.7 2.3 %collective-permute-done.3 = f32[40,640]{1,0:T(8,128)S(1)} collective-permute-done((f32[40,640]{1,0:T(8,128)S(1)}, f32[40,640]{1,0:T(8,128)S(1)}, u32[]{:S(2)}, u32[]{:S(2)}) %collective-permute-start.3) | collective-permute-done | bytes 102432 | tf_op jit(solution)/shard_map/ppermute | solution.py:339
  108.0 18.1 %all_to_all.20 = f32[4,40,128]{2,1,0:T(8,128)S(1)} all-to-all(f32[4,40,128]{2,1,0:T(8,128)S(1)} %broadcast_in_dim.6), channel_id=1, replica_groups={{0,1,2,3},{4,5,6,7},{8,9,10,11},{12,13,14,15},{16,17,18,19},{20,21,22,2..., dimensions={0} | all-to-all | bytes 163840 | tf_op jit(solution)/shard_map/all_to_all | solution.py:343
  126.2 0.0 copy-start.3
  126.2 1.0 broadcast_in_dim.7
  127.1 10.1 %all-to-all-start.3 = ((f32[16,104,128]{2,1,0:T(8,128)}), f32[16,104,128]{2,1,0:T(8,128)S(1)}, u32[]{:S(2)}, u32[]{:S(2)}) async-start(f32[16,104,128]{2,1,0:T(8,128)} %broadcast_in_dim.7), calls=%async_computation.3 | async-start | bytes 1703936 | tf_op jit(solution)/shard_map/all_to_all | solution.py:343
  137.3 2.7 %collective-permute-start.7 = (f32[160,512]{1,0:T(8,128)S(1)}, f32[160,512]{1,0:T(8,128)S(1)}, u32[]{:S(2)}, u32[]{:S(2)}) collective-permute-start(f32[160,512]{1,0:T(8,128)S(1)} %pad_maximum_fusion.refs_0_), channel_id=1, source_target_pairs={{0,2},{1,3},{2,4},{3,5},{4,6},{5,7},{6,8},{7,9},{8,10},{9,11},{10,... | collective-permute-start | bytes 983048 | tf_op jit(solution)/shard_map/ppermute | solution.py:339
  140.0 2.6 %collective-permute-start.6 = (f32[160,512]{1,0:T(8,128)S(1)}, f32[160,512]{1,0:T(8,128)S(1)}, u32[]{:S(2)}, u32[]{:S(2)}) collective-permute-start(f32[160,512]{1,0:T(8,128)S(1)} %pad_maximum_fusion.refs_0_), channel_id=1, source_target_pairs={{0,1},{1,2},{2,3},{3,4},{4,5},{5,6},{6,7},{7,8},{8,9},{9,10},{10,1... | collective-permute-start | bytes 983048 | tf_op jit(solution)/shard_map/ppermute | solution.py:339
  142.6 7.9 %collective-permute-done.7.refs_2_ = f32[160,512]{1,0:T(8,128)S(1)} collective-permute-done((f32[160,512]{1,0:T(8,128)S(1)}, f32[160,512]{1,0:T(8,128)S(1)}, u32[]{:S(2)}, u32[]{:S(2)}) %collective-permute-start.7) | collective-permute-done | bytes 327712 | tf_op jit(solution)/shard_map/ppermute | solution.py:339
  150.5 14.3 %collective-permute-done.6.refs_1_ = f32[160,512]{1,0:T(8,128)S(1)} collective-permute-done((f32[160,512]{1,0:T(8,128)S(1)}, f32[160,512]{1,0:T(8,128)S(1)}, u32[]{:S(2)}, u32[]{:S(2)}) %collective-permute-start.6) | collective-permute-done | bytes 327712 | tf_op jit(solution)/shard_map/ppermute | solution.py:339
  164.8 0.0 all-to-all-done.3.mine_ref
  164.8 2.8 %collective-permute-start.9 = (f32[16,104,128]{2,1,0:T(8,128)S(1)}, f32[16,104,128]{2,1,0:T(8,128)S(1)}, u32[]{:S(2)}, u32[]{:S(2)}) collective-permute-start(f32[16,104,128]{2,1,0:T(8,128)S(1)} %all-to-all-done.3.mine_ref), channel_id=1, source_target_pairs={{0,16},{16,0},{32,48},{48,32},{64,80},{80,64},{96,112},{112,96},{1... | collective-permute-start | bytes 2555912 | tf_op jit(solution)/shard_map/ppermute | solution.py:380
  167.6 2.6 %collective-permute-start.8 = (f32[160,512]{1,0:T(8,128)S(1)}, f32[160,512]{1,0:T(8,128)S(1)}, u32[]{:S(2)}, u32[]{:S(2)}) collective-permute-start(f32[160,512]{1,0:T(8,128)S(1)} %pad_maximum_fusion.refs_0_), channel_id=1, source_target_pairs={{0,15},{1,0},{2,1},{3,2},{4,3},{5,4},{6,5},{7,6},{8,7},{9,8},{10,9... | collective-permute-start | bytes 983048 | tf_op jit(solution)/shard_map/ppermute | solution.py:339
  170.2 0.0 collective-permute-done.9.other_ref
  170.2 0.0 copy-done.3
  170.2 35.8 %shard_map.57 = (bf16[448,512]{1,0:T(8,128)(2,1)S(1)}, bf16[448,512]{1,0:T(8,128)(2,1)S(1)}) custom-call(f32[16,104,128]{2,1,0:T(8,128)S(1)} %all-to-all-done.3.mine_ref, f32[16,104,128]{2,1,0:T(8,128)S(1)} %collective-permute-done.9.other_ref, bf16[2,448,256]{2,1,0:T(8,128)(2,1)S(1)} %bitcast.7), custom_call_target="tpu_custom_call" | custom-call | flops 5368709120 | bytes 4194304 | tf_op jit(solution)/shard_map/pallas_call | solution.py:174
  206.0 0.0 collective-permute-done.8.refs_3_
  206.0 2.3 %shard_map.58 = bf16[448,576]{1,0:T(8,128)(2,1)} custom-call(f32[160,512]{1,0:T(8,128)S(1)} %pad_maximum_fusion.refs_0_, f32[160,512]{1,0:T(8,128)S(1)} %collective-permute-done.6.refs_1_, f32[160,512]{1,0:T(8,128)S(1)} %collective-permute-done.7.refs_2_, f32[160,512]{1,0:T(8,128)S(1)} %collective-permute-done.8.refs_3_, ...), custom_call_target="tpu_custom_call" | custom-call | tf_op jit(solution)/shard_map/pallas_call | solution.py:327
  (10 shorter events, 0.1 us)
Async XLA Ops:
  0.0 1.3 copy-start
  1.3 1.1 copy-start.1
  2.3 0.7 copy-start.2
  8.4 12.2 %collective-permute-start = (f32[16,56,512]{2,1,0:T(8,128)S(1)}, f32[16,56,512]{2,1,0:T(8,128)S(1)}, u32[]{:S(2)}, u32[]{:S(2)}) collective-permute-start(f32[16,56,512]{2,1,0:T(8,128)S(1)} %get-tuple-element.21), channel_id=1, source_target_pairs={{0,16},{16,0},{32,48},{48,32},{64,80},{80,64},{96,112},{112,96},{1... | collective-permute-start | bytes 5505032 | tf_op jit(solution)/shard_map/ppermute | solution.py:361
  22.3 33.4 %all-to-all-start = ((f32[16,56,512]{2,1,0:T(8,128)}), f32[16,56,512]{2,1,0:T(8,128)S(1)}, u32[]{:S(2)}, u32[]{:S(2)}) async-start(f32[16,56,512]{2,1,0:T(8,128)} %add.12), calls=%async_computation | async-start | bytes 3670016 | tf_op jit(solution)/shard_map/all_to_all | solution.py:343
  26.0 0.7 collective-permute-start.1
  57.2 19.1 %all-to-all-start.1 = ((f32[32,40,128]{2,1,0:T(8,128)}), f32[32,40,128]{2,1,0:T(8,128)S(1)}, u32[]{:S(2)}, u32[]{:S(2)}) async-start(f32[32,40,128]{2,1,0:T(8,128)} %bitcast.2), calls=%async_computation.1 | async-start | bytes 1310720 | tf_op jit(solution)/shard_map/all_to_all | solution.py:343
  63.4 13.0 %collective-permute-start.2 = (f32[40,512]{1,0:T(8,128)S(1)}, f32[40,512]{1,0:T(8,128)S(1)}, u32[]{:S(2)}, u32[]{:S(2)}) collective-permute-start(f32[40,512]{1,0:T(8,128)S(1)} %get-tuple-element.23), channel_id=1, source_target_pairs={{0,0},{16,16},{1,32},{17,48},{2,64},{18,80},{3,96},{19,112},{4,128... | collective-permute-start | bytes 245768 | tf_op jit(solution)/shard_map/ppermute | solution.py:365
  76.4 29.4 %collective-permute-start.5 = (f32[40,640]{1,0:T(8,128)S(1)}, f32[40,640]{1,0:T(8,128)S(1)}, u32[]{:S(2)}, u32[]{:S(2)}) collective-permute-start(f32[40,640]{1,0:T(8,128)S(1)} %pad_maximum_fusion.1), channel_id=1, source_target_pairs={{0,12},{1,13},{2,14},{3,15},{4,0},{5,1},{6,2},{7,3},{8,4},{9,5},{1... | collective-permute-start | bytes 307208 | tf_op jit(solution)/shard_map/ppermute | solution.py:339
  88.1 17.6 %collective-permute-start.4 = (f32[40,640]{1,0:T(8,128)S(1)}, f32[40,640]{1,0:T(8,128)S(1)}, u32[]{:S(2)}, u32[]{:S(2)}) collective-permute-start(f32[40,640]{1,0:T(8,128)S(1)} %pad_maximum_fusion.1), channel_id=1, source_target_pairs={{0,8},{1,9},{2,10},{3,11},{4,12},{5,13},{6,14},{7,15},{8,0},{9,1},... | collective-permute-start | bytes 307208 | tf_op jit(solution)/shard_map/ppermute | solution.py:339
  98.4 9.6 %collective-permute-start.3 = (f32[40,640]{1,0:T(8,128)S(1)}, f32[40,640]{1,0:T(8,128)S(1)}, u32[]{:S(2)}, u32[]{:S(2)}) collective-permute-start(f32[40,640]{1,0:T(8,128)S(1)} %pad_maximum_fusion.1), channel_id=1, source_target_pairs={{0,4},{1,5},{2,6},{3,7},{4,8},{5,9},{6,10},{7,11},{8,12},{9,13},{1... | collective-permute-start | bytes 307208 | tf_op jit(solution)/shard_map/ppermute | solution.py:339
  126.2 44.0 %copy-start.3 = (bf16[2,256,448]{1,2,0:T(8,128)(2,1)S(1)}, bf16[2,256,448]{1,2,0:T(8,128)(2,1)}, u32[]{:S(2)}) copy-start(bf16[2,256,448]{1,2,0:T(8,128)(2,1)} %param.9) | copy-start | bytes 1376260
  127.1 37.6 %all-to-all-start.3 = ((f32[16,104,128]{2,1,0:T(8,128)}), f32[16,104,128]{2,1,0:T(8,128)S(1)}, u32[]{:S(2)}, u32[]{:S(2)}) async-start(f32[16,104,128]{2,1,0:T(8,128)} %broadcast_in_dim.7), calls=%async_computation.3 | async-start | bytes 1703936 | tf_op jit(solution)/shard_map/all_to_all | solution.py:343
  137.3 13.1 %collective-permute-start.7 = (f32[160,512]{1,0:T(8,128)S(1)}, f32[160,512]{1,0:T(8,128)S(1)}, u32[]{:S(2)}, u32[]{:S(2)}) collective-permute-start(f32[160,512]{1,0:T(8,128)S(1)} %pad_maximum_fusion.refs_0_), channel_id=1, source_target_pairs={{0,2},{1,3},{2,4},{3,5},{4,6},{5,7},{6,8},{7,9},{8,10},{9,11},{10,... | collective-permute-start | bytes 983048 | tf_op jit(solution)/shard_map/ppermute | solution.py:339
  140.0 24.7 %collective-permute-start.6 = (f32[160,512]{1,0:T(8,128)S(1)}, f32[160,512]{1,0:T(8,128)S(1)}, u32[]{:S(2)}, u32[]{:S(2)}) collective-permute-start(f32[160,512]{1,0:T(8,128)S(1)} %pad_maximum_fusion.refs_0_), channel_id=1, source_target_pairs={{0,1},{1,2},{2,3},{3,4},{4,5},{5,6},{6,7},{7,8},{8,9},{9,10},{10,1... | collective-permute-start | bytes 983048 | tf_op jit(solution)/shard_map/ppermute | solution.py:339
  164.8 5.4 %collective-permute-start.9 = (f32[16,104,128]{2,1,0:T(8,128)S(1)}, f32[16,104,128]{2,1,0:T(8,128)S(1)}, u32[]{:S(2)}, u32[]{:S(2)}) collective-permute-start(f32[16,104,128]{2,1,0:T(8,128)S(1)} %all-to-all-done.3.mine_ref), channel_id=1, source_target_pairs={{0,16},{16,0},{32,48},{48,32},{64,80},{80,64},{96,112},{112,96},{1... | collective-permute-start | bytes 2555912 | tf_op jit(solution)/shard_map/ppermute | solution.py:380
  167.6 38.4 %collective-permute-start.8 = (f32[160,512]{1,0:T(8,128)S(1)}, f32[160,512]{1,0:T(8,128)S(1)}, u32[]{:S(2)}, u32[]{:S(2)}) collective-permute-start(f32[160,512]{1,0:T(8,128)S(1)} %pad_maximum_fusion.refs_0_), channel_id=1, source_target_pairs={{0,15},{1,0},{2,1},{3,2},{4,3},{5,4},{6,5},{7,6},{8,7},{9,8},{10,9... | collective-permute-start | bytes 983048 | tf_op jit(solution)/shard_map/ppermute | solution.py:339

commit v7 on v6

--- a/solution.py
+++ b/solution.py
@@ -26,18 +26,14 @@
     return jnp.dot(a, b, preferred_element_type=jnp.float32)
 
 
-def solve_kernel(mine_ref, other_ref, target_hbm, high_out, low_out, gram_ref, a_ref, a16_ref, z_ref, s_ref, r_ref, y_ref, target_ref, sem):
+def solve_kernel(pieces_ref, target_hbm, high_out, low_out, gram_ref, a_ref, a16_ref, z_ref, s_ref, r_ref, y_ref, target_ref, sem):
     n = a_ref.shape[0]
     width = r_ref.shape[0]
     target_copy = pltpu.make_async_copy(target_hbm, target_ref, sem)
     target_copy.start()
-    core = lax.axis_index("row") % 2
-    chips = mine_ref.shape[0]
-    share = gram_ref.shape[0] // (2 * chips)
-    sources = ((core, mine_ref), (1 - core, other_ref))
-    for h, ref in sources:
-        for k in range(chips):
-            gram_ref[pl.ds(pl.multiple_of((2 * k + h) * share, 8), share), :] = ref[k, :share, :]
+    share = gram_ref.shape[0] // pieces_ref.shape[0]
+    for r in range(pieces_ref.shape[0]):
+        gram_ref[r * share:(r + 1) * share, :] = pieces_ref[r, :share, :]
     blocks = n // LANES
     rows = lax.broadcasted_iota(jnp.int32, (LANES, LANES), 0)
     cols = lax.broadcasted_iota(jnp.int32, (LANES, LANES), 1)
@@ -73,16 +69,16 @@
         per_batch = target_ref.shape[2]
         for b in range(target_ref.shape[0]):
             r_ref[:, b * per_batch:(b + 1) * per_batch] = target_ref[b].astype(jnp.float32)
-        tile = (mine_ref.shape[1] - share) * LANES // n
-        for h, ref in sources:
-            for k in range(chips):
-                begin = k // 2 * (2 * tile + V_SHORT) + k % 2 * 2 * tile
-                for q in range(n // LANES):
-                    row = begin + q // 2 * tile
-                    tall = tile if q < 2 or k % 2 == 0 else V_SHORT - tile
-                    lanes = pl.ds(pl.multiple_of(h * (n // 2) + q % 2 * LANES, LANES), LANES)
-                    at = share + q * tile
-                    r_ref[row:row + tall, lanes] -= ref[k, at:at + tall, :]
+        tile = (pieces_ref.shape[1] - share) * LANES // n
+        for r in range(pieces_ref.shape[0]):
+            k, h = r // 2, r % 2
+            begin = k // 2 * (2 * tile + V_SHORT) + k % 2 * 2 * tile
+            for q in range(n // LANES):
+                row = begin + q // 2 * tile
+                tall = tile if q < 2 or k % 2 == 0 else V_SHORT - tile
+                lane = h * (n // 2) + q % 2 * LANES
+                at = share + q * tile
+                r_ref[row:row + tall, lane:lane + LANES] -= pieces_ref[r, at:at + tall, :]
 
     def more(carry):
         step, before, worst, limit = carry
@@ -163,7 +159,7 @@
         finish()
 
 
-def solve(mine, other, targets):
+def solve(pieces, targets):
     batches, width, per_batch = targets.shape
     n = batches * per_batch
     blocks = n // LANES
@@ -174,7 +170,7 @@
     return pl.pallas_call(
         solve_kernel,
         out_shape=(out, out),
-        in_specs=[vmem, vmem, pl.BlockSpec(memory_space=pl.ANY)],
+        in_specs=[vmem, pl.BlockSpec(memory_space=pl.ANY)],
         out_specs=(vmem, vmem),
         scratch_shapes=[
             pltpu.VMEM((blocks * (blocks + 1) // 2 * LANES, LANES), jnp.float32),
@@ -189,7 +185,7 @@
         ],
         compiler_params=pltpu.CompilerParams(vmem_limit_bytes=VMEM_LIMIT),
         cost_estimate=pl.CostEstimate(flops=40 * n * n * n, bytes_accessed=4 * 2**20, transcendentals=0),
-    )(mine, other, targets)
+    )(pieces, targets)
 
 
 def contract_first(a, b):
@@ -373,12 +369,10 @@
     part = sum(item[:, n:] for item in joined)
     part = jnp.sum(swapped(copies(part, STRIDE), "col", neighbours), axis=0)
     piece = jnp.concatenate([part, value_piece], axis=0)
-    mine = swapped(copies(piece, chips), "row", same_core)
+    pieces = swapped(copies(piece, rows), "row")
     far = jnp.concatenate(far, axis=0)
     bundles = [far] + [moved(far, "col", shift) for shift in SHIFTS[1:]]
-    mine, bundles[1], bundles[2] = lax.optimization_barrier((mine, bundles[1], bundles[2]))
-    other = lax.ppermute(mine, "row", other_core)
-    solved = solve(mine, other, jnp.swapaxes(targets, 1, 2))
+    solved = solve(pieces, jnp.swapaxes(targets, 1, 2))
     return change(bundles, solved, here).T
 
 

time: 209 us -> 202 us (0.967)
  waiting for transfers between devices: 69.1 us -> 61.9 us
    ppermute x6, waiting for transfers between devices: 24.4 us -> 2.29 us  [moved(): lax.ppermute(value, axis, [(i, (i + shift) % size) for i in range(size)])]
    all_to_all x3, waiting for transfers between devices: 41.3 us -> 56.2 us  [swapped(): lax.all_to_all(value, axis, 0, 0, axis_index_groups=groups, tiled=True)]
    ppermute x1 -> x0, starting transfers between devices: 2.82 us -> none  [shards(): other = lax.ppermute(mine, 'row', other_core)]
    all_to_all x3, starting transfers between devices: 20 us -> 22.6 us  [swapped(): lax.all_to_all(value, axis, 0, 0, axis_index_groups=groups, tiled=True)]
  transfers between devices with their start and end apart: 13 -> 12, of which waited for: 6 -> 5; matrix products, arithmetic and copies ran while one was open for 0% -> 0% of each run, Pallas kernels for 17% -> 18%
where the time goes in v7:
time: 202 us; the launch traced here: 201 us
  starting transfers between devices  70.5 us (35%)
  waiting for transfers between devices  61.9 us (31%)
  Pallas kernels  44.5 us (22%)
  blocking collectives  18.1 us (9%)
  local copies, waits for them, and re-layouts  4.36 us (2%)
    all_to_all x3, waiting for transfers between devices, swapped(): lax.all_to_all(value, axis, 0, 0, axis_index_groups=groups, tiled=True)  56.2 us
    ppermute x6, starting transfers between devices, moved(): lax.ppermute(value, axis, [(i, (i + shift) % size) for i in range(size)])  37.7 us
    pallas_call x1, Pallas kernels, solve(): pl.pallas_call(solve_kernel, out_shape=(out, out), in_specs=[vmem, pl.Blo...  35.3 us
    all_to_all x3, starting transfers between devices, swapped(): lax.all_to_all(value, axis, 0, 0, axis_index_groups=groups, tiled=True)  22.6 us
    all_to_all x1, blocking collectives, swapped(): lax.all_to_all(value, axis, 0, 0, axis_index_groups=groups, tiled=True)  18.1 us
    ppermute x1, starting transfers between devices, shards(): half_sum = mine + lax.ppermute(other, 'row', other_core)  8.78 us
    pallas_call x1, Pallas kernels, front(): pl.pallas_call(front_kernel, out_shape=(payload, payload, jax.ShapeDtypeS...  5.39 us
  transfers between devices with their start and end apart: 12, of which 5 were waited for; matrix products, arithmetic and copies ran while one was open for 0% of the time, Pallas kernels for 18%

profile of v7, /device:TPU:1, one launch (start us, length us, event | category | flops | bytes accessed | tf_op | source)
XLA Modules:
  0.0 201.4 jit_solution(16276993116563614115)
XLA Ops:
  0.0 0.0 copy-start
  0.0 1.3 copy-done
  1.3 0.0 copy-start.1
  1.3 1.1 copy-done.1
  2.3 0.0 copy-start.2
  2.3 0.7 copy-done.2
  3.0 5.4 %shard_map.55 = (f32[16,56,512]{2,1,0:T(8,128)S(1)}, f32[16,56,512]{2,1,0:T(8,128)S(1)}, bf16[48,512]{1,0:T(8,128)(2,1)S(1)}) custom-call(s32[2,256]{1,0:T(2,128)S(1)} %copy-done.2, bf16[576,1024]{1,0:T(8,128)(2,1)S(1)} %bitcast.5, f32[576,1152]{1,0:T(8,128)} %cov_ref.1, bf16[448,576]{1,0:T(8,128)(2,1)S(1)} %bitcast.6), custom_call_target="tpu_custom_call" | custom-call | tf_op jit(solution)/shard_map/pallas_call | solution.py:243
  8.4 8.8 %collective-permute-start = (f32[16,56,512]{2,1,0:T(8,128)S(1)}, f32[16,56,512]{2,1,0:T(8,128)S(1)}, u32[]{:S(2)}, u32[]{:S(2)}) collective-permute-start(f32[16,56,512]{2,1,0:T(8,128)S(1)} %get-tuple-element.18), channel_id=1, source_target_pairs={{0,16},{16,0},{32,48},{48,32},{64,80},{80,64},{96,112},{112,96},{1... | collective-permute-start | bytes 5505032 | tf_op jit(solution)/shard_map/ppermute | solution.py:357
  17.2 3.4 %collective-permute-done = f32[16,56,512]{2,1,0:T(8,128)S(1)} collective-permute-done((f32[16,56,512]{2,1,0:T(8,128)S(1)}, f32[16,56,512]{2,1,0:T(8,128)S(1)}, u32[]{:S(2)}, u32[]{:S(2)}) %collective-permute-start) | collective-permute-done | bytes 1835040 | tf_op jit(solution)/shard_map/ppermute | solution.py:357
  20.6 1.7 add.12
  22.3 3.7 %all-to-all-start = ((f32[16,56,512]{2,1,0:T(8,128)}), f32[16,56,512]{2,1,0:T(8,128)S(1)}, u32[]{:S(2)}, u32[]{:S(2)}) async-start(f32[16,56,512]{2,1,0:T(8,128)} %add.12), calls=%async_computation | async-start | bytes 3670016 | tf_op jit(solution)/shard_map/all_to_all | solution.py:339
  26.0 0.7 collective-permute-start.1
  26.7 0.0 collective-permute-done.1.key_ref
  26.7 29.0 %all-to-all-done.received_ref = f32[16,56,512]{2,1,0:T(8,128)S(1)} async-done(((f32[16,56,512]{2,1,0:T(8,128)}), f32[16,56,512]{2,1,0:T(8,128)S(1)}, u32[]{:S(2)}, u32[]{:S(2)}) %all-to-all-start) | async-done | bytes 1835040 | tf_op jit(solution)/shard_map/all_to_all | solution.py:339
  55.7 1.5 shard_map.56
  57.2 6.2 %all-to-all-start.1 = ((f32[32,40,128]{2,1,0:T(8,128)}), f32[32,40,128]{2,1,0:T(8,128)S(1)}, u32[]{:S(2)}, u32[]{:S(2)}) async-start(f32[32,40,128]{2,1,0:T(8,128)} %bitcast.2), calls=%async_computation.1 | async-start | bytes 1310720 | tf_op jit(solution)/shard_map/all_to_all | solution.py:339
  63.4 0.7 collective-permute-start.2
  64.0 12.2 %all-to-all-done.1 = f32[32,40,128]{2,1,0:T(8,128)S(1)} async-done(((f32[32,40,128]{2,1,0:T(8,128)}), f32[32,40,128]{2,1,0:T(8,128)S(1)}, u32[]{:S(2)}, u32[]{:S(2)}) %all-to-all-start.1) | async-done | bytes 655392 | tf_op jit(solution)/shard_map/all_to_all | solution.py:339
  76.3 0.1 reduce_sum.18
  76.3 0.0 collective-permute-done.2
  76.4 11.8 %collective-permute-start.5 = (f32[40,640]{1,0:T(8,128)S(1)}, f32[40,640]{1,0:T(8,128)S(1)}, u32[]{:S(2)}, u32[]{:S(2)}) collective-permute-start(f32[40,640]{1,0:T(8,128)S(1)} %pad_maximum_fusion.1), channel_id=1, source_target_pairs={{0,12},{1,13},{2,14},{3,15},{4,0},{5,1},{6,2},{7,3},{8,4},{9,5},{1... | collective-permute-start | bytes 307208 | tf_op jit(solution)/shard_map/ppermute | solution.py:335
  88.2 10.3 %collective-permute-start.4 = (f32[40,640]{1,0:T(8,128)S(1)}, f32[40,640]{1,0:T(8,128)S(1)}, u32[]{:S(2)}, u32[]{:S(2)}) collective-permute-start(f32[40,640]{1,0:T(8,128)S(1)} %pad_maximum_fusion.1), channel_id=1, source_target_pairs={{0,8},{1,9},{2,10},{3,11},{4,12},{5,13},{6,14},{7,15},{8,0},{9,1},... | collective-permute-start | bytes 307208 | tf_op jit(solution)/shard_map/ppermute | solution.py:335
  98.5 7.3 %collective-permute-start.3 = (f32[40,640]{1,0:T(8,128)S(1)}, f32[40,640]{1,0:T(8,128)S(1)}, u32[]{:S(2)}, u32[]{:S(2)}) collective-permute-start(f32[40,640]{1,0:T(8,128)S(1)} %pad_maximum_fusion.1), channel_id=1, source_target_pairs={{0,4},{1,5},{2,6},{3,7},{4,8},{5,9},{6,10},{7,11},{8,12},{9,13},{1... | collective-permute-start | bytes 307208 | tf_op jit(solution)/shard_map/ppermute | solution.py:335
  105.7 0.0 collective-permute-done.5
  105.7 0.0 collective-permute-done.4
  105.8 2.3 %collective-permute-done.3 = f32[40,640]{1,0:T(8,128)S(1)} collective-permute-done((f32[40,640]{1,0:T(8,128)S(1)}, f32[40,640]{1,0:T(8,128)S(1)}, u32[]{:S(2)}, u32[]{:S(2)}) %collective-permute-start.3) | collective-permute-done | bytes 102432 | tf_op jit(solution)/shard_map/ppermute | solution.py:335
  108.0 18.1 %all_to_all.20 = f32[4,40,128]{2,1,0:T(8,128)S(1)} all-to-all(f32[4,40,128]{2,1,0:T(8,128)S(1)} %broadcast_in_dim.6), channel_id=1, replica_groups={{0,1,2,3},{4,5,6,7},{8,9,10,11},{12,13,14,15},{16,17,18,19},{20,21,22,2..., dimensions={0} | all-to-all | bytes 163840 | tf_op jit(solution)/shard_map/all_to_all | solution.py:339
  126.2 1.3 broadcast_in_dim.7
  127.5 0.0 copy-start.3
  127.5 12.7 %all-to-all-start.3 = ((f32[32,104,128]{2,1,0:T(8,128)}), f32[32,104,128]{2,1,0:T(8,128)S(1)}, u32[]{:S(2)}, u32[]{:S(2)}) async-start(f32[32,104,128]{2,1,0:T(8,128)} %broadcast_in_dim.7), calls=%async_computation.3 | async-start | bytes 3407872 | tf_op jit(solution)/shard_map/all_to_all | solution.py:339
  140.3 4.6 %collective-permute-start.8 = (f32[160,512]{1,0:T(8,128)S(1)}, f32[160,512]{1,0:T(8,128)S(1)}, u32[]{:S(2)}, u32[]{:S(2)}) collective-permute-start(f32[160,512]{1,0:T(8,128)S(1)} %pad_maximum_fusion.refs_0_), channel_id=1, source_target_pairs={{0,15},{1,0},{2,1},{3,2},{4,3},{5,4},{6,5},{7,6},{8,7},{9,8},{10,9... | collective-permute-start | bytes 983048 | tf_op jit(solution)/shard_map/ppermute | solution.py:335
  144.9 1.9 collective-permute-start.7
  146.8 1.9 collective-permute-start.6
  148.7 15.0 %all-to-all-done.3.pieces_ref = f32[32,104,128]{2,1,0:T(8,128)S(1)} async-done(((f32[32,104,128]{2,1,0:T(8,128)}), f32[32,104,128]{2,1,0:T(8,128)S(1)}, u32[]{:S(2)}, u32[]{:S(2)}) %all-to-all-start.3) | async-done | bytes 1703968 | tf_op jit(solution)/shard_map/all_to_all | solution.py:339
  163.7 0.0 copy-done.3
  163.7 35.3 %shard_map.57 = (bf16[448,512]{1,0:T(8,128)(2,1)S(1)}, bf16[448,512]{1,0:T(8,128)(2,1)S(1)}) custom-call(f32[32,104,128]{2,1,0:T(8,128)S(1)} %all-to-all-done.3.pieces_ref, bf16[2,448,256]{2,1,0:T(8,128)(2,1)S(1)} %bitcast.7), custom_call_target="tpu_custom_call" | custom-call | flops 5368709120 | bytes 4194304 | tf_op jit(solution)/shard_map/pallas_call | solution.py:170
  199.1 0.0 collective-permute-done.8.refs_3_
  199.1 0.0 collective-permute-done.7.refs_2_
  199.1 0.0 collective-permute-done.6.refs_1_
  199.1 2.3 %shard_map.58 = bf16[448,576]{1,0:T(8,128)(2,1)} custom-call(f32[160,512]{1,0:T(8,128)S(1)} %pad_maximum_fusion.refs_0_, f32[160,512]{1,0:T(8,128)S(1)} %collective-permute-done.6.refs_1_, f32[160,512]{1,0:T(8,128)S(1)} %collective-permute-done.7.refs_2_, f32[160,512]{1,0:T(8,128)S(1)} %collective-permute-done.8.refs_3_, ...), custom_call_target="tpu_custom_call" | custom-call | tf_op jit(solution)/shard_map/pallas_call | solution.py:323
  (10 shorter events, 0.1 us)
Async XLA Ops:
  0.0 1.3 copy-start
  1.3 1.1 copy-start.1
  2.3 0.7 copy-start.2
  8.4 12.2 %collective-permute-start = (f32[16,56,512]{2,1,0:T(8,128)S(1)}, f32[16,56,512]{2,1,0:T(8,128)S(1)}, u32[]{:S(2)}, u32[]{:S(2)}) collective-permute-start(f32[16,56,512]{2,1,0:T(8,128)S(1)} %get-tuple-element.18), channel_id=1, source_target_pairs={{0,16},{16,0},{32,48},{48,32},{64,80},{80,64},{96,112},{112,96},{1... | collective-permute-start | bytes 5505032 | tf_op jit(solution)/shard_map/ppermute | solution.py:357
  22.3 33.4 %all-to-all-start = ((f32[16,56,512]{2,1,0:T(8,128)}), f32[16,56,512]{2,1,0:T(8,128)S(1)}, u32[]{:S(2)}, u32[]{:S(2)}) async-start(f32[16,56,512]{2,1,0:T(8,128)} %add.12), calls=%async_computation | async-start | bytes 3670016 | tf_op jit(solution)/shard_map/all_to_all | solution.py:339
  26.0 0.7 collective-permute-start.1
  57.2 19.1 %all-to-all-start.1 = ((f32[32,40,128]{2,1,0:T(8,128)}), f32[32,40,128]{2,1,0:T(8,128)S(1)}, u32[]{:S(2)}, u32[]{:S(2)}) async-start(f32[32,40,128]{2,1,0:T(8,128)} %bitcast.2), calls=%async_computation.1 | async-start | bytes 1310720 | tf_op jit(solution)/shard_map/all_to_all | solution.py:339
  63.4 13.0 %collective-permute-start.2 = (f32[40,512]{1,0:T(8,128)S(1)}, f32[40,512]{1,0:T(8,128)S(1)}, u32[]{:S(2)}, u32[]{:S(2)}) collective-permute-start(f32[40,512]{1,0:T(8,128)S(1)} %get-tuple-element.20), channel_id=1, source_target_pairs={{0,0},{16,16},{1,32},{17,48},{2,64},{18,80},{3,96},{19,112},{4,128... | collective-permute-start | bytes 245768 | tf_op jit(solution)/shard_map/ppermute | solution.py:361
  76.4 29.4 %collective-permute-start.5 = (f32[40,640]{1,0:T(8,128)S(1)}, f32[40,640]{1,0:T(8,128)S(1)}, u32[]{:S(2)}, u32[]{:S(2)}) collective-permute-start(f32[40,640]{1,0:T(8,128)S(1)} %pad_maximum_fusion.1), channel_id=1, source_target_pairs={{0,12},{1,13},{2,14},{3,15},{4,0},{5,1},{6,2},{7,3},{8,4},{9,5},{1... | collective-permute-start | bytes 307208 | tf_op jit(solution)/shard_map/ppermute | solution.py:335
  88.2 17.6 %collective-permute-start.4 = (f32[40,640]{1,0:T(8,128)S(1)}, f32[40,640]{1,0:T(8,128)S(1)}, u32[]{:S(2)}, u32[]{:S(2)}) collective-permute-start(f32[40,640]{1,0:T(8,128)S(1)} %pad_maximum_fusion.1), channel_id=1, source_target_pairs={{0,8},{1,9},{2,10},{3,11},{4,12},{5,13},{6,14},{7,15},{8,0},{9,1},... | collective-permute-start | bytes 307208 | tf_op jit(solution)/shard_map/ppermute | solution.py:335
  98.5 9.6 %collective-permute-start.3 = (f32[40,640]{1,0:T(8,128)S(1)}, f32[40,640]{1,0:T(8,128)S(1)}, u32[]{:S(2)}, u32[]{:S(2)}) collective-permute-start(f32[40,640]{1,0:T(8,128)S(1)} %pad_maximum_fusion.1), channel_id=1, source_target_pairs={{0,4},{1,5},{2,6},{3,7},{4,8},{5,9},{6,10},{7,11},{8,12},{9,13},{1... | collective-permute-start | bytes 307208 | tf_op jit(solution)/shard_map/ppermute | solution.py:335
  127.5 36.2 %copy-start.3 = (bf16[2,256,448]{1,2,0:T(8,128)(2,1)S(1)}, bf16[2,256,448]{1,2,0:T(8,128)(2,1)}, u32[]{:S(2)}) copy-start(bf16[2,256,448]{1,2,0:T(8,128)(2,1)} %param.9) | copy-start | bytes 1376260
  127.5 36.2 %all-to-all-start.3 = ((f32[32,104,128]{2,1,0:T(8,128)}), f32[32,104,128]{2,1,0:T(8,128)S(1)}, u32[]{:S(2)}, u32[]{:S(2)}) async-start(f32[32,104,128]{2,1,0:T(8,128)} %broadcast_in_dim.7), calls=%async_computation.3 | async-start | bytes 3407872 | tf_op jit(solution)/shard_map/all_to_all | solution.py:339
  140.3 58.8 %collective-permute-start.8 = (f32[160,512]{1,0:T(8,128)S(1)}, f32[160,512]{1,0:T(8,128)S(1)}, u32[]{:S(2)}, u32[]{:S(2)}) collective-permute-start(f32[160,512]{1,0:T(8,128)S(1)} %pad_maximum_fusion.refs_0_), channel_id=1, source_target_pairs={{0,15},{1,0},{2,1},{3,2},{4,3},{5,4},{6,5},{7,6},{8,7},{9,8},{10,9... | collective-permute-start | bytes 983048 | tf_op jit(solution)/shard_map/ppermute | solution.py:335
  144.9 54.2 %collective-permute-start.7 = (f32[160,512]{1,0:T(8,128)S(1)}, f32[160,512]{1,0:T(8,128)S(1)}, u32[]{:S(2)}, u32[]{:S(2)}) collective-permute-start(f32[160,512]{1,0:T(8,128)S(1)} %pad_maximum_fusion.refs_0_), channel_id=1, source_target_pairs={{0,2},{1,3},{2,4},{3,5},{4,6},{5,7},{6,8},{7,9},{8,10},{9,11},{10,... | collective-permute-start | bytes 983048 | tf_op jit(solution)/shard_map/ppermute | solution.py:335
  146.8 52.3 %collective-permute-start.6 = (f32[160,512]{1,0:T(8,128)S(1)}, f32[160,512]{1,0:T(8,128)S(1)}, u32[]{:S(2)}, u32[]{:S(2)}) collective-permute-start(f32[160,512]{1,0:T(8,128)S(1)} %pad_maximum_fusion.refs_0_), channel_id=1, source_target_pairs={{0,1},{1,2},{2,3},{3,4},{4,5},{5,6},{6,7},{7,8},{8,9},{9,10},{10,1... | collective-permute-start | bytes 983048 | tf_op jit(solution)/shard_map/ppermute | solution.py:335

commit v8 on v7

--- a/solution.py
+++ b/solution.py
@@ -11,8 +11,8 @@
 LANES = 128
 HIGHEST = lax.Precision.HIGHEST
 VMEM_LIMIT = 48 * 2**20
-TALL, SHORT, PADDED = 40, 32, 48
-V_SHORT = 24
+PADDED = 48
+PAIRS = 8
 STRIDE = 4
 SHIFTS = (0, 1, 2, -1)
 
@@ -69,16 +69,14 @@
         per_batch = target_ref.shape[2]
         for b in range(target_ref.shape[0]):
             r_ref[:, b * per_batch:(b + 1) * per_batch] = target_ref[b].astype(jnp.float32)
-        tile = (pieces_ref.shape[1] - share) * LANES // n
+        half = n // 2 // LANES
+        tall = (pieces_ref.shape[1] - share) // half
         for r in range(pieces_ref.shape[0]):
             k, h = r // 2, r % 2
-            begin = k // 2 * (2 * tile + V_SHORT) + k % 2 * 2 * tile
-            for q in range(n // LANES):
-                row = begin + q // 2 * tile
-                tall = tile if q < 2 or k % 2 == 0 else V_SHORT - tile
-                lane = h * (n // 2) + q % 2 * LANES
-                at = share + q * tile
-                r_ref[row:row + tall, lane:lane + LANES] -= pieces_ref[r, at:at + tall, :]
+            for q in range(half):
+                lane = (h * half + q) * LANES
+                at = share + q * tall
+                r_ref[k * tall:(k + 1) * tall, lane:lane + LANES] -= pieces_ref[r, at:at + tall, :]
 
     def more(carry):
         step, before, worst, limit = carry
@@ -192,14 +190,11 @@
     return lax.dot_general(a, b, (((0,), (0,)), ((), ())), preferred_element_type=jnp.float32)
 
 
-def piece_start(index):
-    return index // 2 * (TALL + SHORT) + index % 2 * TALL
-
-
-def front_kernel(index_ref, table_ref, cov_ref, weight_ref, other_ref, mine_ref, slice_ref, part_ref, value_ref):
+def front_kernel(index_ref, table_ref, cov_hbm, weight_ref, other_ref, mine_ref, slice_ref, cov_ref, part_ref, value_ref, sem):
+    load = pltpu.make_async_copy(cov_hbm, cov_ref, sem)
+    load.start()
     here, n = table_ref.shape[0], slice_ref.shape[1]
     chips = mine_ref.shape[0]
-    share = mine_ref.shape[1] - TALL
     core, col = lax.axis_index("row") % 2, lax.axis_index("col")
     batches, per_batch = index_ref.shape
     spot = lax.broadcasted_iota(jnp.int32, (table_ref.shape[1], per_batch), 0)
@@ -210,44 +205,46 @@
     padded = slice_ref.shape[0]
     slot = lax.broadcasted_iota(jnp.int32, (padded, here), 0)
     spot = lax.broadcasted_iota(jnp.int32, (padded, here), 1)
-    odd = lax.rem(col, 2)
-    first = lax.div(col, 2) * (TALL + SHORT) + odd * TALL
-    taken = jnp.logical_and(slot + first == spot, slot < TALL - odd * (TALL - SHORT))
+    tall = here // chips
+    taken = jnp.logical_and(slot + col * tall == spot, slot < tall)
     taken = jnp.where(taken, 1.0, 0.0).astype(jnp.bfloat16)
     slice_ref[...] = dot16(taken, keys).astype(jnp.bfloat16)
-    value_ref[...] = dot16(weight_ref[...], keys)
+    value = dot16(weight_ref[...], keys)
+    load.wait()
     high, low = split(cov_ref[...])
-    part_ref[...] = contract_first(high, keys) + contract_first(low, keys)
+    part = contract_first(high, keys) + contract_first(low, keys)
+    for h in range(2):
+        value_ref[h] = value[:, h * (n // 2):(h + 1) * (n // 2)]
+        part_ref[h] = part[h * here:(h + 1) * here]
+    wide = weight_ref.shape[0] // chips
     for which, ref in ((core, mine_ref), (1 - core, other_ref)):
-        lanes = pl.ds(pl.multiple_of(which * (n // 2), LANES), n // 2)
         for j in range(chips):
-            begin = pl.multiple_of(which * here + piece_start(j), 8)
-            tall = TALL if j % 2 == 0 else SHORT
-            ref[j, :tall, :] = part_ref[pl.ds(begin, tall), :]
-            if tall < TALL:
-                ref[j, tall:TALL, :] = jnp.zeros((TALL - tall, n), jnp.float32)
-            at = j // 2 * (2 * share + V_SHORT) + j % 2 * 2 * share
-            second = share if j % 2 == 0 else V_SHORT - share
-            ref[j, TALL:, :n // 2] = value_ref[at:at + share, lanes]
-            ref[j, TALL:TALL + second, n // 2:] = value_ref[at + share:at + share + second, lanes]
-            if second < share:
-                ref[j, TALL + second:, n // 2:] = jnp.zeros((share - second, n // 2), jnp.float32)
+            at = 0
+            for q in range(n // LANES):
+                ref[j, at:at + tall, :] = part_ref[which, j * tall:(j + 1) * tall, q * LANES:(q + 1) * LANES]
+                at += tall
+            for q in range(n // 2 // LANES):
+                ref[j, at:at + wide, :] = value_ref[which, j * wide:(j + 1) * wide, q * LANES:(q + 1) * LANES]
+                at += wide
 
 
 def front(index, table, cov, weight, chips):
     n = index.size
-    width = weight.shape[0]
-    share = width // (2 * chips) + 2
-    payload = jax.ShapeDtypeStruct((chips, TALL + share, n), jnp.float32)
+    here, width = table.shape[0], weight.shape[0]
+    blocks = n // LANES
+    rows = here // chips * blocks + width // chips * blocks // 2
+    payload = jax.ShapeDtypeStruct((chips, rows, LANES), jnp.float32)
     vmem = pl.BlockSpec(memory_space=pltpu.VMEM)
     return pl.pallas_call(
         front_kernel,
         out_shape=(payload, payload, jax.ShapeDtypeStruct((PADDED, n), jnp.bfloat16)),
-        in_specs=[vmem] * 4,
+        in_specs=[vmem, vmem, pl.BlockSpec(memory_space=pltpu.HBM), vmem],
         out_specs=(vmem, vmem, vmem),
         scratch_shapes=[
-            pltpu.VMEM((cov.shape[1], n), jnp.float32),
-            pltpu.VMEM((width, n), jnp.float32),
+            pltpu.VMEM(cov.shape, cov.dtype),
+            pltpu.VMEM((2, here, n), jnp.float32),
+            pltpu.VMEM((2, width, n // 2), jnp.float32),
+            pltpu.SemaphoreType.DMA,
         ],
         compiler_params=pltpu.CompilerParams(vmem_limit_bytes=VMEM_LIMIT),
     )(index, table, cov, weight)
@@ -257,17 +254,17 @@
     total = received_ref[0]
     for j in range(1, received_ref.shape[0]):
         total = total + received_ref[j]
-    panel = total[:TALL]
-    panel_ref[...] = panel
-    tile = total.shape[0] - TALL
-    for q in range(total.shape[1] // LANES):
-        value_ref[q * tile:(q + 1) * tile, :] = total[TALL:, q * LANES:(q + 1) * LANES]
-    n = panel.shape[1]
-    padded = jnp.concatenate([panel, jnp.zeros((PADDED - TALL, n), jnp.float32)], axis=0)
+    rows = panel_ref.shape[0]
+    panel_ref[...] = total[:rows]
+    value_ref[...] = total[rows:]
+    keys = key_ref[...]
+    n = keys.shape[1]
+    tall = rows * LANES // n
+    panel = jnp.concatenate([total[q * tall:(q + 1) * tall] for q in range(n // LANES)], axis=1)
+    padded = jnp.concatenate([panel, jnp.zeros((PADDED - tall, n), jnp.float32)], axis=0)
     high = padded.astype(jnp.bfloat16)
     rest = padded - high.astype(jnp.float32)
     middle, low = split(rest)
-    keys = key_ref[...]
     gram = contract_first(keys, high) + (contract_first(keys, middle) + contract_first(keys, low))
     place = 0
     for i in range(n // LANES):
@@ -278,15 +275,14 @@
             place += 1
 
 
-def gram_share(received, key_piece):
-    n = received.shape[2]
-    blocks = n // LANES
+def gram_share(received, key_piece, rows):
+    blocks = key_piece.shape[1] // LANES
     vmem = pl.BlockSpec(memory_space=pltpu.VMEM)
     return pl.pallas_call(
         gram_kernel,
         out_shape=(
-            jax.ShapeDtypeStruct((TALL, n), jnp.float32),
-            jax.ShapeDtypeStruct(((received.shape[1] - TALL) * blocks, LANES), jnp.float32),
+            jax.ShapeDtypeStruct((rows, LANES), jnp.float32),
+            jax.ShapeDtypeStruct((received.shape[1] - rows, LANES), jnp.float32),
             jax.ShapeDtypeStruct((blocks * (blocks + 1) // 2 * LANES, LANES), jnp.float32),
         ),
         in_specs=[vmem] * 2,
@@ -298,18 +294,19 @@
 def change_kernel(*refs):
     *bundle_refs, high_ref, low_ref, out_ref, panel_ref = refs
     cols = len(bundle_refs) * STRIDE
+    blocks, tall = high_ref.shape[1] // LANES, out_ref.shape[1] // cols
     for shift, ref in zip(SHIFTS, bundle_refs):
         for t in range(cols // STRIDE):
             piece = lax.rem(lax.axis_index("col") - shift - STRIDE * t + 2 * cols, cols)
-            odd = lax.rem(piece, 2)
-            begin = pl.multiple_of(lax.div(piece, 2) * (TALL + SHORT) + odd * TALL, 8)
-            panel_ref[pl.ds(begin, SHORT), :] = ref[t * TALL:t * TALL + SHORT, :]
-
-            @pl.when(odd == 0)
-            def _(ref=ref, t=t, begin=begin):
-                panel_ref[pl.ds(begin + SHORT, TALL - SHORT), :] = ref[t * TALL + SHORT:(t + 1) * TALL, :]
-
-    high, low = split(panel_ref[...])
+            for parity in range(2):
+
+                @pl.when(lax.rem(piece, 2) == parity)
+                def _(ref=ref, t=t, pair=lax.div(piece, 2), parity=parity):
+                    for q in range(blocks):
+                        at = (t * blocks + q) * tall
+                        panel_ref[pair, parity * tall:(parity + 1) * tall, q * LANES:(q + 1) * LANES] = ref[at:at + tall, :]
+
+    high, low = split(panel_ref[...].reshape(out_ref.shape[1], blocks * LANES))
     last = (((1,), (1,)), ((), ()))
     out = lax.dot_general(high_ref[...], high, last, preferred_element_type=jnp.float32)
     out += lax.dot_general(low_ref[...], high, last, preferred_element_type=jnp.float32)
@@ -325,7 +322,7 @@
         out_shape=jax.ShapeDtypeStruct((width, here), jnp.bfloat16),
         in_specs=[vmem] * (len(bundles) + 2),
         out_specs=vmem,
-        scratch_shapes=[pltpu.VMEM((here, n), jnp.float32)],
+        scratch_shapes=[pltpu.VMEM((PAIRS, here // PAIRS, n), jnp.float32)],
         compiler_params=pltpu.CompilerParams(vmem_limit_bytes=VMEM_LIMIT),
     )(*bundles, *solved)
 
@@ -356,17 +353,19 @@
     other, mine, key_slice = front(edit_index, key_table.T, inverse_cov, weight.T, chips)
     half_sum = mine + lax.ppermute(other, "row", other_core)
     key_piece = lax.ppermute(key_slice, ("row", "col"), turned)
-    panel_piece, value_piece, packed = gram_share(swapped(half_sum, "row", same_core), key_piece)
+    panel_piece, value_piece, packed = gram_share(
+        swapped(half_sum, "row", same_core), key_piece, here // chips * (n // LANES)
+    )
 
     own = lax.ppermute(panel_piece, ("row", "col"), turned)
     share = packed.shape[0] // rows
     part = jnp.sum(swapped(packed.reshape(rows, share, LANES), "row"), axis=0)
     neighbours = [[STRIDE * g + i for i in range(STRIDE)] for g in range(cols // STRIDE)]
-    joined = jnp.concatenate([own, part], axis=1)
+    joined = jnp.concatenate([own, part], axis=0)
     joined = [joined] + [moved(joined, "col", STRIDE * t) for t in range(1, cols // STRIDE)]
     joined = lax.optimization_barrier(tuple(joined))
-    far = [item[:, :n] for item in joined]
-    part = sum(item[:, n:] for item in joined)
+    far = [item[:-share] for item in joined]
+    part = sum(item[-share:] for item in joined)
     part = jnp.sum(swapped(copies(part, STRIDE), "col", neighbours), axis=0)
     piece = jnp.concatenate([part, value_piece], axis=0)
     pieces = swapped(copies(piece, rows), "row")

time: 202 us -> 197 us (0.975)
  waiting for transfers between devices: 61.9 us -> 59.6 us
    ppermute x6, starting transfers between devices: 37.7 us -> 35.6 us  [moved(): lax.ppermute(value, axis, [(i, (i + shift) % size) for i in range(size)])]
where the time goes in v8:
time: 197 us; the launch traced here: 196 us
  starting transfers between devices  69.3 us (35%)
  waiting for transfers between devices  59.6 us (30%)
  Pallas kernels  44.6 us (23%)
  blocking collectives  16.7 us (8%)
  local copies, waits for them, and re-layouts  4.4 us (2%)
    all_to_all x3, waiting for transfers between devices, swapped(): lax.all_to_all(value, axis, 0, 0, axis_index_groups=groups, tiled=True)  54.2 us
    ppermute x6, starting transfers between devices, moved(): lax.ppermute(value, axis, [(i, (i + shift) % size) for i in range(size)])  35.6 us
    pallas_call x1, Pallas kernels, solve(): pl.pallas_call(solve_kernel, out_shape=(out, out), in_specs=[vmem, pl.Blo...  35.5 us
    all_to_all x3, starting transfers between devices, swapped(): lax.all_to_all(value, axis, 0, 0, axis_index_groups=groups, tiled=True)  23.6 us
    all_to_all x1, blocking collectives, swapped(): lax.all_to_all(value, axis, 0, 0, axis_index_groups=groups, tiled=True)  16.7 us
    ppermute x1, starting transfers between devices, shards(): half_sum = mine + lax.ppermute(other, 'row', other_core)  8.79 us
    pallas_call x1, Pallas kernels, front(): pl.pallas_call(front_kernel, out_shape=(payload, payload, jax.ShapeDtypeS...  5.33 us
  transfers between devices with their start and end apart: 12, of which 5 were waited for; matrix products, arithmetic and copies ran while one was open for 0% of the time, Pallas kernels for 18%

profile of v8, /device:TPU:1, one launch (start us, length us, event | category | flops | bytes accessed | tf_op | source)
XLA Modules:
  0.0 196.3 jit_solution(17483431280622710489)
XLA Ops:
  0.0 0.0 copy-start
  0.0 1.3 copy-done
  1.3 0.0 copy-start.1
  1.3 1.1 copy-done.1
  2.3 0.0 copy-start.2
  2.3 0.7 copy-done.2
  3.0 5.3 %shard_map.55 = (f32[16,200,128]{2,1,0:T(8,128)S(1)}, f32[16,200,128]{2,1,0:T(8,128)S(1)}, bf16[48,512]{1,0:T(8,128)(2,1)S(1)}) custom-call(s32[2,256]{1,0:T(2,128)S(1)} %copy-done.2, bf16[576,1024]{1,0:T(8,128)(2,1)S(1)} %bitcast.5, f32[576,1152]{1,0:T(8,128)} %cov_hbm.1, bf16[448,576]{1,0:T(8,128)(2,1)S(1)} %bitcast.6), custom_call_target="tpu_custom_call" | custom-call | tf_op jit(solution)/shard_map/pallas_call | solution.py:238
  8.3 8.8 %collective-permute-start = (f32[16,200,128]{2,1,0:T(8,128)S(1)}, f32[16,200,128]{2,1,0:T(8,128)S(1)}, u32[]{:S(2)}, u32[]{:S(2)}) collective-permute-start(f32[16,200,128]{2,1,0:T(8,128)S(1)} %get-tuple-element.18), channel_id=1, source_target_pairs={{0,16},{16,0},{32,48},{48,32},{64,80},{80,64},{96,112},{112,96},{1... | collective-permute-start | bytes 4915208 | tf_op jit(solution)/shard_map/ppermute | solution.py:354
  17.1 3.1 %collective-permute-done = f32[16,200,128]{2,1,0:T(8,128)S(1)} collective-permute-done((f32[16,200,128]{2,1,0:T(8,128)S(1)}, f32[16,200,128]{2,1,0:T(8,128)S(1)}, u32[]{:S(2)}, u32[]{:S(2)}) %collective-permute-start) | collective-permute-done | bytes 1638432 | tf_op jit(solution)/shard_map/ppermute | solution.py:354
  20.3 1.4 add.12
  21.6 3.7 %all-to-all-start = ((f32[16,200,128]{2,1,0:T(8,128)}), f32[16,200,128]{2,1,0:T(8,128)S(1)}, u32[]{:S(2)}, u32[]{:S(2)}) async-start(f32[16,200,128]{2,1,0:T(8,128)} %add.12), calls=%async_computation | async-start | bytes 3276800 | tf_op jit(solution)/shard_map/all_to_all | solution.py:336
  25.3 0.7 collective-permute-start.1
  26.0 0.0 collective-permute-done.1.key_ref
  26.0 27.6 %all-to-all-done.received_ref = f32[16,200,128]{2,1,0:T(8,128)S(1)} async-done(((f32[16,200,128]{2,1,0:T(8,128)}), f32[16,200,128]{2,1,0:T(8,128)S(1)}, u32[]{:S(2)}, u32[]{:S(2)}) %all-to-all-start) | async-done | bytes 1638432 | tf_op jit(solution)/shard_map/all_to_all | solution.py:336
  53.6 1.5 shard_map.56
  55.1 6.2 %all-to-all-start.1 = ((f32[32,40,128]{2,1,0:T(8,128)}), f32[32,40,128]{2,1,0:T(8,128)S(1)}, u32[]{:S(2)}, u32[]{:S(2)}) async-start(f32[32,40,128]{2,1,0:T(8,128)} %bitcast.2), calls=%async_computation.1 | async-start | bytes 1310720 | tf_op jit(solution)/shard_map/all_to_all | solution.py:336
  61.3 0.7 collective-permute-start.2
  62.0 12.2 %all-to-all-done.1 = f32[32,40,128]{2,1,0:T(8,128)S(1)} async-done(((f32[32,40,128]{2,1,0:T(8,128)}), f32[32,40,128]{2,1,0:T(8,128)S(1)}, u32[]{:S(2)}, u32[]{:S(2)}) %all-to-all-start.1) | async-done | bytes 655392 | tf_op jit(solution)/shard_map/all_to_all | solution.py:336
  74.2 0.1 reduce_sum.18
  74.3 0.0 collective-permute-done.2
  74.3 10.9 %collective-permute-start.5 = (f32[184,128]{1,0:T(8,128)S(1)}, f32[184,128]{1,0:T(8,128)S(1)}, u32[]{:S(2)}, u32[]{:S(2)}) collective-permute-start(f32[184,128]{1,0:T(8,128)S(1)} %pad_maximum_fusion.1), channel_id=1, source_target_pairs={{0,12},{1,13},{2,14},{3,15},{4,0},{5,1},{6,2},{7,3},{8,4},{9,5},{1... | collective-permute-start | bytes 282632 | tf_op jit(solution)/shard_map/ppermute | solution.py:332
  85.2 9.7 %collective-permute-start.4 = (f32[184,128]{1,0:T(8,128)S(1)}, f32[184,128]{1,0:T(8,128)S(1)}, u32[]{:S(2)}, u32[]{:S(2)}) collective-permute-start(f32[184,128]{1,0:T(8,128)S(1)} %pad_maximum_fusion.1), channel_id=1, source_target_pairs={{0,8},{1,9},{2,10},{3,11},{4,12},{5,13},{6,14},{7,15},{8,0},{9,1},... | collective-permute-start | bytes 282632 | tf_op jit(solution)/shard_map/ppermute | solution.py:332
  94.9 7.3 %collective-permute-start.3 = (f32[184,128]{1,0:T(8,128)S(1)}, f32[184,128]{1,0:T(8,128)S(1)}, u32[]{:S(2)}, u32[]{:S(2)}) collective-permute-start(f32[184,128]{1,0:T(8,128)S(1)} %pad_maximum_fusion.1), channel_id=1, source_target_pairs={{0,4},{1,5},{2,6},{3,7},{4,8},{5,9},{6,10},{7,11},{8,12},{9,13},{1... | collective-permute-start | bytes 282632 | tf_op jit(solution)/shard_map/ppermute | solution.py:332
  102.2 0.0 collective-permute-done.5
  102.2 0.0 collective-permute-done.4
  102.2 2.2 %collective-permute-done.3 = f32[184,128]{1,0:T(8,128)S(1)} collective-permute-done((f32[184,128]{1,0:T(8,128)S(1)}, f32[184,128]{1,0:T(8,128)S(1)}, u32[]{:S(2)}, u32[]{:S(2)}) %collective-permute-start.3) | collective-permute-done | bytes 94240 | tf_op jit(solution)/shard_map/ppermute | solution.py:332
  104.5 16.7 %all_to_all.20 = f32[4,40,128]{2,1,0:T(8,128)S(1)} all-to-all(f32[4,40,128]{2,1,0:T(8,128)S(1)} %broadcast_in_dim.6), channel_id=1, replica_groups={{0,1,2,3},{4,5,6,7},{8,9,10,11},{12,13,14,15},{16,17,18,19},{20,21,22,2..., dimensions={0} | all-to-all | bytes 163840 | tf_op jit(solution)/shard_map/all_to_all | solution.py:336
  121.2 1.4 broadcast_in_dim.7
  122.6 0.0 copy-start.3
  122.6 13.7 %all-to-all-start.3 = ((f32[32,96,128]{2,1,0:T(8,128)}), f32[32,96,128]{2,1,0:T(8,128)S(1)}, u32[]{:S(2)}, u32[]{:S(2)}) async-start(f32[32,96,128]{2,1,0:T(8,128)} %broadcast_in_dim.7), calls=%async_computation.3 | async-start | bytes 3145728 | tf_op jit(solution)/shard_map/all_to_all | solution.py:336
  136.4 3.2 %collective-permute-start.8 = (f32[576,128]{1,0:T(8,128)S(1)}, f32[576,128]{1,0:T(8,128)S(1)}, u32[]{:S(2)}, u32[]{:S(2)}) collective-permute-start(f32[576,128]{1,0:T(8,128)S(1)} %pad_maximum_fusion.refs_0_), channel_id=1, source_target_pairs={{0,15},{1,0},{2,1},{3,2},{4,3},{5,4},{6,5},{7,6},{8,7},{9,8},{10,9... | collective-permute-start | bytes 884744 | tf_op jit(solution)/shard_map/ppermute | solution.py:332
  139.6 2.5 %collective-permute-start.7 = (f32[576,128]{1,0:T(8,128)S(1)}, f32[576,128]{1,0:T(8,128)S(1)}, u32[]{:S(2)}, u32[]{:S(2)}) collective-permute-start(f32[576,128]{1,0:T(8,128)S(1)} %pad_maximum_fusion.refs_0_), channel_id=1, source_target_pairs={{0,2},{1,3},{2,4},{3,5},{4,6},{5,7},{6,8},{7,9},{8,10},{9,11},{10,... | collective-permute-start | bytes 884744 | tf_op jit(solution)/shard_map/ppermute | solution.py:332
  142.1 2.0 %collective-permute-start.6 = (f32[576,128]{1,0:T(8,128)S(1)}, f32[576,128]{1,0:T(8,128)S(1)}, u32[]{:S(2)}, u32[]{:S(2)}) collective-permute-start(f32[576,128]{1,0:T(8,128)S(1)} %pad_maximum_fusion.refs_0_), channel_id=1, source_target_pairs={{0,1},{1,2},{2,3},{3,4},{4,5},{5,6},{6,7},{7,8},{8,9},{9,10},{10,1... | collective-permute-start | bytes 884744 | tf_op jit(solution)/shard_map/ppermute | solution.py:332
  144.1 14.4 %all-to-all-done.3.pieces_ref = f32[32,96,128]{2,1,0:T(8,128)S(1)} async-done(((f32[32,96,128]{2,1,0:T(8,128)}), f32[32,96,128]{2,1,0:T(8,128)S(1)}, u32[]{:S(2)}, u32[]{:S(2)}) %all-to-all-start.3) | async-done | bytes 1572896 | tf_op jit(solution)/shard_map/all_to_all | solution.py:336
  158.5 0.0 copy-done.3
  158.5 35.5 %shard_map.57 = (bf16[448,512]{1,0:T(8,128)(2,1)S(1)}, bf16[448,512]{1,0:T(8,128)(2,1)S(1)}) custom-call(f32[32,96,128]{2,1,0:T(8,128)S(1)} %all-to-all-done.3.pieces_ref, bf16[2,448,256]{2,1,0:T(8,128)(2,1)S(1)} %bitcast.7), custom_call_target="tpu_custom_call" | custom-call | flops 5368709120 | bytes 4194304 | tf_op jit(solution)/shard_map/pallas_call | solution.py:168
  194.0 0.0 collective-permute-done.8.refs_3_
  194.0 0.0 collective-permute-done.7.refs_2_
  194.0 0.0 collective-permute-done.6.refs_1_
  194.0 2.3 %shard_map.58 = bf16[448,576]{1,0:T(8,128)(2,1)} custom-call(f32[576,128]{1,0:T(8,128)S(1)} %pad_maximum_fusion.refs_0_, f32[576,128]{1,0:T(8,128)S(1)} %collective-permute-done.6.refs_1_, f32[576,128]{1,0:T(8,128)S(1)} %collective-permute-done.7.refs_2_, f32[576,128]{1,0:T(8,128)S(1)} %collective-permute-done.8.refs_3_, ...), custom_call_target="tpu_custom_call" | custom-call | tf_op jit(solution)/shard_map/pallas_call | solution.py:320
  (10 shorter events, 0.1 us)
Async XLA Ops:
  0.0 1.3 copy-start
  1.3 1.1 copy-start.1
  2.3 0.7 copy-start.2
  8.3 11.9 %collective-permute-start = (f32[16,200,128]{2,1,0:T(8,128)S(1)}, f32[16,200,128]{2,1,0:T(8,128)S(1)}, u32[]{:S(2)}, u32[]{:S(2)}) collective-permute-start(f32[16,200,128]{2,1,0:T(8,128)S(1)} %get-tuple-element.18), channel_id=1, source_target_pairs={{0,16},{16,0},{32,48},{48,32},{64,80},{80,64},{96,112},{112,96},{1... | collective-permute-start | bytes 4915208 | tf_op jit(solution)/shard_map/ppermute | solution.py:354
  21.6 32.0 %all-to-all-start = ((f32[16,200,128]{2,1,0:T(8,128)}), f32[16,200,128]{2,1,0:T(8,128)S(1)}, u32[]{:S(2)}, u32[]{:S(2)}) async-start(f32[16,200,128]{2,1,0:T(8,128)} %add.12), calls=%async_computation | async-start | bytes 3276800 | tf_op jit(solution)/shard_map/all_to_all | solution.py:336
  25.3 0.7 collective-permute-start.1
  55.1 19.1 %all-to-all-start.1 = ((f32[32,40,128]{2,1,0:T(8,128)}), f32[32,40,128]{2,1,0:T(8,128)S(1)}, u32[]{:S(2)}, u32[]{:S(2)}) async-start(f32[32,40,128]{2,1,0:T(8,128)} %bitcast.2), calls=%async_computation.1 | async-start | bytes 1310720 | tf_op jit(solution)/shard_map/all_to_all | solution.py:336
  61.3 13.0 %collective-permute-start.2 = (f32[144,128]{1,0:T(8,128)S(1)}, f32[144,128]{1,0:T(8,128)S(1)}, u32[]{:S(2)}, u32[]{:S(2)}) collective-permute-start(f32[144,128]{1,0:T(8,128)S(1)} %get-tuple-element.20), channel_id=1, source_target_pairs={{0,0},{16,16},{1,32},{17,48},{2,64},{18,80},{3,96},{19,112},{4,128... | collective-permute-start | bytes 221192 | tf_op jit(solution)/shard_map/ppermute | solution.py:360
  74.3 27.9 %collective-permute-start.5 = (f32[184,128]{1,0:T(8,128)S(1)}, f32[184,128]{1,0:T(8,128)S(1)}, u32[]{:S(2)}, u32[]{:S(2)}) collective-permute-start(f32[184,128]{1,0:T(8,128)S(1)} %pad_maximum_fusion.1), channel_id=1, source_target_pairs={{0,12},{1,13},{2,14},{3,15},{4,0},{5,1},{6,2},{7,3},{8,4},{9,5},{1... | collective-permute-start | bytes 282632 | tf_op jit(solution)/shard_map/ppermute | solution.py:332
  85.2 17.0 %collective-permute-start.4 = (f32[184,128]{1,0:T(8,128)S(1)}, f32[184,128]{1,0:T(8,128)S(1)}, u32[]{:S(2)}, u32[]{:S(2)}) collective-permute-start(f32[184,128]{1,0:T(8,128)S(1)} %pad_maximum_fusion.1), channel_id=1, source_target_pairs={{0,8},{1,9},{2,10},{3,11},{4,12},{5,13},{6,14},{7,15},{8,0},{9,1},... | collective-permute-start | bytes 282632 | tf_op jit(solution)/shard_map/ppermute | solution.py:332
  94.9 9.5 %collective-permute-start.3 = (f32[184,128]{1,0:T(8,128)S(1)}, f32[184,128]{1,0:T(8,128)S(1)}, u32[]{:S(2)}, u32[]{:S(2)}) collective-permute-start(f32[184,128]{1,0:T(8,128)S(1)} %pad_maximum_fusion.1), channel_id=1, source_target_pairs={{0,4},{1,5},{2,6},{3,7},{4,8},{5,9},{6,10},{7,11},{8,12},{9,13},{1... | collective-permute-start | bytes 282632 | tf_op jit(solution)/shard_map/ppermute | solution.py:332
  122.6 35.9 %copy-start.3 = (bf16[2,256,448]{1,2,0:T(8,128)(2,1)S(1)}, bf16[2,256,448]{1,2,0:T(8,128)(2,1)}, u32[]{:S(2)}) copy-start(bf16[2,256,448]{1,2,0:T(8,128)(2,1)} %param.9) | copy-start | bytes 1376260
  122.6 35.9 %all-to-all-start.3 = ((f32[32,96,128]{2,1,0:T(8,128)}), f32[32,96,128]{2,1,0:T(8,128)S(1)}, u32[]{:S(2)}, u32[]{:S(2)}) async-start(f32[32,96,128]{2,1,0:T(8,128)} %broadcast_in_dim.7), calls=%async_computation.3 | async-start | bytes 3145728 | tf_op jit(solution)/shard_map/all_to_all | solution.py:336
  136.4 57.6 %collective-permute-start.8 = (f32[576,128]{1,0:T(8,128)S(1)}, f32[576,128]{1,0:T(8,128)S(1)}, u32[]{:S(2)}, u32[]{:S(2)}) collective-permute-start(f32[576,128]{1,0:T(8,128)S(1)} %pad_maximum_fusion.refs_0_), channel_id=1, source_target_pairs={{0,15},{1,0},{2,1},{3,2},{4,3},{5,4},{6,5},{7,6},{8,7},{9,8},{10,9... | collective-permute-start | bytes 884744 | tf_op jit(solution)/shard_map/ppermute | solution.py:332
  139.6 54.4 %collective-permute-start.7 = (f32[576,128]{1,0:T(8,128)S(1)}, f32[576,128]{1,0:T(8,128)S(1)}, u32[]{:S(2)}, u32[]{:S(2)}) collective-permute-start(f32[576,128]{1,0:T(8,128)S(1)} %pad_maximum_fusion.refs_0_), channel_id=1, source_target_pairs={{0,2},{1,3},{2,4},{3,5},{4,6},{5,7},{6,8},{7,9},{8,10},{9,11},{10,... | collective-permute-start | bytes 884744 | tf_op jit(solution)/shard_map/ppermute | solution.py:332
  142.1 51.9 %collective-permute-start.6 = (f32[576,128]{1,0:T(8,128)S(1)}, f32[576,128]{1,0:T(8,128)S(1)}, u32[]{:S(2)}, u32[]{:S(2)}) collective-permute-start(f32[576,128]{1,0:T(8,128)S(1)} %pad_maximum_fusion.refs_0_), channel_id=1, source_target_pairs={{0,1},{1,2},{2,3},{3,4},{4,5},{5,6},{6,7},{7,8},{8,9},{9,10},{10,1... | collective-permute-start | bytes 884744 | tf_op jit(solution)/shard_map/ppermute | solution.py:332

commit v9 on v8

--- a/solution.py
+++ b/solution.py
@@ -361,12 +361,13 @@
     share = packed.shape[0] // rows
     part = jnp.sum(swapped(packed.reshape(rows, share, LANES), "row"), axis=0)
     neighbours = [[STRIDE * g + i for i in range(STRIDE)] for g in range(cols // STRIDE)]
+    part, own = lax.optimization_barrier((part, own))
+    part = jnp.sum(swapped(copies(part, STRIDE), "col", neighbours), axis=0)
     joined = jnp.concatenate([own, part], axis=0)
     joined = [joined] + [moved(joined, "col", STRIDE * t) for t in range(1, cols // STRIDE)]
     joined = lax.optimization_barrier(tuple(joined))
     far = [item[:-share] for item in joined]
     part = sum(item[-share:] for item in joined)
-    part = jnp.sum(swapped(copies(part, STRIDE), "col", neighbours), axis=0)
     piece = jnp.concatenate([part, value_piece], axis=0)
     pieces = swapped(copies(piece, rows), "row")
     far = jnp.concatenate(far, axis=0)

time: 197 us -> 196 us (level)
  starting transfers between devices: 69.3 us -> 79 us
  blocking collectives: 16.7 us -> 7.82 us
  waiting for transfers between devices: 59.6 us -> 57.4 us
    ppermute x6, starting transfers between devices: 35.6 us -> 44.7 us  [moved(): lax.ppermute(value, axis, [(i, (i + shift) % size) for i in range(size)])]
    all_to_all x1, blocking collectives: 16.7 us -> 7.82 us  [swapped(): lax.all_to_all(value, axis, 0, 0, axis_index_groups=groups, tiled=True)]
    all_to_all x3, waiting for transfers between devices: 54.2 us -> 51.9 us  [swapped(): lax.all_to_all(value, axis, 0, 0, axis_index_groups=groups, tiled=True)]
where the time goes in v9:
time: 196 us; the launch traced here: 195 us
  starting transfers between devices  79 us (40%)
  waiting for transfers between devices  57.4 us (29%)
  Pallas kernels  44.6 us (23%)
  blocking collectives  7.82 us (4%)
  local copies, waits for them, and re-layouts  4.4 us (2%)
    all_to_all x3, waiting for transfers between devices, swapped(): lax.all_to_all(value, axis, 0, 0, axis_index_groups=groups, tiled=True)  51.9 us
    ppermute x6, starting transfers between devices, moved(): lax.ppermute(value, axis, [(i, (i + shift) % size) for i in range(size)])  44.7 us
    pallas_call x1, Pallas kernels, solve(): pl.pallas_call(solve_kernel, out_shape=(out, out), in_specs=[vmem, pl.Blo...  35.5 us
    all_to_all x3, starting transfers between devices, swapped(): lax.all_to_all(value, axis, 0, 0, axis_index_groups=groups, tiled=True)  24.3 us
    ppermute x1, starting transfers between devices, shards(): half_sum = mine + lax.ppermute(other, 'row', other_core)  8.79 us
    all_to_all x1, blocking collectives, swapped(): lax.all_to_all(value, axis, 0, 0, axis_index_groups=groups, tiled=True)  7.82 us
    pallas_call x1, Pallas kernels, front(): pl.pallas_call(front_kernel, out_shape=(payload, payload, jax.ShapeDtypeS...  5.33 us
  transfers between devices with their start and end apart: 12, of which 5 were waited for; matrix products, arithmetic and copies ran while one was open for 0% of the time, Pallas kernels for 18%

profile of v9, /device:TPU:1, one launch (start us, length us, event | category | flops | bytes accessed | tf_op | source)
XLA Modules:
  0.0 195.0 jit_solution(15907993177903884372)
XLA Ops:
  0.0 0.0 copy-start
  0.0 1.3 copy-done
  1.3 0.0 copy-start.1
  1.3 1.1 copy-done.1
  2.3 0.0 copy-start.2
  2.3 0.7 copy-done.2
  3.0 5.3 %shard_map.55 = (f32[16,200,128]{2,1,0:T(8,128)S(1)}, f32[16,200,128]{2,1,0:T(8,128)S(1)}, bf16[48,512]{1,0:T(8,128)(2,1)S(1)}) custom-call(s32[2,256]{1,0:T(2,128)S(1)} %copy-done.2, bf16[576,1024]{1,0:T(8,128)(2,1)S(1)} %bitcast.5, f32[576,1152]{1,0:T(8,128)} %cov_hbm.1, bf16[448,576]{1,0:T(8,128)(2,1)S(1)} %bitcast.6), custom_call_target="tpu_custom_call" | custom-call | tf_op jit(solution)/shard_map/pallas_call | solution.py:238
  8.3 8.8 %collective-permute-start = (f32[16,200,128]{2,1,0:T(8,128)S(1)}, f32[16,200,128]{2,1,0:T(8,128)S(1)}, u32[]{:S(2)}, u32[]{:S(2)}) collective-permute-start(f32[16,200,128]{2,1,0:T(8,128)S(1)} %get-tuple-element.20), channel_id=1, source_target_pairs={{0,16},{16,0},{32,48},{48,32},{64,80},{80,64},{96,112},{112,96},{1... | collective-permute-start | bytes 4915208 | tf_op jit(solution)/shard_map/ppermute | solution.py:354
  17.1 3.1 %collective-permute-done = f32[16,200,128]{2,1,0:T(8,128)S(1)} collective-permute-done((f32[16,200,128]{2,1,0:T(8,128)S(1)}, f32[16,200,128]{2,1,0:T(8,128)S(1)}, u32[]{:S(2)}, u32[]{:S(2)}) %collective-permute-start) | collective-permute-done | bytes 1638432 | tf_op jit(solution)/shard_map/ppermute | solution.py:354
  20.3 1.4 add.12
  21.6 3.7 %all-to-all-start = ((f32[16,200,128]{2,1,0:T(8,128)}), f32[16,200,128]{2,1,0:T(8,128)S(1)}, u32[]{:S(2)}, u32[]{:S(2)}) async-start(f32[16,200,128]{2,1,0:T(8,128)} %add.12), calls=%async_computation | async-start | bytes 3276800 | tf_op jit(solution)/shard_map/all_to_all | solution.py:336
  25.3 0.7 collective-permute-start.1
  26.0 0.0 collective-permute-done.1.key_ref
  26.0 27.6 %all-to-all-done.received_ref = f32[16,200,128]{2,1,0:T(8,128)S(1)} async-done(((f32[16,200,128]{2,1,0:T(8,128)}), f32[16,200,128]{2,1,0:T(8,128)S(1)}, u32[]{:S(2)}, u32[]{:S(2)}) %all-to-all-start) | async-done | bytes 1638432 | tf_op jit(solution)/shard_map/all_to_all | solution.py:336
  53.6 1.5 shard_map.56
  55.1 6.2 %all-to-all-start.1 = ((f32[32,40,128]{2,1,0:T(8,128)}), f32[32,40,128]{2,1,0:T(8,128)S(1)}, u32[]{:S(2)}, u32[]{:S(2)}) async-start(f32[32,40,128]{2,1,0:T(8,128)} %bitcast.2), calls=%async_computation.1 | async-start | bytes 1310720 | tf_op jit(solution)/shard_map/all_to_all | solution.py:336
  61.3 0.7 collective-permute-start.2
  62.0 12.2 %all-to-all-done.1 = f32[32,40,128]{2,1,0:T(8,128)S(1)} async-done(((f32[32,40,128]{2,1,0:T(8,128)}), f32[32,40,128]{2,1,0:T(8,128)S(1)}, u32[]{:S(2)}, u32[]{:S(2)}) %all-to-all-start.1) | async-done | bytes 655392 | tf_op jit(solution)/shard_map/all_to_all | solution.py:336
  74.2 0.1 reduce_sum.18
  74.3 0.0 collective-permute-done.2
  74.3 7.8 %all_to_all.20 = f32[4,40,128]{2,1,0:T(8,128)S(1)} all-to-all(f32[4,40,128]{2,1,0:T(8,128)S(1)} %broadcast_in_dim.6), channel_id=1, replica_groups={{0,1,2,3},{4,5,6,7},{8,9,10,11},{12,13,14,15},{16,17,18,19},{20,21,22,2..., dimensions={0} | all-to-all | bytes 163840 | tf_op jit(solution)/shard_map/all_to_all | solution.py:336
  82.1 19.1 %collective-permute-start.5 = (f32[184,128]{1,0:T(8,128)S(1)}, f32[184,128]{1,0:T(8,128)S(1)}, u32[]{:S(2)}, u32[]{:S(2)}) collective-permute-start(f32[184,128]{1,0:T(8,128)S(1)} %pad_maximum_fusion.1), channel_id=1, source_target_pairs={{0,12},{1,13},{2,14},{3,15},{4,0},{5,1},{6,2},{7,3},{8,4},{9,5},{1... | collective-permute-start | bytes 282632 | tf_op jit(solution)/shard_map/ppermute | solution.py:332
  101.3 8.3 %collective-permute-start.4 = (f32[184,128]{1,0:T(8,128)S(1)}, f32[184,128]{1,0:T(8,128)S(1)}, u32[]{:S(2)}, u32[]{:S(2)}) collective-permute-start(f32[184,128]{1,0:T(8,128)S(1)} %pad_maximum_fusion.1), channel_id=1, source_target_pairs={{0,8},{1,9},{2,10},{3,11},{4,12},{5,13},{6,14},{7,15},{8,0},{9,1},... | collective-permute-start | bytes 282632 | tf_op jit(solution)/shard_map/ppermute | solution.py:332
  109.6 7.3 %collective-permute-start.3 = (f32[184,128]{1,0:T(8,128)S(1)}, f32[184,128]{1,0:T(8,128)S(1)}, u32[]{:S(2)}, u32[]{:S(2)}) collective-permute-start(f32[184,128]{1,0:T(8,128)S(1)} %pad_maximum_fusion.1), channel_id=1, source_target_pairs={{0,4},{1,5},{2,6},{3,7},{4,8},{5,9},{6,10},{7,11},{8,12},{9,13},{1... | collective-permute-start | bytes 282632 | tf_op jit(solution)/shard_map/ppermute | solution.py:332
  116.8 0.0 collective-permute-done.5
  116.8 0.0 collective-permute-done.4
  116.9 2.4 %collective-permute-done.3 = f32[184,128]{1,0:T(8,128)S(1)} collective-permute-done((f32[184,128]{1,0:T(8,128)S(1)}, f32[184,128]{1,0:T(8,128)S(1)}, u32[]{:S(2)}, u32[]{:S(2)}) %collective-permute-start.3) | collective-permute-done | bytes 94240 | tf_op jit(solution)/shard_map/ppermute | solution.py:332
  119.3 1.4 broadcast_in_dim.7
  120.6 0.0 copy-start.3
  120.6 14.4 %all-to-all-start.3 = ((f32[32,96,128]{2,1,0:T(8,128)}), f32[32,96,128]{2,1,0:T(8,128)S(1)}, u32[]{:S(2)}, u32[]{:S(2)}) async-start(f32[32,96,128]{2,1,0:T(8,128)} %broadcast_in_dim.7), calls=%async_computation.3 | async-start | bytes 3145728 | tf_op jit(solution)/shard_map/all_to_all | solution.py:336
  135.1 6.1 %collective-permute-start.8 = (f32[576,128]{1,0:T(8,128)S(1)}, f32[576,128]{1,0:T(8,128)S(1)}, u32[]{:S(2)}, u32[]{:S(2)}) collective-permute-start(f32[576,128]{1,0:T(8,128)S(1)} %pad_maximum_fusion.refs_0_), channel_id=1, source_target_pairs={{0,15},{1,0},{2,1},{3,2},{4,3},{5,4},{6,5},{7,6},{8,7},{9,8},{10,9... | collective-permute-start | bytes 884744 | tf_op jit(solution)/shard_map/ppermute | solution.py:332
  141.2 1.9 collective-permute-start.7
  143.1 1.9 collective-permute-start.6
  145.1 12.1 %all-to-all-done.3.pieces_ref = f32[32,96,128]{2,1,0:T(8,128)S(1)} async-done(((f32[32,96,128]{2,1,0:T(8,128)}), f32[32,96,128]{2,1,0:T(8,128)S(1)}, u32[]{:S(2)}, u32[]{:S(2)}) %all-to-all-start.3) | async-done | bytes 1572896 | tf_op jit(solution)/shard_map/all_to_all | solution.py:336
  157.2 0.0 copy-done.3
  157.2 35.5 %shard_map.57 = (bf16[448,512]{1,0:T(8,128)(2,1)S(1)}, bf16[448,512]{1,0:T(8,128)(2,1)S(1)}) custom-call(f32[32,96,128]{2,1,0:T(8,128)S(1)} %all-to-all-done.3.pieces_ref, bf16[2,448,256]{2,1,0:T(8,128)(2,1)S(1)} %bitcast.7), custom_call_target="tpu_custom_call" | custom-call | flops 5368709120 | bytes 4194304 | tf_op jit(solution)/shard_map/pallas_call | solution.py:168
  192.7 0.0 collective-permute-done.8.refs_3_
  192.7 0.0 collective-permute-done.7.refs_2_
  192.7 0.0 collective-permute-done.6.refs_1_
  192.7 2.3 %shard_map.58 = bf16[448,576]{1,0:T(8,128)(2,1)} custom-call(f32[576,128]{1,0:T(8,128)S(1)} %pad_maximum_fusion.refs_0_, f32[576,128]{1,0:T(8,128)S(1)} %collective-permute-done.6.refs_1_, f32[576,128]{1,0:T(8,128)S(1)} %collective-permute-done.7.refs_2_, f32[576,128]{1,0:T(8,128)S(1)} %collective-permute-done.8.refs_3_, ...), custom_call_target="tpu_custom_call" | custom-call | tf_op jit(solution)/shard_map/pallas_call | solution.py:320
  (10 shorter events, 0.1 us)
Async XLA Ops:
  0.0 1.3 copy-start
  1.3 1.1 copy-start.1
  2.3 0.7 copy-start.2
  8.3 11.9 %collective-permute-start = (f32[16,200,128]{2,1,0:T(8,128)S(1)}, f32[16,200,128]{2,1,0:T(8,128)S(1)}, u32[]{:S(2)}, u32[]{:S(2)}) collective-permute-start(f32[16,200,128]{2,1,0:T(8,128)S(1)} %get-tuple-element.20), channel_id=1, source_target_pairs={{0,16},{16,0},{32,48},{48,32},{64,80},{80,64},{96,112},{112,96},{1... | collective-permute-start | bytes 4915208 | tf_op jit(solution)/shard_map/ppermute | solution.py:354
  21.6 32.0 %all-to-all-start = ((f32[16,200,128]{2,1,0:T(8,128)}), f32[16,200,128]{2,1,0:T(8,128)S(1)}, u32[]{:S(2)}, u32[]{:S(2)}) async-start(f32[16,200,128]{2,1,0:T(8,128)} %add.12), calls=%async_computation | async-start | bytes 3276800 | tf_op jit(solution)/shard_map/all_to_all | solution.py:336
  25.3 0.7 collective-permute-start.1
  55.1 19.1 %all-to-all-start.1 = ((f32[32,40,128]{2,1,0:T(8,128)}), f32[32,40,128]{2,1,0:T(8,128)S(1)}, u32[]{:S(2)}, u32[]{:S(2)}) async-start(f32[32,40,128]{2,1,0:T(8,128)} %bitcast.2), calls=%async_computation.1 | async-start | bytes 1310720 | tf_op jit(solution)/shard_map/all_to_all | solution.py:336
  61.3 13.0 %collective-permute-start.2 = (f32[144,128]{1,0:T(8,128)S(1)}, f32[144,128]{1,0:T(8,128)S(1)}, u32[]{:S(2)}, u32[]{:S(2)}) collective-permute-start(f32[144,128]{1,0:T(8,128)S(1)} %get-tuple-element.23), channel_id=1, source_target_pairs={{0,0},{16,16},{1,32},{17,48},{2,64},{18,80},{3,96},{19,112},{4,128... | collective-permute-start | bytes 221192 | tf_op jit(solution)/shard_map/ppermute | solution.py:360
  82.1 34.7 %collective-permute-start.5 = (f32[184,128]{1,0:T(8,128)S(1)}, f32[184,128]{1,0:T(8,128)S(1)}, u32[]{:S(2)}, u32[]{:S(2)}) collective-permute-start(f32[184,128]{1,0:T(8,128)S(1)} %pad_maximum_fusion.1), channel_id=1, source_target_pairs={{0,12},{1,13},{2,14},{3,15},{4,0},{5,1},{6,2},{7,3},{8,4},{9,5},{1... | collective-permute-start | bytes 282632 | tf_op jit(solution)/shard_map/ppermute | solution.py:332
  101.3 15.6 %collective-permute-start.4 = (f32[184,128]{1,0:T(8,128)S(1)}, f32[184,128]{1,0:T(8,128)S(1)}, u32[]{:S(2)}, u32[]{:S(2)}) collective-permute-start(f32[184,128]{1,0:T(8,128)S(1)} %pad_maximum_fusion.1), channel_id=1, source_target_pairs={{0,8},{1,9},{2,10},{3,11},{4,12},{5,13},{6,14},{7,15},{8,0},{9,1},... | collective-permute-start | bytes 282632 | tf_op jit(solution)/shard_map/ppermute | solution.py:332
  109.6 9.7 %collective-permute-start.3 = (f32[184,128]{1,0:T(8,128)S(1)}, f32[184,128]{1,0:T(8,128)S(1)}, u32[]{:S(2)}, u32[]{:S(2)}) collective-permute-start(f32[184,128]{1,0:T(8,128)S(1)} %pad_maximum_fusion.1), channel_id=1, source_target_pairs={{0,4},{1,5},{2,6},{3,7},{4,8},{5,9},{6,10},{7,11},{8,12},{9,13},{1... | collective-permute-start | bytes 282632 | tf_op jit(solution)/shard_map/ppermute | solution.py:332
  120.6 36.6 %copy-start.3 = (bf16[2,256,448]{1,2,0:T(8,128)(2,1)S(1)}, bf16[2,256,448]{1,2,0:T(8,128)(2,1)}, u32[]{:S(2)}) copy-start(bf16[2,256,448]{1,2,0:T(8,128)(2,1)} %param.9) | copy-start | bytes 1376260
  120.6 36.5 %all-to-all-start.3 = ((f32[32,96,128]{2,1,0:T(8,128)}), f32[32,96,128]{2,1,0:T(8,128)S(1)}, u32[]{:S(2)}, u32[]{:S(2)}) async-start(f32[32,96,128]{2,1,0:T(8,128)} %broadcast_in_dim.7), calls=%async_computation.3 | async-start | bytes 3145728 | tf_op jit(solution)/shard_map/all_to_all | solution.py:336
  135.1 57.6 %collective-permute-start.8 = (f32[576,128]{1,0:T(8,128)S(1)}, f32[576,128]{1,0:T(8,128)S(1)}, u32[]{:S(2)}, u32[]{:S(2)}) collective-permute-start(f32[576,128]{1,0:T(8,128)S(1)} %pad_maximum_fusion.refs_0_), channel_id=1, source_target_pairs={{0,15},{1,0},{2,1},{3,2},{4,3},{5,4},{6,5},{7,6},{8,7},{9,8},{10,9... | collective-permute-start | bytes 884744 | tf_op jit(solution)/shard_map/ppermute | solution.py:332
  141.2 51.5 %collective-permute-start.7 = (f32[576,128]{1,0:T(8,128)S(1)}, f32[576,128]{1,0:T(8,128)S(1)}, u32[]{:S(2)}, u32[]{:S(2)}) collective-permute-start(f32[576,128]{1,0:T(8,128)S(1)} %pad_maximum_fusion.refs_0_), channel_id=1, source_target_pairs={{0,2},{1,3},{2,4},{3,5},{4,6},{5,7},{6,8},{7,9},{8,10},{9,11},{10,... | collective-permute-start | bytes 884744 | tf_op jit(solution)/shard_map/ppermute | solution.py:332
  143.1 49.5 %collective-permute-start.6 = (f32[576,128]{1,0:T(8,128)S(1)}, f32[576,128]{1,0:T(8,128)S(1)}, u32[]{:S(2)}, u32[]{:S(2)}) collective-permute-start(f32[576,128]{1,0:T(8,128)S(1)} %pad_maximum_fusion.refs_0_), channel_id=1, source_target_pairs={{0,1},{1,2},{2,3},{3,4},{4,5},{5,6},{6,7},{7,8},{8,9},{9,10},{10,1... | collective-permute-start | bytes 884744 | tf_op jit(solution)/shard_map/ppermute | solution.py:332

commit v10 on v8

--- a/solution.py
+++ b/solution.py
@@ -360,13 +360,12 @@
     own = lax.ppermute(panel_piece, ("row", "col"), turned)
     share = packed.shape[0] // rows
     part = jnp.sum(swapped(packed.reshape(rows, share, LANES), "row"), axis=0)
-    neighbours = [[STRIDE * g + i for i in range(STRIDE)] for g in range(cols // STRIDE)]
+    part = part + sum(moved(part, "col", shift) for shift in SHIFTS[1:])
     joined = jnp.concatenate([own, part], axis=0)
     joined = [joined] + [moved(joined, "col", STRIDE * t) for t in range(1, cols // STRIDE)]
     joined = lax.optimization_barrier(tuple(joined))
     far = [item[:-share] for item in joined]
     part = sum(item[-share:] for item in joined)
-    part = jnp.sum(swapped(copies(part, STRIDE), "col", neighbours), axis=0)
     piece = jnp.concatenate([part, value_piece], axis=0)
     pieces = swapped(copies(piece, rows), "row")
     far = jnp.concatenate(far, axis=0)

time: 197 us -> 205 us (1.041)
  starting transfers between devices: 69.3 us -> 86.6 us
  waiting for transfers between devices: 59.6 us -> 48.4 us
  blocking collectives: 16.7 us -> 18.9 us
    ppermute x6 -> x9, starting transfers between devices: 35.6 us -> 53.9 us  [moved(): lax.ppermute(value, axis, [(i, (i + shift) % size) for i in range(size)])]
    all_to_all x3 -> x2, waiting for transfers between devices: 54.2 us -> 39.8 us  [swapped(): lax.all_to_all(value, axis, 0, 0, axis_index_groups=groups, tiled=True)]
    ppermute x6 -> x9, waiting for transfers between devices: 2.24 us -> 5.46 us  [moved(): lax.ppermute(value, axis, [(i, (i + shift) % size) for i in range(size)])]
    all_to_all x1, blocking collectives: 16.7 us -> 18.9 us  [swapped(): lax.all_to_all(value, axis, 0, 0, axis_index_groups=groups, tiled=True)]
    all_to_all x3 -> x2, starting transfers between devices: 23.6 us -> 22.7 us  [swapped(): lax.all_to_all(value, axis, 0, 0, axis_index_groups=groups, tiled=True)]
  transfers between devices with their start and end apart: 12 -> 14, of which waited for: 5 -> 6; matrix products, arithmetic and copies ran while one was open for 0% -> 0% of each run, Pallas kernels for 18% -> 17%
where the time goes in v10:
time: 205 us; the launch traced here: 204 us
  starting transfers between devices  86.6 us (42%)
  waiting for transfers between devices  48.4 us (24%)
  Pallas kernels  43.8 us (21%)
  blocking collectives  18.9 us (9%)
  local copies, waits for them, and re-layouts  4.39 us (2%)
    ppermute x9, starting transfers between devices, moved(): lax.ppermute(value, axis, [(i, (i + shift) % size) for i in range(size)])  53.9 us
    all_to_all x2, waiting for transfers between devices, swapped(): lax.all_to_all(value, axis, 0, 0, axis_index_groups=groups, tiled=True)  39.8 us
    pallas_call x1, Pallas kernels, solve(): pl.pallas_call(solve_kernel, out_shape=(out, out), in_specs=[vmem, pl.Blo...  35.5 us
    all_to_all x2, starting transfers between devices, swapped(): lax.all_to_all(value, axis, 0, 0, axis_index_groups=groups, tiled=True)  22.7 us
    all_to_all x1, blocking collectives, swapped(): lax.all_to_all(value, axis, 0, 0, axis_index_groups=groups, tiled=True)  18.9 us
    ppermute x1, starting transfers between devices, shards(): half_sum = mine + lax.ppermute(other, 'row', other_core)  8.79 us
    ppermute x9, waiting for transfers between devices, moved(): lax.ppermute(value, axis, [(i, (i + shift) % size) for i in range(size)])  5.46 us
    pallas_call x1, Pallas kernels, front(): pl.pallas_call(front_kernel, out_shape=(payload, payload, jax.ShapeDtypeS...  5.33 us
  transfers between devices with their start and end apart: 14, of which 6 were waited for; matrix products, arithmetic and copies ran while one was open for 0% of the time, Pallas kernels for 17%

profile of v10, /device:TPU:1, one launch (start us, length us, event | category | flops | bytes accessed | tf_op | source)
XLA Modules:
  0.0 203.8 jit_solution(9815558966430724346)
XLA Ops:
  0.0 0.0 copy-start
  0.0 1.3 copy-done
  1.3 0.0 copy-start.1
  1.3 1.1 copy-done.1
  2.3 0.0 copy-start.2
  2.3 0.7 copy-done.2
  3.0 5.3 %shard_map.55 = (f32[16,200,128]{2,1,0:T(8,128)S(1)}, f32[16,200,128]{2,1,0:T(8,128)S(1)}, bf16[48,512]{1,0:T(8,128)(2,1)S(1)}) custom-call(s32[2,256]{1,0:T(2,128)S(1)} %copy-done.2, bf16[576,1024]{1,0:T(8,128)(2,1)S(1)} %bitcast.5, f32[576,1152]{1,0:T(8,128)} %cov_hbm.1, bf16[448,576]{1,0:T(8,128)(2,1)S(1)} %bitcast.7), custom_call_target="tpu_custom_call" | custom-call | tf_op jit(solution)/shard_map/pallas_call | solution.py:238
  8.3 8.8 %collective-permute-start = (f32[16,200,128]{2,1,0:T(8,128)S(1)}, f32[16,200,128]{2,1,0:T(8,128)S(1)}, u32[]{:S(2)}, u32[]{:S(2)}) collective-permute-start(f32[16,200,128]{2,1,0:T(8,128)S(1)} %get-tuple-element.18), channel_id=1, source_target_pairs={{0,16},{16,0},{32,48},{48,32},{64,80},{80,64},{96,112},{112,96},{1... | collective-permute-start | bytes 4915208 | tf_op jit(solution)/shard_map/ppermute | solution.py:354
  17.1 3.1 %collective-permute-done = f32[16,200,128]{2,1,0:T(8,128)S(1)} collective-permute-done((f32[16,200,128]{2,1,0:T(8,128)S(1)}, f32[16,200,128]{2,1,0:T(8,128)S(1)}, u32[]{:S(2)}, u32[]{:S(2)}) %collective-permute-start) | collective-permute-done | bytes 1638432 | tf_op jit(solution)/shard_map/ppermute | solution.py:354
  20.3 1.3 add.21
  21.6 3.7 %all-to-all-start = ((f32[16,200,128]{2,1,0:T(8,128)}), f32[16,200,128]{2,1,0:T(8,128)S(1)}, u32[]{:S(2)}, u32[]{:S(2)}) async-start(f32[16,200,128]{2,1,0:T(8,128)} %add.21), calls=%async_computation | async-start | bytes 3276800 | tf_op jit(solution)/shard_map/all_to_all | solution.py:336
  25.3 0.7 collective-permute-start.1
  26.0 0.0 collective-permute-done.1.key_ref
  26.0 27.6 %all-to-all-done.received_ref = f32[16,200,128]{2,1,0:T(8,128)S(1)} async-done(((f32[16,200,128]{2,1,0:T(8,128)}), f32[16,200,128]{2,1,0:T(8,128)S(1)}, u32[]{:S(2)}, u32[]{:S(2)}) %all-to-all-start) | async-done | bytes 1638432 | tf_op jit(solution)/shard_map/all_to_all | solution.py:336
  53.6 0.6 shard_map.56
  54.2 18.9 %all_to_all.15 = f32[32,40,128]{2,1,0:T(8,128)S(1)} all-to-all(f32[32,40,128]{2,1,0:T(8,128)S(1)} %bitcast.6), channel_id=1, replica_groups=mesh['row'=32,'col'=16] {'row'}, dimensions={0} | all-to-all | bytes 1310720 | tf_op jit(solution)/shard_map/all_to_all | solution.py:336
  73.1 0.1 reduce_sum.9
  73.2 9.5 %collective-permute-start.5 = (f32[40,128]{1,0:T(8,128)S(1)}, f32[40,128]{1,0:T(8,128)S(1)}, u32[]{:S(2)}, u32[]{:S(2)}) collective-permute-start(f32[40,128]{1,0:T(8,128)S(1)} %reduce_sum.9), channel_id=1, source_target_pairs={{0,15},{1,0},{2,1},{3,2},{4,3},{5,4},{6,5},{7,6},{8,7},{9,8},{10,9... | collective-permute-start | bytes 61448 | tf_op jit(solution)/shard_map/ppermute | solution.py:332
  82.7 1.9 collective-permute-start.4
  84.6 1.9 collective-permute-start.3
  86.6 0.7 collective-permute-start.2
  87.2 0.0 collective-permute-done.5
  87.2 2.2 %collective-permute-done.4 = f32[40,128]{1,0:T(8,128)S(1)} collective-permute-done((f32[40,128]{1,0:T(8,128)S(1)}, f32[40,128]{1,0:T(8,128)S(1)}, u32[]{:S(2)}, u32[]{:S(2)}) %collective-permute-start.4) | collective-permute-done | bytes 20512 | tf_op jit(solution)/shard_map/ppermute | solution.py:332
  89.4 1.3 collective-permute-done.3
  90.7 0.0 collective-permute-done.2
  90.7 13.5 %collective-permute-start.8 = (f32[184,128]{1,0:T(8,128)S(1)}, f32[184,128]{1,0:T(8,128)S(1)}, u32[]{:S(2)}, u32[]{:S(2)}) collective-permute-start(f32[184,128]{1,0:T(8,128)S(1)} %pad_maximum_fusion.1), channel_id=1, source_target_pairs={{0,12},{1,13},{2,14},{3,15},{4,0},{5,1},{6,2},{7,3},{8,4},{9,5},{1... | collective-permute-start | bytes 282632 | tf_op jit(solution)/shard_map/ppermute | solution.py:332
  104.2 9.9 %collective-permute-start.7 = (f32[184,128]{1,0:T(8,128)S(1)}, f32[184,128]{1,0:T(8,128)S(1)}, u32[]{:S(2)}, u32[]{:S(2)}) collective-permute-start(f32[184,128]{1,0:T(8,128)S(1)} %pad_maximum_fusion.1), channel_id=1, source_target_pairs={{0,8},{1,9},{2,10},{3,11},{4,12},{5,13},{6,14},{7,15},{8,0},{9,1},... | collective-permute-start | bytes 282632 | tf_op jit(solution)/shard_map/ppermute | solution.py:332
  114.1 7.3 %collective-permute-start.6 = (f32[184,128]{1,0:T(8,128)S(1)}, f32[184,128]{1,0:T(8,128)S(1)}, u32[]{:S(2)}, u32[]{:S(2)}) collective-permute-start(f32[184,128]{1,0:T(8,128)S(1)} %pad_maximum_fusion.1), channel_id=1, source_target_pairs={{0,4},{1,5},{2,6},{3,7},{4,8},{5,9},{6,10},{7,11},{8,12},{9,13},{1... | collective-permute-start | bytes 282632 | tf_op jit(solution)/shard_map/ppermute | solution.py:332
  121.4 0.0 collective-permute-done.8
  121.4 0.0 collective-permute-done.7
  121.4 2.0 collective-permute-done.6
  123.4 1.4 broadcast_in_dim.3
  124.8 0.0 copy-start.3
  124.8 18.9 %all-to-all-start.2 = ((f32[32,96,128]{2,1,0:T(8,128)}), f32[32,96,128]{2,1,0:T(8,128)S(1)}, u32[]{:S(2)}, u32[]{:S(2)}) async-start(f32[32,96,128]{2,1,0:T(8,128)} %broadcast_in_dim.3), calls=%async_computation.2 | async-start | bytes 3145728 | tf_op jit(solution)/shard_map/all_to_all | solution.py:336
  143.8 6.0 %collective-permute-start.11 = (f32[576,128]{1,0:T(8,128)S(1)}, f32[576,128]{1,0:T(8,128)S(1)}, u32[]{:S(2)}, u32[]{:S(2)}) collective-permute-start(f32[576,128]{1,0:T(8,128)S(1)} %pad_maximum_fusion.refs_0_), channel_id=1, source_target_pairs={{0,15},{1,0},{2,1},{3,2},{4,3},{5,4},{6,5},{7,6},{8,7},{9,8},{10,9... | collective-permute-start | bytes 884744 | tf_op jit(solution)/shard_map/ppermute | solution.py:332
  149.9 1.9 collective-permute-start.10
  151.8 1.9 collective-permute-start.9
  153.7 12.2 %all-to-all-done.2.pieces_ref = f32[32,96,128]{2,1,0:T(8,128)S(1)} async-done(((f32[32,96,128]{2,1,0:T(8,128)}), f32[32,96,128]{2,1,0:T(8,128)S(1)}, u32[]{:S(2)}, u32[]{:S(2)}) %all-to-all-start.2) | async-done | bytes 1572896 | tf_op jit(solution)/shard_map/all_to_all | solution.py:336
  165.9 0.0 copy-done.3
  165.9 35.5 %shard_map.57 = (bf16[448,512]{1,0:T(8,128)(2,1)S(1)}, bf16[448,512]{1,0:T(8,128)(2,1)S(1)}) custom-call(f32[32,96,128]{2,1,0:T(8,128)S(1)} %all-to-all-done.2.pieces_ref, bf16[2,448,256]{2,1,0:T(8,128)(2,1)S(1)} %bitcast.8), custom_call_target="tpu_custom_call" | custom-call | flops 5368709120 | bytes 4194304 | tf_op jit(solution)/shard_map/pallas_call | solution.py:168
  201.4 0.0 collective-permute-done.11.refs_3_
  201.4 0.0 collective-permute-done.10.refs_2_
  201.4 0.0 collective-permute-done.9.refs_1_
  201.5 2.3 %shard_map.58 = bf16[448,576]{1,0:T(8,128)(2,1)} custom-call(f32[576,128]{1,0:T(8,128)S(1)} %pad_maximum_fusion.refs_0_, f32[576,128]{1,0:T(8,128)S(1)} %collective-permute-done.9.refs_1_, f32[576,128]{1,0:T(8,128)S(1)} %collective-permute-done.10.refs_2_, f32[576,128]{1,0:T(8,128)S(1)} %collective-permute-done.11.refs_3_, ...), custom_call_target="tpu_custom_call" | custom-call | tf_op jit(solution)/shard_map/pallas_call | solution.py:320
  (9 shorter events, 0.1 us)
Async XLA Ops:
  0.0 1.3 copy-start
  1.3 1.1 copy-start.1
  2.3 0.7 copy-start.2
  8.3 11.9 %collective-permute-start = (f32[16,200,128]{2,1,0:T(8,128)S(1)}, f32[16,200,128]{2,1,0:T(8,128)S(1)}, u32[]{:S(2)}, u32[]{:S(2)}) collective-permute-start(f32[16,200,128]{2,1,0:T(8,128)S(1)} %get-tuple-element.18), channel_id=1, source_target_pairs={{0,16},{16,0},{32,48},{48,32},{64,80},{80,64},{96,112},{112,96},{1... | collective-permute-start | bytes 4915208 | tf_op jit(solution)/shard_map/ppermute | solution.py:354
  21.6 32.0 %all-to-all-start = ((f32[16,200,128]{2,1,0:T(8,128)}), f32[16,200,128]{2,1,0:T(8,128)S(1)}, u32[]{:S(2)}, u32[]{:S(2)}) async-start(f32[16,200,128]{2,1,0:T(8,128)} %add.21), calls=%async_computation | async-start | bytes 3276800 | tf_op jit(solution)/shard_map/all_to_all | solution.py:336
  25.3 0.7 collective-permute-start.1
  73.2 14.0 %collective-permute-start.5 = (f32[40,128]{1,0:T(8,128)S(1)}, f32[40,128]{1,0:T(8,128)S(1)}, u32[]{:S(2)}, u32[]{:S(2)}) collective-permute-start(f32[40,128]{1,0:T(8,128)S(1)} %reduce_sum.9), channel_id=1, source_target_pairs={{0,15},{1,0},{2,1},{3,2},{4,3},{5,4},{6,5},{7,6},{8,7},{9,8},{10,9... | collective-permute-start | bytes 61448 | tf_op jit(solution)/shard_map/ppermute | solution.py:332
  82.7 6.7 %collective-permute-start.4 = (f32[40,128]{1,0:T(8,128)S(1)}, f32[40,128]{1,0:T(8,128)S(1)}, u32[]{:S(2)}, u32[]{:S(2)}) collective-permute-start(f32[40,128]{1,0:T(8,128)S(1)} %reduce_sum.9), channel_id=1, source_target_pairs={{0,2},{1,3},{2,4},{3,5},{4,6},{5,7},{6,8},{7,9},{8,10},{9,11},{10,... | collective-permute-start | bytes 61448 | tf_op jit(solution)/shard_map/ppermute | solution.py:332
  84.6 6.0 %collective-permute-start.3 = (f32[40,128]{1,0:T(8,128)S(1)}, f32[40,128]{1,0:T(8,128)S(1)}, u32[]{:S(2)}, u32[]{:S(2)}) collective-permute-start(f32[40,128]{1,0:T(8,128)S(1)} %reduce_sum.9), channel_id=1, source_target_pairs={{0,1},{1,2},{2,3},{3,4},{4,5},{5,6},{6,7},{7,8},{8,9},{9,10},{10,1... | collective-permute-start | bytes 61448 | tf_op jit(solution)/shard_map/ppermute | solution.py:332
  86.6 4.1 %collective-permute-start.2 = (f32[144,128]{1,0:T(8,128)S(1)}, f32[144,128]{1,0:T(8,128)S(1)}, u32[]{:S(2)}, u32[]{:S(2)}) collective-permute-start(f32[144,128]{1,0:T(8,128)S(1)} %get-tuple-element.20), channel_id=1, source_target_pairs={{0,0},{16,16},{1,32},{17,48},{2,64},{18,80},{3,96},{19,112},{4,128... | collective-permute-start | bytes 221192 | tf_op jit(solution)/shard_map/ppermute | solution.py:360
  90.7 30.7 %collective-permute-start.8 = (f32[184,128]{1,0:T(8,128)S(1)}, f32[184,128]{1,0:T(8,128)S(1)}, u32[]{:S(2)}, u32[]{:S(2)}) collective-permute-start(f32[184,128]{1,0:T(8,128)S(1)} %pad_maximum_fusion.1), channel_id=1, source_target_pairs={{0,12},{1,13},{2,14},{3,15},{4,0},{5,1},{6,2},{7,3},{8,4},{9,5},{1... | collective-permute-start | bytes 282632 | tf_op jit(solution)/shard_map/ppermute | solution.py:332
  104.2 17.2 %collective-permute-start.7 = (f32[184,128]{1,0:T(8,128)S(1)}, f32[184,128]{1,0:T(8,128)S(1)}, u32[]{:S(2)}, u32[]{:S(2)}) collective-permute-start(f32[184,128]{1,0:T(8,128)S(1)} %pad_maximum_fusion.1), channel_id=1, source_target_pairs={{0,8},{1,9},{2,10},{3,11},{4,12},{5,13},{6,14},{7,15},{8,0},{9,1},... | collective-permute-start | bytes 282632 | tf_op jit(solution)/shard_map/ppermute | solution.py:332
  114.1 9.3 %collective-permute-start.6 = (f32[184,128]{1,0:T(8,128)S(1)}, f32[184,128]{1,0:T(8,128)S(1)}, u32[]{:S(2)}, u32[]{:S(2)}) collective-permute-start(f32[184,128]{1,0:T(8,128)S(1)} %pad_maximum_fusion.1), channel_id=1, source_target_pairs={{0,4},{1,5},{2,6},{3,7},{4,8},{5,9},{6,10},{7,11},{8,12},{9,13},{1... | collective-permute-start | bytes 282632 | tf_op jit(solution)/shard_map/ppermute | solution.py:332
  124.8 41.1 %copy-start.3 = (bf16[2,256,448]{1,2,0:T(8,128)(2,1)S(1)}, bf16[2,256,448]{1,2,0:T(8,128)(2,1)}, u32[]{:S(2)}) copy-start(bf16[2,256,448]{1,2,0:T(8,128)(2,1)} %param.9) | copy-start | bytes 1376260
  124.8 41.1 %all-to-all-start.2 = ((f32[32,96,128]{2,1,0:T(8,128)}), f32[32,96,128]{2,1,0:T(8,128)S(1)}, u32[]{:S(2)}, u32[]{:S(2)}) async-start(f32[32,96,128]{2,1,0:T(8,128)} %broadcast_in_dim.3), calls=%async_computation.2 | async-start | bytes 3145728 | tf_op jit(solution)/shard_map/all_to_all | solution.py:336
  143.8 57.6 %collective-permute-start.11 = (f32[576,128]{1,0:T(8,128)S(1)}, f32[576,128]{1,0:T(8,128)S(1)}, u32[]{:S(2)}, u32[]{:S(2)}) collective-permute-start(f32[576,128]{1,0:T(8,128)S(1)} %pad_maximum_fusion.refs_0_), channel_id=1, source_target_pairs={{0,15},{1,0},{2,1},{3,2},{4,3},{5,4},{6,5},{7,6},{8,7},{9,8},{10,9... | collective-permute-start | bytes 884744 | tf_op jit(solution)/shard_map/ppermute | solution.py:332
  149.9 51.6 %collective-permute-start.10 = (f32[576,128]{1,0:T(8,128)S(1)}, f32[576,128]{1,0:T(8,128)S(1)}, u32[]{:S(2)}, u32[]{:S(2)}) collective-permute-start(f32[576,128]{1,0:T(8,128)S(1)} %pad_maximum_fusion.refs_0_), channel_id=1, source_target_pairs={{0,2},{1,3},{2,4},{3,5},{4,6},{5,7},{6,8},{7,9},{8,10},{9,11},{10,... | collective-permute-start | bytes 884744 | tf_op jit(solution)/shard_map/ppermute | solution.py:332
  151.8 49.6 %collective-permute-start.9 = (f32[576,128]{1,0:T(8,128)S(1)}, f32[576,128]{1,0:T(8,128)S(1)}, u32[]{:S(2)}, u32[]{:S(2)}) collective-permute-start(f32[576,128]{1,0:T(8,128)S(1)} %pad_maximum_fusion.refs_0_), channel_id=1, source_target_pairs={{0,1},{1,2},{2,3},{3,4},{4,5},{5,6},{6,7},{7,8},{8,9},{9,10},{10,1... | collective-permute-start | bytes 884744 | tf_op jit(solution)/shard_map/ppermute | solution.py:332
